TPU v7x, 256 devices: a whole 4x4x8 slice. The times are simulated.
256 devices in a mesh: walk: 32 (over y, z), det: 8 (over x, core).
Axes of the slice: x: 4, y: 4, z: 8, core: 2. Of those that a mesh axis runs over, the one named last changes fastest.
Arguments:
- positions: float32 [3, 4096, 50], P(None, ('walk', 'det')), may hold values from -6 to 6
- inverse: float32 [4096, 50, 50], P(('walk', 'det')), may hold values from -0.875 to 0.875
- centers: float32 [3, 512], replicated, may hold values from -4 to 4
- exponent: float32 [512], replicated, may hold values from 0.05 to 0.5
- orbital_weights: float32 [512, 128], replicated, may hold values from -0.25 to 0.25
- excitations: int32 [4, 65536], P(None, 'det'), may hold values from 0 to 127, as said below
- state_coeffs: float32 [4, 65536], P(None, 'det'), may hold values from -0.09375 to 0.09375
- local_energy: float32 [4, 4096], P(None, 'walk'), may hold values from -24 to 24
Outputs:
- ci_grad: float32 [4, 8, 8192], P(None, 'det', 'walk')
- state_values: float32 [4, 4096], P(None, ('walk', 'det'))
- state_energy: float32 [4], replicated
Inputs may be any that keep to these rules, and one draw needn't show every extreme that they name: `excitations`: rows 0 and 2 are occupied orbitals below 50, rows 1 and 3 virtual orbitals below 128. In each aligned block of 128 determinants rows 0 and 1 are the same; row 2 differs from row 0 and row 3 from row 1.
All inputs are finite; a program needn't handle non-finite values.
Results may differ from a plain program's by a relative error of at most 0.012.
The roundings to bfloat16 on the way count: a program that leaves them out, or rounds other values in their place, can miss the bound.
Values may be sent and summed in bfloat16 or wider, within the bound.
No kernel may reach another device: no remote copies, remote signals or barrier semaphores. Data moves between devices by JAX's collectives and lax.ppermute only.
A program may use at most 64 MiB of HBM per device.

v0:
```python
import math

import jax
import jax.numpy as jnp
from jax import lax
from jax.sharding import PartitionSpec as P

BLOCK = 128


def build_tables(positions, inverse, centers, exponent, orbital_weights):
    distance = jnp.zeros(positions.shape[1:] + (centers.shape[1],), jnp.float32)
    for component in range(3):
        offset = positions[component][:, :, None] - centers[component][None, None, :]
        distance = distance + offset * offset
    basis = jnp.exp(-exponent * distance)
    virtual = jnp.einsum("wem,ma->wea", basis, orbital_weights, precision=lax.Precision.HIGHEST)
    product = jnp.einsum("wie,wea->wia", inverse, virtual, precision=lax.Precision.HIGHEST)
    return product.astype(jnp.bfloat16).reshape(product.shape[0], -1)


def pair_ratios(ratio_table, excitations, width):
    count = ratio_table.shape[0]
    orbitals = ratio_table.shape[1] // width
    dets = excitations.shape[1]
    blocks = dets // BLOCK
    first_row, first_col = (excitations[0], excitations[1])
    second_row, second_col = (excitations[2], excitations[3])
    col_ids = lax.broadcasted_iota(jnp.int32, (dets, width), 1)
    pick_col = (second_col[:, None] == col_ids).astype(jnp.bfloat16)
    parent_cols = first_col.reshape(blocks, BLOCK)[:, 0]
    parent_ids = lax.broadcasted_iota(jnp.int32, (width, blocks), 0)
    pick_parent = (parent_cols[None, :] == parent_ids).astype(jnp.bfloat16)
    row_ids = lax.broadcasted_iota(jnp.int32, (orbitals, dets), 0)
    own_row = (first_row[None, :] == row_ids).astype(jnp.float32)
    other_row = (second_row[None, :] == row_ids).astype(jnp.float32)
    group = math.gcd(count, 16)

    def one_group(tables):
        along = jnp.einsum("wec,kc->wek", tables, pick_col, preferred_element_type=jnp.bfloat16)
        parent = jnp.einsum("wec,cb->web", tables, pick_parent, preferred_element_type=jnp.float32)
        parent = jnp.broadcast_to(parent[:, :, :, None], parent.shape + (BLOCK,)).reshape(
            parent.shape[0], orbitals, dets
        )
        value_ia = jnp.sum(own_row * parent, axis=1)
        value_ja = jnp.sum(other_row * parent, axis=1)
        value_ib = jnp.sum(own_row * along, axis=1)
        value_jb = jnp.sum(other_row * along, axis=1)
        return value_ia * value_jb - value_ib * value_ja

    grouped = ratio_table.reshape(count // group, group, orbitals, width)
    return lax.map(one_group, grouped).reshape(count, dets)


def shards(
    positions, inverse, centers, exponent, orbital_weights, excitations, state_coeffs, local_energy
):
    width = orbital_weights.shape[1]
    own_count = positions.shape[1]
    own_tables = build_tables(positions, inverse, centers, exponent, orbital_weights)
    ratios = pair_ratios(lax.all_gather(own_tables, "det", axis=0, tiled=True), excitations, width)
    partial_values = lax.dot_general(
        state_coeffs, ratios, (((1,), (1,)), ((), ())), precision=lax.Precision.HIGHEST
    )
    values = lax.psum(partial_values, "det")
    guide = 1.0 + jnp.sum(values * values, axis=0)
    weight = values * values / guide
    scaled = values / guide
    own_values = lax.dynamic_slice_in_dim(values, lax.axis_index("det") * own_count, own_count, 1)
    total, weighted = lax.psum(
        (jnp.sum(weight, axis=1), jnp.sum(weight * local_energy, axis=1)), "walk"
    )
    energy = weighted / total
    factor = 2.0 * scaled * (local_energy - energy[:, None]) / total[:, None]
    term = jnp.dot(factor, ratios, precision=lax.Precision.HIGHEST)
    grad = lax.psum_scatter(term, "walk", scatter_dimension=1, tiled=True)
    return (grad[:, None, :], own_values, energy)


def solution(mesh):
    in_specs = (
        P(None, ("walk", "det"), None),
        P(("walk", "det"), None, None),
        P(),
        P(),
        P(),
        P(None, "det"),
        P(None, "det"),
        P(None, "walk"),
    )
    out_specs = (P(None, "det", "walk"), P(None, ("walk", "det")), P())
    return jax.shard_map(shards, mesh=mesh, in_specs=in_specs, out_specs=out_specs, check_vma=False)
```

profile of v0, /device:TPU:32, one launch (start us, length us, event | category | flops | bytes accessed | tf_op | source)
XLA Modules:
  0.0 578.2 jit_solution(10473067513230239565)
XLA Ops:
  9.5 3.1 fusion.30
  14.5 29.5 %all-gather.2.cloned.1.call-done = bf16[128,6400]{1,0:T(8,128)(2,1)} async-done(((bf16[16,6400]{1,0:T(8,128)(2,1)}), bf16[128,6400]{1,0:T(8,128)(2,1)}) %all-gather.2.cloned.1.call-update) | async-done | bytes 1638416 | tf_op jit(solution)/shard_map/all_gather | solution.py:61
  44.0 3.9 reshape.72
  47.9 207.0 %while.11 = (s32[]{:T(128)}, f32[8,16,8192]{2,1,0:T(8,128)}, bf16[8,16,50,128]{3,2,1,0:T(8,128)(2,1)}, s32[8192]{0:T(1024)S(1)}, s32[64]{0:T(128)S(1)}, /*index=5*/s32[8192]{0:T(1024)S(1)}, s32[8192]{0:T(1024)S(1)}, s32[]{:T(128)}) while((s32[]{:T(128)}, f32[8,16,8192]{2,1,0:T(8,128)}, bf16[8,16,50,128]{3,2,1,0:T(8,128)(2,1)}, ...), condition=%wide.region_5.6_spmd.clone, body=%wide.region_0.5_spmd.clone.sunk | while | flops 1753432064 | bytes 31506792 | solution.py:52
  47.9 1.3 fusion.75
  49.5 13.0 %fusion.77 = (f32[16,8192]{1,0:T(8,128)S(1)}, f32[16,8192]{1,0:T(8,128)S(1)}) fusion(f32[50,8192]{1,0:T(8,128)S(1)} %get-tuple-element.160, f32[50,8192]{1,0:T(8,128)S(1)} %get-tuple-element.159, s32[8192]{0:T(1024)S(1)} %get-tuple-element.187, bf16[8,16,50,128]{3,2,1,0:T(8,128)(2,1)} %get-tuple-element.183, s32[]{:T(128)S(6)} %copy.40), kind=kOutput, calls=%fused_computation.6.clone.1 | convolution fusion | flops 1712324608 | bytes 4587524 | tf_op jit(solution)/shard_map/while/body/eval_jaxpr/wec,kc->wek/dot_general | solution.py:40
  63.4 9.3 %multiply_reduce_fusion.5 = (f32[16,64,128]{2,1,0:T(8,128)S(1)}, f32[16,64,128]{2,1,0:T(8,128)S(1)}) fusion(f32[16,50,64]{2,1,0:T(8,128)S(1)} %fusion.75, f32[50,64,128]{2,1,0:T(8,128)S(1)} %slice.59, f32[50,64,128]{2,1,0:T(8,128)S(1)} %slice.60), kind=kLoop, calls=%fused_computation.9.clone.1 | loop fusion | flops 25952256 | bytes 4530176 | tf_op jit(solution)/shard_map/while/body/eval_jaxpr/reduce_sum | solution.py:45
  73.8 1.2 fusion.75
  75.4 13.0 %fusion.77 = (f32[16,8192]{1,0:T(8,128)S(1)}, f32[16,8192]{1,0:T(8,128)S(1)}) fusion(f32[50,8192]{1,0:T(8,128)S(1)} %get-tuple-element.160, f32[50,8192]{1,0:T(8,128)S(1)} %get-tuple-element.159, s32[8192]{0:T(1024)S(1)} %get-tuple-element.187, bf16[8,16,50,128]{3,2,1,0:T(8,128)(2,1)} %get-tuple-element.183, s32[]{:T(128)S(6)} %copy.40), kind=kOutput, calls=%fused_computation.6.clone.1 | convolution fusion | flops 1712324608 | bytes 4587524 | tf_op jit(solution)/shard_map/while/body/eval_jaxpr/wec,kc->wek/dot_general | solution.py:40
  89.3 9.3 %multiply_reduce_fusion.5 = (f32[16,64,128]{2,1,0:T(8,128)S(1)}, f32[16,64,128]{2,1,0:T(8,128)S(1)}) fusion(f32[16,50,64]{2,1,0:T(8,128)S(1)} %fusion.75, f32[50,64,128]{2,1,0:T(8,128)S(1)} %slice.59, f32[50,64,128]{2,1,0:T(8,128)S(1)} %slice.60), kind=kLoop, calls=%fused_computation.9.clone.1 | loop fusion | flops 25952256 | bytes 4530176 | tf_op jit(solution)/shard_map/while/body/eval_jaxpr/reduce_sum | solution.py:45
  99.6 1.2 fusion.75
  101.2 13.0 %fusion.77 = (f32[16,8192]{1,0:T(8,128)S(1)}, f32[16,8192]{1,0:T(8,128)S(1)}) fusion(f32[50,8192]{1,0:T(8,128)S(1)} %get-tuple-element.160, f32[50,8192]{1,0:T(8,128)S(1)} %get-tuple-element.159, s32[8192]{0:T(1024)S(1)} %get-tuple-element.187, bf16[8,16,50,128]{3,2,1,0:T(8,128)(2,1)} %get-tuple-element.183, s32[]{:T(128)S(6)} %copy.40), kind=kOutput, calls=%fused_computation.6.clone.1 | convolution fusion | flops 1712324608 | bytes 4587524 | tf_op jit(solution)/shard_map/while/body/eval_jaxpr/wec,kc->wek/dot_general | solution.py:40
  115.1 9.3 %multiply_reduce_fusion.5 = (f32[16,64,128]{2,1,0:T(8,128)S(1)}, f32[16,64,128]{2,1,0:T(8,128)S(1)}) fusion(f32[16,50,64]{2,1,0:T(8,128)S(1)} %fusion.75, f32[50,64,128]{2,1,0:T(8,128)S(1)} %slice.59, f32[50,64,128]{2,1,0:T(8,128)S(1)} %slice.60), kind=kLoop, calls=%fused_computation.9.clone.1 | loop fusion | flops 25952256 | bytes 4530176 | tf_op jit(solution)/shard_map/while/body/eval_jaxpr/reduce_sum | solution.py:45
  125.5 1.2 fusion.75
  127.1 13.0 %fusion.77 = (f32[16,8192]{1,0:T(8,128)S(1)}, f32[16,8192]{1,0:T(8,128)S(1)}) fusion(f32[50,8192]{1,0:T(8,128)S(1)} %get-tuple-element.160, f32[50,8192]{1,0:T(8,128)S(1)} %get-tuple-element.159, s32[8192]{0:T(1024)S(1)} %get-tuple-element.187, bf16[8,16,50,128]{3,2,1,0:T(8,128)(2,1)} %get-tuple-element.183, s32[]{:T(128)S(6)} %copy.40), kind=kOutput, calls=%fused_computation.6.clone.1 | convolution fusion | flops 1712324608 | bytes 4587524 | tf_op jit(solution)/shard_map/while/body/eval_jaxpr/wec,kc->wek/dot_general | solution.py:40
  141.0 9.3 %multiply_reduce_fusion.5 = (f32[16,64,128]{2,1,0:T(8,128)S(1)}, f32[16,64,128]{2,1,0:T(8,128)S(1)}) fusion(f32[16,50,64]{2,1,0:T(8,128)S(1)} %fusion.75, f32[50,64,128]{2,1,0:T(8,128)S(1)} %slice.59, f32[50,64,128]{2,1,0:T(8,128)S(1)} %slice.60), kind=kLoop, calls=%fused_computation.9.clone.1 | loop fusion | flops 25952256 | bytes 4530176 | tf_op jit(solution)/shard_map/while/body/eval_jaxpr/reduce_sum | solution.py:45
  153.0 13.0 %fusion.77 = (f32[16,8192]{1,0:T(8,128)S(1)}, f32[16,8192]{1,0:T(8,128)S(1)}) fusion(f32[50,8192]{1,0:T(8,128)S(1)} %get-tuple-element.160, f32[50,8192]{1,0:T(8,128)S(1)} %get-tuple-element.159, s32[8192]{0:T(1024)S(1)} %get-tuple-element.187, bf16[8,16,50,128]{3,2,1,0:T(8,128)(2,1)} %get-tuple-element.183, s32[]{:T(128)S(6)} %copy.40), kind=kOutput, calls=%fused_computation.6.clone.1 | convolution fusion | flops 1712324608 | bytes 4587524 | tf_op jit(solution)/shard_map/while/body/eval_jaxpr/wec,kc->wek/dot_general | solution.py:40
  166.9 9.3 %multiply_reduce_fusion.5 = (f32[16,64,128]{2,1,0:T(8,128)S(1)}, f32[16,64,128]{2,1,0:T(8,128)S(1)}) fusion(f32[16,50,64]{2,1,0:T(8,128)S(1)} %fusion.75, f32[50,64,128]{2,1,0:T(8,128)S(1)} %slice.59, f32[50,64,128]{2,1,0:T(8,128)S(1)} %slice.60), kind=kLoop, calls=%fused_computation.9.clone.1 | loop fusion | flops 25952256 | bytes 4530176 | tf_op jit(solution)/shard_map/while/body/eval_jaxpr/reduce_sum | solution.py:45
  177.3 1.2 fusion.75
  178.9 13.0 %fusion.77 = (f32[16,8192]{1,0:T(8,128)S(1)}, f32[16,8192]{1,0:T(8,128)S(1)}) fusion(f32[50,8192]{1,0:T(8,128)S(1)} %get-tuple-element.160, f32[50,8192]{1,0:T(8,128)S(1)} %get-tuple-element.159, s32[8192]{0:T(1024)S(1)} %get-tuple-element.187, bf16[8,16,50,128]{3,2,1,0:T(8,128)(2,1)} %get-tuple-element.183, s32[]{:T(128)S(6)} %copy.40), kind=kOutput, calls=%fused_computation.6.clone.1 | convolution fusion | flops 1712324608 | bytes 4587524 | tf_op jit(solution)/shard_map/while/body/eval_jaxpr/wec,kc->wek/dot_general | solution.py:40
  192.8 9.3 %multiply_reduce_fusion.5 = (f32[16,64,128]{2,1,0:T(8,128)S(1)}, f32[16,64,128]{2,1,0:T(8,128)S(1)}) fusion(f32[16,50,64]{2,1,0:T(8,128)S(1)} %fusion.75, f32[50,64,128]{2,1,0:T(8,128)S(1)} %slice.59, f32[50,64,128]{2,1,0:T(8,128)S(1)} %slice.60), kind=kLoop, calls=%fused_computation.9.clone.1 | loop fusion | flops 25952256 | bytes 4530176 | tf_op jit(solution)/shard_map/while/body/eval_jaxpr/reduce_sum | solution.py:45
  203.1 1.2 fusion.75
  204.7 13.0 %fusion.77 = (f32[16,8192]{1,0:T(8,128)S(1)}, f32[16,8192]{1,0:T(8,128)S(1)}) fusion(f32[50,8192]{1,0:T(8,128)S(1)} %get-tuple-element.160, f32[50,8192]{1,0:T(8,128)S(1)} %get-tuple-element.159, s32[8192]{0:T(1024)S(1)} %get-tuple-element.187, bf16[8,16,50,128]{3,2,1,0:T(8,128)(2,1)} %get-tuple-element.183, s32[]{:T(128)S(6)} %copy.40), kind=kOutput, calls=%fused_computation.6.clone.1 | convolution fusion | flops 1712324608 | bytes 4587524 | tf_op jit(solution)/shard_map/while/body/eval_jaxpr/wec,kc->wek/dot_general | solution.py:40
  218.6 9.3 %multiply_reduce_fusion.5 = (f32[16,64,128]{2,1,0:T(8,128)S(1)}, f32[16,64,128]{2,1,0:T(8,128)S(1)}) fusion(f32[16,50,64]{2,1,0:T(8,128)S(1)} %fusion.75, f32[50,64,128]{2,1,0:T(8,128)S(1)} %slice.59, f32[50,64,128]{2,1,0:T(8,128)S(1)} %slice.60), kind=kLoop, calls=%fused_computation.9.clone.1 | loop fusion | flops 25952256 | bytes 4530176 | tf_op jit(solution)/shard_map/while/body/eval_jaxpr/reduce_sum | solution.py:45
  229.0 1.2 fusion.75
  230.6 13.0 %fusion.77 = (f32[16,8192]{1,0:T(8,128)S(1)}, f32[16,8192]{1,0:T(8,128)S(1)}) fusion(f32[50,8192]{1,0:T(8,128)S(1)} %get-tuple-element.160, f32[50,8192]{1,0:T(8,128)S(1)} %get-tuple-element.159, s32[8192]{0:T(1024)S(1)} %get-tuple-element.187, bf16[8,16,50,128]{3,2,1,0:T(8,128)(2,1)} %get-tuple-element.183, s32[]{:T(128)S(6)} %copy.40), kind=kOutput, calls=%fused_computation.6.clone.1 | convolution fusion | flops 1712324608 | bytes 4587524 | tf_op jit(solution)/shard_map/while/body/eval_jaxpr/wec,kc->wek/dot_general | solution.py:40
  244.5 9.3 %multiply_reduce_fusion.5 = (f32[16,64,128]{2,1,0:T(8,128)S(1)}, f32[16,64,128]{2,1,0:T(8,128)S(1)}) fusion(f32[16,50,64]{2,1,0:T(8,128)S(1)} %fusion.75, f32[50,64,128]{2,1,0:T(8,128)S(1)} %slice.59, f32[50,64,128]{2,1,0:T(8,128)S(1)} %slice.60), kind=kLoop, calls=%fused_computation.9.clone.1 | loop fusion | flops 25952256 | bytes 4530176 | tf_op jit(solution)/shard_map/while/body/eval_jaxpr/reduce_sum | solution.py:45
  254.9 5.1 convolution_bitcast_fusion.1
  260.0 13.5 %psum.21 = f32[4,128]{1,0:T(4,128)S(1)} all-reduce(f32[4,128]{1,0:T(4,128)S(1)} %convolution_bitcast_fusion.1), channel_id=1, replica_groups=mesh['walk'=32,'det'=8] {'det'}, use_global_device_ids=true, to_apply=%region_6.7 | all-reduce | flops 512 | bytes 4096 | tf_op jit(solution)/shard_map/psum | solution.py:65
  273.6 71.8 %all-reduce = (f32[4]{0:T(128)S(1)}, f32[4]{0:T(128)S(1)}) all-reduce(f32[4]{0:T(128)S(1)} %get-tuple-element.81, f32[4]{0:T(128)S(1)} %get-tuple-element.80), channel_id=1, replica_groups=mesh['walk'=32,'det'=8] {'walk'}, use_global_device_ids=true, to_apply=%region_11.12 | all-reduce | flops 8 | bytes 64 | tf_op jit(solution)/shard_map/psum | solution.py:70
  345.4 9.9 %convolution_bitcast_fusion = f32[8192,4]{1,0:T(8,128)} fusion(f32[128,8192]{1,0:T(8,128)} %bitcast.90, f32[4,128]{1,0:T(4,128)S(1)} %copy-done.3, f32[4,128]{1,0:T(4,128)S(1)} %psum.21, f32[4]{0:T(128)S(1)} %get-tuple-element.96, f32[4]{0:T(128)S(1)} %div.28, f32[128]{0:T(128)S(1)} %broadcast_add_fusion), kind=kOutput, calls=%fused_computation.34 | convolution fusion | flops 50334208 | bytes 4330016
  356.0 213.8 %reduce-scatter.4.cloned.1.call-done = f32[256,4]{1,0:T(8,128)} async-done(((f32[8192,4]{1,0:T(8,128)}), f32[256,4]{1,0:T(8,128)}) %reduce-scatter.4.cloned.1.call-update) | async-done | bytes 4112
  (94 shorter events, 26.3 us)
Async XLA Ops:
  7.2 5.5 copy-start
  7.2 36.8 %all-gather.2.cloned.1.call-start = ((), (), s32[]{:S(2)}) async-start(), calls=%async_computation.1 | async-start | bytes 1843200 | tf_op jit(solution)/shard_map/all_gather | solution.py:61
  12.6 1.7 copy-start.2
  14.3 555.4 %reduce-scatter.4.cloned.1.call-start = ((), (), s32[]{:S(2)}) async-start(), calls=%async_computation.2 | async-start | bytes 4325376
  47.9 207.0 %copy-start.1 = (f32[4,8192]{1,0:T(4,128)S(1)}, f32[4,8192]{1,0:T(4,128)}, u32[]{:S(2)}) copy-start(f32[4,8192]{1,0:T(4,128)} %param.16) | copy-start | bytes 393220
  254.9 18.6 %copy-start.3 = (f32[4,128]{1,0:T(4,128)S(1)}, f32[4,128]{1,0:T(4,128)}, u32[]{:S(2)}) copy-start(f32[4,128]{1,0:T(4,128)} %param.17) | copy-start | bytes 6148
  345.4 9.9 %copy-start.4 = (f32[4]{0:T(128)}, f32[4]{0:T(128)S(1)}, u32[]{:S(2)}) copy-start(f32[4]{0:T(128)S(1)} %div.28) | copy-start | bytes 52
Sparse Core Ops, SparseCore 0:
  14.4 29.5 all-gather.1
  355.4 214.2 reduce-scatter.3
where the time goes:
time: 580 us; the launch traced here: 578 us
  waiting for transfers between devices  243 us (42%)
  matrix products  133 us (23%)
  blocking collectives  85.3 us (15%)
  other arithmetic  84.9 us (15%)
  local copies, waits for them, and re-layouts  17 us (3%)
  between operations  14.1 us (2%)
    unnamed x3, waiting for transfers between devices  214 us
    dot_general x8, matrix products, one_group(): jnp.einsum('wec,kc->wek', tables, pick_col, preferred_element_type=jnp.bf...  104 us
    reduce_sum x8, other arithmetic, one_group(): value_ia = jnp.sum(own_row * parent, axis=1)  74 us
    psum x1, blocking collectives, shards(): lax.psum((jnp.sum(weight, axis=1), jnp.sum(weight * local_energy, axis=1)...  71.8 us
    all_gather x1, waiting for transfers between devices, shards(): lax.all_gather(own_tables, 'det', axis=0, tiled=True)  29.5 us
    psum x1, blocking collectives, shards(): values = lax.psum(partial_values, 'det')  13.5 us
  transfers between devices with their start and end apart: 2, of which 2 were waited for; matrix products, arithmetic and copies ran while one was open for 0% of the time, Pallas kernels for 0%

commit v1 on v0

v1 whole, which is shorter than its diff:
```python
import functools

import jax
import jax.numpy as jnp
from jax import lax
from jax.experimental import pallas as pl
from jax.experimental.pallas import tpu as pltpu
from jax.sharding import PartitionSpec as P

NEL = 50
ROWS = 56
V = 128
NBAS = 512
STATES = 4
BLOCK = 128
OWN = 16
GROUP = 128
KD = 8192
NBLK = KD // BLOCK
PAIRS = NBLK // 2
JP = NEL // 2
NDET = 8
NWALK = 32
JPAD = 64
MIB = 1024 * 1024

F32, BF16 = jnp.float32, jnp.bfloat16
NN = (((1,), (0,)), ((), ()))
NT = (((1,), (1,)), ((), ()))


def dot(a, b, dims=NN):
    return lax.dot_general(a, b, dims, preferred_element_type=F32)


def split(x):
    hi = x.astype(BF16)
    return hi, (x - hi.astype(F32)).astype(BF16)


def vmem(n):
    return [pl.BlockSpec(memory_space=pltpu.VMEM)] * n


def table_kernel(pos_ref, inv_ref, cen_ref, exp_ref, orb_ref, out_ref, pos_s, basis_s, virt_s, inv_s, tab_s):
    pos_s[...] = jnp.zeros_like(pos_s)
    for c in range(3):
        pos_s[c * OWN:(c + 1) * OWN, 0:NEL] = pos_ref[c]
    cols = pos_s[...].T
    neg = -exp_ref[...]
    for w in range(OWN):
        dist = jnp.zeros((ROWS, NBAS), F32)
        for c in range(3):
            off = cols[0:ROWS, c * OWN + w:c * OWN + w + 1] - cen_ref[c:c + 1, :]
            dist = dist + off * off
        basis_s[w * ROWS:(w + 1) * ROWS, :] = jnp.exp(neg * dist)
    b_hi, b_lo = split(basis_s[...])
    o_hi, o_lo = split(orb_ref[...])
    virt_s[...] = jnp.zeros_like(virt_s)
    virt = dot(b_hi, o_hi) + (dot(b_hi, o_lo) + dot(b_lo, o_hi))
    for w in range(OWN):
        virt_s[w, 0:ROWS, :] = virt[w * ROWS:(w + 1) * ROWS]
    inv_s[...] = jnp.zeros_like(inv_s)
    for w in range(OWN):
        inv_s[w, 0:NEL, 0:NEL] = inv_ref[w]
    for w in range(OWN):
        i_hi, i_lo = split(inv_s[w])
        v_hi, v_lo = split(virt_s[w])
        table = dot(i_hi, v_hi) + (dot(i_hi, v_lo) + dot(i_lo, v_hi))
        tab_s[pl.ds(w, ROWS, stride=OWN), :] = table[0:ROWS]
    for i in range(NEL):
        out_ref[i // 2, :, (i % 2) * V:(i % 2 + 1) * V] = tab_s[i * OWN:(i + 1) * OWN, :].astype(BF16)


def prep_kernel(par_ref, exc_ref, coef_ref, chi_ref, clo_ref, obt_ref, ojt_ref, c16_ref, oa_ref, oa_s):
    lane = lax.broadcasted_iota(jnp.int32, (1, V), 1)

    def one_row(blk, _):
        oa_s[pl.ds(blk, 1), :] = jnp.where(lane == par_ref[1, blk], 1.0, 0.0).astype(F32)
        return _

    lax.fori_loop(0, NBLK, one_row, 0)
    oa_ref[...] = oa_s[...].astype(BF16)
    sub_b = lax.broadcasted_iota(jnp.int32, (V, 2 * BLOCK), 0)
    lane_b = lax.broadcasted_iota(jnp.int32, (2 * BLOCK, V), 1)
    half = lax.broadcasted_iota(jnp.int32, (8, 2 * BLOCK), 1) // BLOCK
    upper = lax.broadcasted_iota(jnp.int32, (8, 2 * BLOCK), 0) // STATES

    def quad(q, _):
        parts = []
        for h in range(2):
            at = pl.multiple_of((2 * q + h) * 2 * BLOCK, 2 * BLOCK)
            where = pl.ds(at, 2 * BLOCK)
            j_row, b_row = exc_ref[2:3, where], exc_ref[3:4, where]
            c4 = coef_ref[:, where]
            c8 = jnp.concatenate([c4, c4], axis=0)
            c_hi, c_lo = split(c8)
            c16_ref[:, where] = jnp.concatenate([c_hi.astype(F32), c_lo.astype(F32)], axis=0).astype(BF16)
            own = half == upper
            q_hi = jnp.where(own, c_hi.astype(F32), 0.0)
            q_lo = jnp.where(own, c_lo.astype(F32), 0.0)
            pick_b = jnp.where(sub_b == b_row, 1.0, 0.0).astype(BF16)
            w_hi, w_lo = [], []
            for jp in range(JP):
                m0, m1 = j_row == 2 * jp, j_row == 2 * jp + 1
                w_hi.append(jnp.concatenate([jnp.where(m0, q_hi, 0.0), jnp.where(m1, q_hi, 0.0)], axis=0).astype(BF16))
                w_lo.append(jnp.concatenate([jnp.where(m0, q_lo, 0.0), jnp.where(m1, q_lo, 0.0)], axis=0).astype(BF16))
            parts.append(dot(jnp.concatenate(w_hi, axis=0), pick_b, NT) + dot(jnp.concatenate(w_lo, axis=0), pick_b, NT))
            idx = jnp.concatenate([j_row, b_row, j_row, b_row, j_row, b_row, j_row, b_row], axis=0).astype(F32).T
            obt_ref[where, :] = jnp.where(idx[:, 1:2].astype(jnp.int32) == lane_b, 1.0, 0.0).astype(BF16)
            ojt_ref[where, :] = jnp.where(idx[:, 0:1].astype(jnp.int32) == lane_b, 1.0, 0.0).astype(BF16)
        rows = pl.ds(pl.multiple_of(q * 16, 16), 16)
        for j in range(NEL):
            both = jnp.concatenate([parts[0][j * 8:(j + 1) * 8], parts[1][j * 8:(j + 1) * 8]], axis=0)
            hi, lo = split(both)
            lanes = slice((j % 2) * V, (j % 2 + 1) * V)
            chi_ref[j // 2, rows, lanes] = hi
            clo_ref[j // 2, rows, lanes] = lo
        return _

    lax.fori_loop(0, PAIRS // 2, quad, 0)


def value_kernel(par_ref, me_ref, t0, t1, t2, t3, t4, t5, t6, t7, chi_ref, clo_ref, obt_ref, ojt_ref, c16_ref, oa_ref,
                 part_ref, tab_ref, p_ref, tia_ref, v_s, x_s, acc_s):
    me = me_ref[1]
    for d, t_ref in enumerate((t0, t1, t2, t3, t4, t5, t6, t7)):
        source = jnp.bitwise_xor(me, d)
        tab_ref[:, pl.ds(pl.multiple_of(source * OWN, OWN), OWN), :] = t_ref[...]
    for j in range(NEL, JPAD):
        v_s[pl.ds(j, NBLK, stride=JPAD), :] = jnp.zeros((NBLK, GROUP), F32)
    x_s[...] = jnp.zeros_like(x_s)
    pick_a = oa_ref[...]

    def over_rows(jp, _):
        t = tab_ref[jp]
        x_s[...] += dot(chi_ref[jp], t, NT) + dot(clo_ref[jp], t, NT)
        for j2 in range(2):
            v_s[pl.ds(2 * jp + j2, NBLK, stride=JPAD), :] = dot(pick_a, t[:, j2 * V:(j2 + 1) * V], NT)
        return _

    lax.fori_loop(0, JP, over_rows, 0)

    def own_entry(blk, _):
        row = v_s[pl.ds(blk * JPAD + par_ref[0, blk], 1), :]
        tia_ref[pl.ds(pl.multiple_of(blk * 8, 8), 8), :] = jnp.broadcast_to(row, (8, GROUP))
        return _

    lax.fori_loop(0, NBLK, own_entry, 0)
    acc_s[...] = jnp.zeros_like(acc_s)
    low = lax.broadcasted_iota(jnp.int32, (8, GROUP), 0) < STATES

    def pair(p, first):
        for h in range(2):
            blk = 2 * p + h
            dets = pl.ds(pl.multiple_of(blk * BLOCK, BLOCK), BLOCK)
            i = par_ref[0, blk]
            t_i = tab_ref[lax.shift_right_logical(i, 1), :, pl.ds(pl.multiple_of(jnp.bitwise_and(i, 1) * V, V), V)]
            along = dot(obt_ref[dets, :], t_i, NT)
            column = v_s[pl.ds(pl.multiple_of(blk * JPAD, JPAD), JPAD), :].astype(BF16)
            down = dot(ojt_ref[dets, 0:JPAD], column)
            hi, lo = split(along * down)
            p_ref[dets, 0:GROUP] = hi
            p_ref[dets, GROUP:2 * GROUP] = lo
        both = pl.ds(pl.multiple_of(p * 2 * BLOCK, 2 * BLOCK), 2 * BLOCK)
        acc_s[...] += dot(c16_ref[:, both], p_ref[both, :])
        tia = jnp.where(low, tia_ref[pl.ds(pl.multiple_of(p * 16, 16), 8), :],
                        tia_ref[pl.ds(pl.multiple_of(p * 16 + 8, 8), 8), :])
        return first + x_s[pl.ds(pl.multiple_of(p * 8, 8), 8), :] * tia

    first = lax.fori_loop(0, PAIRS, pair, jnp.zeros((8, GROUP), F32))
    first = first + jnp.concatenate([first[STATES:], first[:STATES]], axis=0)
    second = acc_s[0:8, :] + acc_s[8:16, :]
    part_ref[...] = first - (second[:, 0:GROUP] + second[:, GROUP:2 * GROUP])


def grad_kernel(me_ref, p0, p1, p2, p3, p4, p5, p6, p7, energy_ref, exc_ref, tab_ref, p_ref, tia_ref, *refs):
    val_ref, outs, (g_s, stage_s, order_s) = refs[0], refs[1:1 + NWALK], refs[1 + NWALK:]
    me = me_ref[0]
    for d, part in enumerate((p0, p1, p2, p3, p4, p5, p6, p7)):
        order_s[jnp.bitwise_xor(me_ref[1], d)] = part[...]
    val = order_s[0]
    for d in range(1, NDET):
        val = val + order_s[d]
    val_ref[...] = val
    low = lax.broadcasted_iota(jnp.int32, (8, GROUP), 0) < STATES
    lane = lax.broadcasted_iota(jnp.int32, (8, GROUP), 1)
    square = val * val
    guide = 1.0 + jnp.sum(jnp.where(low, square, 0.0), axis=0, keepdims=True)
    energy = jnp.concatenate([energy_ref[...], energy_ref[...]], axis=0)
    middle = jnp.sum(energy, axis=1, keepdims=True) * (1.0 / GROUP)
    scaled = val / guide
    weight = square / guide
    sums = jnp.sum(jnp.where(low, weight, weight * energy), axis=1, keepdims=True)
    meta = jnp.where(lane == 0, sums, jnp.where(lane == 1, middle, 0.0))
    factor = jnp.where(low, scaled * (energy - middle), scaled)
    f_hi, f_lo = split(factor)
    f16 = jnp.concatenate([f_hi.astype(F32), f_lo.astype(F32)], axis=0).astype(BF16)
    f16 = jnp.concatenate([f16, f16], axis=1)
    lhs = tia_ref[...].reshape(NBLK, 8, GROUP) * factor[None]
    l_hi, l_lo = split(lhs.reshape(NBLK * 8, GROUP))
    lhs = jnp.concatenate([l_hi, l_lo], axis=1)

    def over_rows(jp, _):
        t = tab_ref[jp]
        g = dot(lhs, jnp.concatenate([t, t], axis=0)).reshape(NBLK, 8, 2 * V)
        hi, lo = split(jnp.concatenate([g[:, :, 0:V], g[:, :, V:2 * V]], axis=1))
        rows = pl.ds(pl.multiple_of(jp * 16, 16), 16)
        g_s[:, rows, 0:V] = hi
        g_s[:, rows, V:2 * V] = lo
        return _

    lax.fori_loop(0, JP, over_rows, 0)
    sub_b = lax.broadcasted_iota(jnp.int32, (V, BLOCK), 0)

    def slot(d, _):
        p = jnp.bitwise_and(me + d, NWALK - 1)
        both = pl.ds(pl.multiple_of(p * 2 * BLOCK, 2 * BLOCK), 2 * BLOCK)
        second = dot(f16, p_ref[both, :], NT)
        second = second[0:8] + second[8:16]
        for h in range(2):
            dets = pl.ds(pl.multiple_of(p * 2 * BLOCK + h * BLOCK, BLOCK), BLOCK)
            j_row, b_row = exc_ref[2:3, dets], exc_ref[3:4, dets]
            pick_b = jnp.where(sub_b == b_row, 1.0, 0.0).astype(BF16)
            y = dot(g_s[2 * p + h], jnp.concatenate([pick_b, pick_b], axis=0))
            first = jnp.zeros((8, BLOCK), F32)
            for j in range(NEL):
                first = jnp.where(j_row == j, y[j * 8:(j + 1) * 8], first)
            stage_s[d, :, h * BLOCK:(h + 1) * BLOCK] = first - second[:, h * BLOCK:(h + 1) * BLOCK]
        stage_s[d, :, 2 * BLOCK:3 * BLOCK] = meta
        return _

    lax.fori_loop(0, NWALK, slot, 0)
    for d in range(NWALK):
        outs[d][...] = stage_s[d]


def final_kernel(me_ref, *refs):
    ins, (grad_ref, energy_ref, order_s) = refs[:NWALK], refs[NWALK:]
    for d in range(NWALK):
        order_s[jnp.bitwise_and(me_ref[0] - d + NWALK, NWALK - 1)] = ins[d][:, 256:384]
    meta = order_s[0]
    for d in range(1, NWALK):
        meta = meta + order_s[d]
    total, weighted = meta[0:STATES, 0:1], meta[STATES:8, 0:1]
    energy = weighted / total
    grad = jnp.zeros((STATES, 256), F32)
    for d in range(NWALK):
        grad = grad + (ins[d][0:STATES, 0:256] + (ins[d][0:STATES, 257:258] - energy) * ins[d][STATES:8, 0:256])
    grad_ref[...] = 2.0 * grad / total
    energy_ref[...] = jnp.broadcast_to(energy, (STATES, 128))


def params(mib):
    return pltpu.CompilerParams(vmem_limit_bytes=mib * MIB)


def make_table(positions, inverse, centers, exponent, orbital_weights):
    return pl.pallas_call(
        table_kernel,
        out_shape=jax.ShapeDtypeStruct((JP, OWN, 2 * V), BF16),
        in_specs=vmem(5), out_specs=vmem(1)[0],
        scratch_shapes=[pltpu.VMEM((128, 128), F32), pltpu.VMEM((OWN * ROWS, NBAS), F32),
                        pltpu.VMEM((OWN, 128, V), F32), pltpu.VMEM((OWN, JPAD, 128), F32),
                        pltpu.VMEM((ROWS * OWN, V), F32)],
        compiler_params=params(24), name="tables",
    )(positions, inverse, centers, exponent.reshape(1, NBAS), orbital_weights)


def prepare(parents, excitations, coeffs):
    return pl.pallas_call(
        prep_kernel,
        out_shape=[jax.ShapeDtypeStruct((JP, NBLK * STATES, 2 * V), BF16)] * 2
        + [jax.ShapeDtypeStruct((KD, V), BF16)] * 2
        + [jax.ShapeDtypeStruct((16, KD), BF16), jax.ShapeDtypeStruct((NBLK, V), BF16)],
        in_specs=[pl.BlockSpec(memory_space=pltpu.SMEM)] + vmem(2), out_specs=vmem(6),
        scratch_shapes=[pltpu.VMEM((NBLK, V), F32)],
        compiler_params=params(24), name="prepare",
    )(parents, excitations, coeffs)


def partial_values(parents, me, tables, prepared):
    return pl.pallas_call(
        value_kernel,
        out_shape=[jax.ShapeDtypeStruct((8, GROUP), F32), jax.ShapeDtypeStruct((JP, GROUP, 2 * V), BF16),
                   jax.ShapeDtypeStruct((KD, 2 * GROUP), BF16), jax.ShapeDtypeStruct((NBLK * 8, GROUP), F32)],
        in_specs=[pl.BlockSpec(memory_space=pltpu.SMEM)] * 2 + vmem(NDET + 6), out_specs=vmem(4),
        scratch_shapes=[pltpu.VMEM((NBLK * JPAD, GROUP), F32), pltpu.VMEM((NBLK * STATES, GROUP), F32),
                        pltpu.VMEM((16, 2 * GROUP), F32)],
        compiler_params=params(32), name="partial_values",
    )(parents, me, *tables, *prepared)


def gradient(me, parts, local_energy, excitations, tab, pair_products, tia):
    return pl.pallas_call(
        grad_kernel,
        out_shape=[jax.ShapeDtypeStruct((8, GROUP), F32)] + [jax.ShapeDtypeStruct((8, 384), F32)] * NWALK,
        in_specs=[pl.BlockSpec(memory_space=pltpu.SMEM)] + vmem(NDET + 5), out_specs=vmem(1 + NWALK),
        scratch_shapes=[pltpu.VMEM((NBLK, JP * 16, 2 * V), BF16), pltpu.VMEM((NWALK, 8, 384), F32),
                        pltpu.VMEM((NDET, 8, GROUP), F32)],
        compiler_params=params(40), name="gradient",
    )(me, *parts, local_energy, excitations, tab, pair_products, tia)


def finish(me, messages):
    return pl.pallas_call(
        final_kernel,
        out_shape=[jax.ShapeDtypeStruct((STATES, 256), F32), jax.ShapeDtypeStruct((STATES, 128), F32)],
        in_specs=[pl.BlockSpec(memory_space=pltpu.SMEM)] + vmem(NWALK), out_specs=vmem(2),
        scratch_shapes=[pltpu.VMEM((NWALK, 8, 128), F32)],
        compiler_params=params(8), name="finish",
    )(me, *messages)


def to_group(x):
    return [x] + [lax.ppermute(x, "det", [(i, i ^ d) for i in range(NDET)]) for d in range(1, NDET)]


def shards(positions, inverse, centers, exponent, orbital_weights, excitations, state_coeffs, local_energy):
    det, walk = lax.axis_index("det"), lax.axis_index("walk")
    tables = to_group(make_table(positions, inverse, centers, exponent, orbital_weights))
    me = jnp.stack([walk, det])
    parents = excitations[0:2, ::BLOCK]
    prepared = prepare(parents, excitations, state_coeffs)
    part, tab, products, tia = partial_values(parents, me, tables, prepared)
    values, *messages = gradient(me, to_group(part), local_energy, excitations, tab, products, tia)
    arrived = [messages[0]]
    for d in range(1, NWALK):
        arrived.append(lax.ppermute(messages[d], "walk", [(i, (i + d) % NWALK) for i in range(NWALK)]))
    grad, energy = finish(me, arrived)
    own = lax.dynamic_slice_in_dim(values[0:STATES], det * OWN, OWN, 1)
    return grad[:, None, :], own, energy[:, 0]


def solution(mesh):
    in_specs = (
        P(None, ("walk", "det"), None),
        P(("walk", "det"), None, None),
        P(),
        P(),
        P(),
        P(None, "det"),
        P(None, "det"),
        P(None, "walk"),
    )
    out_specs = (P(None, "det", "walk"), P(None, ("walk", "det")), P())
    return jax.shard_map(shards, mesh=mesh, in_specs=in_specs, out_specs=out_specs, check_vma=False)
```

time: 580 us -> 192 us (0.33)
  waiting for transfers between devices: 243 us -> 19.9 us
  matrix products: 133 us -> 0 us
  starting transfers between devices: 0.08 us -> 113 us
  blocking collectives: 85.3 us -> 0 us
  other arithmetic: 84.9 us -> 0.08 us
  Pallas kernels: 0 us -> 48.1 us
  between operations: 14.1 us -> 0.8 us
  local copies, waits for them, and re-layouts: 17 us -> 8.94 us
    unnamed x3 -> x0, waiting for transfers between devices: 214 us -> none
    dot_general x19 -> x0, matrix products: 123 us -> none  [the longest x8 104 us: one_group(): jnp.einsum('wec,kc->wek', tables, pick_col, preferred_element_type=jnp.bf...]
    ppermute x0 -> x45, starting transfers between devices: none -> 113 us  [the longest x31 98.4 us: shards(): lax.ppermute(messages[d], 'walk', [(i, (i + d) % NWALK) for i in range(NW...]
    psum x2 -> x0, blocking collectives: 85.3 us -> none  [the longest x1 71.8 us: shards(): lax.psum((jnp.sum(weight, axis=1), jnp.sum(weight * local_energy, axis=1)...]
    reduce_sum x10 -> x0, other arithmetic: 74.2 us -> none  [the longest x8 74 us: one_group(): value_ia = jnp.sum(own_row * parent, axis=1)]
    pallas_call x0 -> x5, Pallas kernels: none -> 48.1 us  [the longest x1 20 us: partial_values(): pl.pallas_call(value_kernel, out_shape=[jax.ShapeDtypeStruct((8, GROUP),...]
    all_gather x1 -> x0, waiting for transfers between devices: 29.5 us -> none  [shards(): lax.all_gather(own_tables, 'det', axis=0, tiled=True)]
    ppermute x0 -> x45, waiting for transfers between devices: none -> 19.9 us  [the longest x14 17.1 us: to_group(): lax.ppermute(x, 'det', [(i, i ^ d) for i in range(NDET)])]
  transfers between devices with their start and end apart: 2 -> 45, of which waited for: 2 -> 6; matrix products, arithmetic and copies ran while one was open for 0% -> 1% of each run, Pallas kernels for 0% -> 4%
where the time goes in v1:
time: 192 us; the launch traced here: 191 us
  starting transfers between devices  113 us (59%)
  Pallas kernels  48.1 us (25%)
  waiting for transfers between devices  19.9 us (10%)
  local copies, waits for them, and re-layouts  8.94 us (5%)
    ppermute x31, starting transfers between devices, shards(): lax.ppermute(messages[d], 'walk', [(i, (i + d) % NWALK) for i in range(NW...  98.4 us
    pallas_call x1, Pallas kernels, partial_values(): pl.pallas_call(value_kernel, out_shape=[jax.ShapeDtypeStruct((8, GROUP),...  20 us
    ppermute x14, waiting for transfers between devices, to_group(): lax.ppermute(x, 'det', [(i, i ^ d) for i in range(NDET)])  17.1 us
    pallas_call x1, Pallas kernels, gradient(): pl.pallas_call(grad_kernel, out_shape=[jax.ShapeDtypeStruct((8, GROUP), F...  16.6 us
    ppermute x14, starting transfers between devices, to_group(): lax.ppermute(x, 'det', [(i, i ^ d) for i in range(NDET)])  15.1 us
    pallas_call x1, Pallas kernels, prepare(): pl.pallas_call(prep_kernel, out_shape=[jax.ShapeDtypeStruct((JP, NBLK * S...  8.37 us
    unnamed x18, local copies, waits for them, and re-layouts  6.62 us
  transfers between devices with their start and end apart: 45, of which 6 were waited for; matrix products, arithmetic and copies ran while one was open for 1% of the time, Pallas kernels for 4%

profile of v1, /device:TPU:32, one launch (start us, length us, event | category | flops | bytes accessed | tf_op | source)
XLA Modules:
  0.0 191.3 jit_solution(17675028056785093708)
XLA Ops:
  4.8 2.3 %tables.1.t0 = bf16[25,16,256]{2,1,0:T(8,128)(2,1)S(1)} custom-call(f32[3,16,50]{2,1,0:T(8,128)S(1)} %copy-done.4, f32[16,50,50]{2,1,0:T(8,128)S(1)} %copy.13.inv_ref, f32[3,512]{1,0:T(4,128)S(1)} %copy-done.5, f32[1,512]{1,0:T(1,128)S(1)} %bitcast.5, f32[512,128]{1,0:T(8,128)S(1)} %copy-done.2), custom_call_target="tpu_custom_call" | custom-call | tf_op jit(solution)/shard_map/tables/pallas_call | solution.py:259
  7.2 2.3 %collective-permute-start.6 = (bf16[25,16,256]{2,1,0:T(8,128)(2,1)S(1)}, bf16[25,16,256]{2,1,0:T(8,128)(2,1)S(1)}, u32[]{:S(2)}, u32[]{:S(2)}) collective-permute-start(bf16[25,16,256]{2,1,0:T(8,128)(2,1)S(1)} %tables.1.t0), channel_id=1, source_target_pairs={{0,7},{1,6},{2,5},{3,4},{4,3},{5,2},{6,1},{7,0},{8,15},{9,14},{10,... | collective-permute-start | bytes 614408 | tf_op jit(solution)/shard_map/ppermute | solution.py:316
  13.5 11.1 %collective-permute-done.6.t7 = bf16[25,16,256]{2,1,0:T(8,128)(2,1)S(1)} collective-permute-done((bf16[25,16,256]{2,1,0:T(8,128)(2,1)S(1)}, bf16[25,16,256]{2,1,0:T(8,128)(2,1)S(1)}, u32[]{:S(2)}, u32[]{:S(2)}) %collective-permute-start.6) | collective-permute-done | bytes 204832 | tf_op jit(solution)/shard_map/ppermute | solution.py:316
  24.8 4.2 %collective-permute-done.5.t6 = bf16[25,16,256]{2,1,0:T(8,128)(2,1)S(1)} collective-permute-done((bf16[25,16,256]{2,1,0:T(8,128)(2,1)S(1)}, bf16[25,16,256]{2,1,0:T(8,128)(2,1)S(1)}, u32[]{:S(2)}, u32[]{:S(2)}) %collective-permute-start.5) | collective-permute-done | bytes 204832 | tf_op jit(solution)/shard_map/ppermute | solution.py:316
  31.9 8.4 %prepare.1 = (bf16[25,256,256]{2,1,0:T(8,128)(2,1)S(1)}, bf16[25,256,256]{2,1,0:T(8,128)(2,1)S(1)}, bf16[8192,128]{1,0:T(8,128)(2,1)S(1)}, bf16[8192,128]{1,0:T(...) custom-call(s32[2,64]{1,0:T(2,128)S(1)} %slice.9.par_ref, s32[4,8192]{1,0:T(4,128)S(1)} %copy-done, ...), custom_call_target="tpu_custom_call" | custom-call | tf_op jit(solution)/shard_map/prepare/pallas_call | solution.py:271
  40.4 20.0 %partial_values.1 = (f32[8,128]{1,0:T(8,128)S(1)}, bf16[25,128,256]{2,1,0:T(8,128)(2,1)S(1)}, bf16[8192,256]{1,0:T(8,128)(2,1)S(1)}, f32[512,128]{1,0:T(8,128)S(1)}) custom-call(s32[2,64]{1,0:T(2,128)S(1)} %slice.9.par_ref, s32[2]{0:T(128)S(1)} %pad_add_fusion.me_ref, bf16[25,16,256]{2,1,0:T(8,128)(2,1)S(1)} %tables.1.t0, ...), custom_call_target="tpu_custom_call" | custom-call | tf_op jit(solution)/shard_map/partial_values/pallas_call | solution.py:283
  60.4 2.9 %collective-permute-start.13 = (f32[8,128]{1,0:T(8,128)S(1)}, f32[8,128]{1,0:T(8,128)S(1)}, u32[]{:S(2)}, u32[]{:S(2)}) collective-permute-start(f32[8,128]{1,0:T(8,128)S(1)} %get-tuple-element.54.p0), channel_id=1, source_target_pairs={{0,7},{1,6},{2,5},{3,4},{4,3},{5,2},{6,1},{7,0},{8,15},{9,14},{10,... | collective-permute-start | bytes 12296 | tf_op jit(solution)/shard_map/ppermute | solution.py:316
  63.8 3.0 %collective-permute-start.10 = (f32[8,128]{1,0:T(8,128)S(1)}, f32[8,128]{1,0:T(8,128)S(1)}, u32[]{:S(2)}, u32[]{:S(2)}) collective-permute-start(f32[8,128]{1,0:T(8,128)S(1)} %get-tuple-element.54.p0), channel_id=1, source_target_pairs={{0,4},{1,5},{2,6},{3,7},{4,0},{5,1},{6,2},{7,3},{8,12},{9,13},{10,... | collective-permute-start | bytes 12296 | tf_op jit(solution)/shard_map/ppermute | solution.py:316
  70.7 16.6 %gradient.1 = (f32[8,128]{1,0:T(8,128)S(1)}, f32[8,384]{1,0:T(8,128)S(1)}, f32[8,384]{1,0:T(8,128)S(1)}, f32[8,384]{1,0:T(8,128)S(1)}, f32[8,384]{1,0:T(8,128)S(...) custom-call(s32[2]{0:T(128)S(1)} %pad_add_fusion.me_ref, ...), custom_call_target="tpu_custom_call" | custom-call | tf_op jit(solution)/shard_map/gradient/pallas_call | solution.py:295
  87.3 2.2 %collective-permute-start.14 = (f32[8,384]{1,0:T(8,128)S(1)}, f32[8,384]{1,0:T(8,128)S(1)}, u32[]{:S(2)}, u32[]{:S(2)}) collective-permute-start(f32[8,384]{1,0:T(8,128)S(1)} %get-tuple-element.59), channel_id=1, source_target_pairs={{0,8},{8,16},{16,24},{24,32},{32,40},{40,48},{48,56},{56,64},{64,7... | collective-permute-start | bytes 36872 | tf_op jit(solution)/shard_map/ppermute | solution.py:329
  89.6 4.4 %collective-permute-start.15 = (f32[8,384]{1,0:T(8,128)S(1)}, f32[8,384]{1,0:T(8,128)S(1)}, u32[]{:S(2)}, u32[]{:S(2)}) collective-permute-start(f32[8,384]{1,0:T(8,128)S(1)} %get-tuple-element.60), channel_id=1, source_target_pairs={{0,16},{8,24},{16,32},{24,40},{32,48},{40,56},{48,64},{56,72},{64,... | collective-permute-start | bytes 36872 | tf_op jit(solution)/shard_map/ppermute | solution.py:329
  94.0 2.1 %collective-permute-start.16 = (f32[8,384]{1,0:T(8,128)S(1)}, f32[8,384]{1,0:T(8,128)S(1)}, u32[]{:S(2)}, u32[]{:S(2)}) collective-permute-start(f32[8,384]{1,0:T(8,128)S(1)} %get-tuple-element.61), channel_id=1, source_target_pairs={{0,24},{8,32},{16,40},{24,48},{32,56},{40,64},{48,72},{56,80},{64,... | collective-permute-start | bytes 36872 | tf_op jit(solution)/shard_map/ppermute | solution.py:329
  96.1 2.3 %collective-permute-start.17 = (f32[8,384]{1,0:T(8,128)S(1)}, f32[8,384]{1,0:T(8,128)S(1)}, u32[]{:S(2)}, u32[]{:S(2)}) collective-permute-start(f32[8,384]{1,0:T(8,128)S(1)} %get-tuple-element.62), channel_id=1, source_target_pairs={{0,32},{8,40},{16,48},{24,56},{32,64},{40,72},{48,80},{56,88},{64,... | collective-permute-start | bytes 36872 | tf_op jit(solution)/shard_map/ppermute | solution.py:329
  98.4 3.4 %collective-permute-start.18 = (f32[8,384]{1,0:T(8,128)S(1)}, f32[8,384]{1,0:T(8,128)S(1)}, u32[]{:S(2)}, u32[]{:S(2)}) collective-permute-start(f32[8,384]{1,0:T(8,128)S(1)} %get-tuple-element.63), channel_id=1, source_target_pairs={{0,40},{8,48},{16,56},{24,64},{32,72},{40,80},{48,88},{56,96},{64,... | collective-permute-start | bytes 36872 | tf_op jit(solution)/shard_map/ppermute | solution.py:329
  101.8 3.1 %collective-permute-start.19 = (f32[8,384]{1,0:T(8,128)S(1)}, f32[8,384]{1,0:T(8,128)S(1)}, u32[]{:S(2)}, u32[]{:S(2)}) collective-permute-start(f32[8,384]{1,0:T(8,128)S(1)} %get-tuple-element.64), channel_id=1, source_target_pairs={{0,48},{8,56},{16,64},{24,72},{32,80},{40,88},{48,96},{56,104},{64... | collective-permute-start | bytes 36872 | tf_op jit(solution)/shard_map/ppermute | solution.py:329
  104.9 3.0 %collective-permute-start.20 = (f32[8,384]{1,0:T(8,128)S(1)}, f32[8,384]{1,0:T(8,128)S(1)}, u32[]{:S(2)}, u32[]{:S(2)}) collective-permute-start(f32[8,384]{1,0:T(8,128)S(1)} %get-tuple-element.65), channel_id=1, source_target_pairs={{0,56},{8,64},{16,72},{24,80},{32,88},{40,96},{48,104},{56,112},{6... | collective-permute-start | bytes 36872 | tf_op jit(solution)/shard_map/ppermute | solution.py:329
  108.9 2.7 %collective-permute-start.23 = (f32[8,384]{1,0:T(8,128)S(1)}, f32[8,384]{1,0:T(8,128)S(1)}, u32[]{:S(2)}, u32[]{:S(2)}) collective-permute-start(f32[8,384]{1,0:T(8,128)S(1)} %get-tuple-element.68), channel_id=1, source_target_pairs={{0,80},{8,88},{16,96},{24,104},{32,112},{40,120},{48,128},{56,136}... | collective-permute-start | bytes 36872 | tf_op jit(solution)/shard_map/ppermute | solution.py:329
  111.7 2.8 %collective-permute-start.24 = (f32[8,384]{1,0:T(8,128)S(1)}, f32[8,384]{1,0:T(8,128)S(1)}, u32[]{:S(2)}, u32[]{:S(2)}) collective-permute-start(f32[8,384]{1,0:T(8,128)S(1)} %get-tuple-element.69), channel_id=1, source_target_pairs={{0,88},{8,96},{16,104},{24,112},{32,120},{40,128},{48,136},{56,144... | collective-permute-start | bytes 36872 | tf_op jit(solution)/shard_map/ppermute | solution.py:329
  114.5 4.4 %collective-permute-start.25 = (f32[8,384]{1,0:T(8,128)S(1)}, f32[8,384]{1,0:T(8,128)S(1)}, u32[]{:S(2)}, u32[]{:S(2)}) collective-permute-start(f32[8,384]{1,0:T(8,128)S(1)} %get-tuple-element.70), channel_id=1, source_target_pairs={{0,96},{8,104},{16,112},{24,120},{32,128},{40,136},{48,144},{56,15... | collective-permute-start | bytes 36872 | tf_op jit(solution)/shard_map/ppermute | solution.py:329
  118.9 5.6 %collective-permute-start.26 = (f32[8,384]{1,0:T(8,128)S(1)}, f32[8,384]{1,0:T(8,128)S(1)}, u32[]{:S(2)}, u32[]{:S(2)}) collective-permute-start(f32[8,384]{1,0:T(8,128)S(1)} %get-tuple-element.71), channel_id=1, source_target_pairs={{0,104},{8,112},{16,120},{24,128},{32,136},{40,144},{48,152},{56,1... | collective-permute-start | bytes 36872 | tf_op jit(solution)/shard_map/ppermute | solution.py:329
  124.6 2.4 %collective-permute-start.28 = (f32[8,384]{1,0:T(8,128)S(1)}, f32[8,384]{1,0:T(8,128)S(1)}, u32[]{:S(2)}, u32[]{:S(2)}) collective-permute-start(f32[8,384]{1,0:T(8,128)S(1)} %get-tuple-element.73), channel_id=1, source_target_pairs={{0,120},{8,128},{16,136},{24,144},{32,152},{40,160},{48,168},{56,1... | collective-permute-start | bytes 36872 | tf_op jit(solution)/shard_map/ppermute | solution.py:329
  130.9 6.5 %collective-permute-start.31 = (f32[8,384]{1,0:T(8,128)S(1)}, f32[8,384]{1,0:T(8,128)S(1)}, u32[]{:S(2)}, u32[]{:S(2)}) collective-permute-start(f32[8,384]{1,0:T(8,128)S(1)} %get-tuple-element.76), channel_id=1, source_target_pairs={{0,144},{8,152},{16,160},{24,168},{32,176},{40,184},{48,192},{56,2... | collective-permute-start | bytes 36872 | tf_op jit(solution)/shard_map/ppermute | solution.py:329
  138.4 2.6 %collective-permute-start.33 = (f32[8,384]{1,0:T(8,128)S(1)}, f32[8,384]{1,0:T(8,128)S(1)}, u32[]{:S(2)}, u32[]{:S(2)}) collective-permute-start(f32[8,384]{1,0:T(8,128)S(1)} %get-tuple-element.78), channel_id=1, source_target_pairs={{0,160},{8,168},{16,176},{24,184},{32,192},{40,200},{48,208},{56,2... | collective-permute-start | bytes 36872 | tf_op jit(solution)/shard_map/ppermute | solution.py:329
  141.0 4.8 %collective-permute-start.34 = (f32[8,384]{1,0:T(8,128)S(1)}, f32[8,384]{1,0:T(8,128)S(1)}, u32[]{:S(2)}, u32[]{:S(2)}) collective-permute-start(f32[8,384]{1,0:T(8,128)S(1)} %get-tuple-element.79), channel_id=1, source_target_pairs={{0,168},{8,176},{16,184},{24,192},{32,200},{40,208},{48,216},{56,2... | collective-permute-start | bytes 36872 | tf_op jit(solution)/shard_map/ppermute | solution.py:329
  145.8 2.5 %collective-permute-start.35 = (f32[8,384]{1,0:T(8,128)S(1)}, f32[8,384]{1,0:T(8,128)S(1)}, u32[]{:S(2)}, u32[]{:S(2)}) collective-permute-start(f32[8,384]{1,0:T(8,128)S(1)} %get-tuple-element.80), channel_id=1, source_target_pairs={{0,176},{8,184},{16,192},{24,200},{32,208},{40,216},{48,224},{56,2... | collective-permute-start | bytes 36872 | tf_op jit(solution)/shard_map/ppermute | solution.py:329
  148.3 5.5 %collective-permute-start.36 = (f32[8,384]{1,0:T(8,128)S(1)}, f32[8,384]{1,0:T(8,128)S(1)}, u32[]{:S(2)}, u32[]{:S(2)}) collective-permute-start(f32[8,384]{1,0:T(8,128)S(1)} %get-tuple-element.81), channel_id=1, source_target_pairs={{0,184},{8,192},{16,200},{24,208},{32,216},{40,224},{48,232},{56,2... | collective-permute-start | bytes 36872 | tf_op jit(solution)/shard_map/ppermute | solution.py:329
  153.9 2.7 %collective-permute-start.39 = (f32[8,384]{1,0:T(8,128)S(1)}, f32[8,384]{1,0:T(8,128)S(1)}, u32[]{:S(2)}, u32[]{:S(2)}) collective-permute-start(f32[8,384]{1,0:T(8,128)S(1)} %get-tuple-element.84), channel_id=1, source_target_pairs={{0,208},{8,216},{16,224},{24,232},{32,240},{40,248},{48,0},{56,8},... | collective-permute-start | bytes 36872 | tf_op jit(solution)/shard_map/ppermute | solution.py:329
  158.1 3.3 %collective-permute-start.41 = (f32[8,384]{1,0:T(8,128)S(1)}, f32[8,384]{1,0:T(8,128)S(1)}, u32[]{:S(2)}, u32[]{:S(2)}) collective-permute-start(f32[8,384]{1,0:T(8,128)S(1)} %get-tuple-element.86), channel_id=1, source_target_pairs={{0,224},{8,232},{16,240},{24,248},{32,0},{40,8},{48,16},{56,24},{6... | collective-permute-start | bytes 36872 | tf_op jit(solution)/shard_map/ppermute | solution.py:329
  161.4 6.6 %collective-permute-start.42 = (f32[8,384]{1,0:T(8,128)S(1)}, f32[8,384]{1,0:T(8,128)S(1)}, u32[]{:S(2)}, u32[]{:S(2)}) collective-permute-start(f32[8,384]{1,0:T(8,128)S(1)} %get-tuple-element.87), channel_id=1, source_target_pairs={{0,232},{8,240},{16,248},{24,0},{32,8},{40,16},{48,24},{56,32},{64... | collective-permute-start | bytes 36872 | tf_op jit(solution)/shard_map/ppermute | solution.py:329
  168.1 6.0 %collective-permute-start.43 = (f32[8,384]{1,0:T(8,128)S(1)}, f32[8,384]{1,0:T(8,128)S(1)}, u32[]{:S(2)}, u32[]{:S(2)}) collective-permute-start(f32[8,384]{1,0:T(8,128)S(1)} %get-tuple-element.88), channel_id=1, source_target_pairs={{0,240},{8,248},{16,0},{24,8},{32,16},{40,24},{48,32},{56,40},{64,... | collective-permute-start | bytes 36872 | tf_op jit(solution)/shard_map/ppermute | solution.py:329
  174.0 11.8 %collective-permute-start.44 = (f32[8,384]{1,0:T(8,128)S(1)}, f32[8,384]{1,0:T(8,128)S(1)}, u32[]{:S(2)}, u32[]{:S(2)}) collective-permute-start(f32[8,384]{1,0:T(8,128)S(1)} %get-tuple-element.89), channel_id=1, source_target_pairs={{0,248},{8,0},{16,8},{24,16},{32,24},{40,32},{48,40},{56,48},{64,5... | collective-permute-start | bytes 36872 | tf_op jit(solution)/shard_map/ppermute | solution.py:329
  186.5 2.7 %collective-permute-done.44.refs_31_ = f32[8,384]{1,0:T(8,128)S(1)} collective-permute-done((f32[8,384]{1,0:T(8,128)S(1)}, f32[8,384]{1,0:T(8,128)S(1)}, u32[]{:S(2)}, u32[]{:S(2)}) %collective-permute-start.44) | collective-permute-done | bytes 12320 | tf_op jit(solution)/shard_map/ppermute | solution.py:329
  (86 shorter events, 26.3 us)
Async XLA Ops:
  7.2 17.3 %collective-permute-start.6 = (bf16[25,16,256]{2,1,0:T(8,128)(2,1)S(1)}, bf16[25,16,256]{2,1,0:T(8,128)(2,1)S(1)}, u32[]{:S(2)}, u32[]{:S(2)}) collective-permute-start(bf16[25,16,256]{2,1,0:T(8,128)(2,1)S(1)} %tables.1.t0), channel_id=1, source_target_pairs={{0,7},{1,6},{2,5},{3,4},{4,3},{5,2},{6,1},{7,0},{8,15},{9,14},{10,... | collective-permute-start | bytes 614408 | tf_op jit(solution)/shard_map/ppermute | solution.py:316
  9.4 19.6 %collective-permute-start.5 = (bf16[25,16,256]{2,1,0:T(8,128)(2,1)S(1)}, bf16[25,16,256]{2,1,0:T(8,128)(2,1)S(1)}, u32[]{:S(2)}, u32[]{:S(2)}) collective-permute-start(bf16[25,16,256]{2,1,0:T(8,128)(2,1)S(1)} %tables.1.t0), channel_id=1, source_target_pairs={{0,6},{1,7},{2,4},{3,5},{4,2},{5,3},{6,0},{7,1},{8,14},{9,15},{10,... | collective-permute-start | bytes 614408 | tf_op jit(solution)/shard_map/ppermute | solution.py:316
  10.1 30.2 %collective-permute-start.4 = (bf16[25,16,256]{2,1,0:T(8,128)(2,1)S(1)}, bf16[25,16,256]{2,1,0:T(8,128)(2,1)S(1)}, u32[]{:S(2)}, u32[]{:S(2)}) collective-permute-start(bf16[25,16,256]{2,1,0:T(8,128)(2,1)S(1)} %tables.1.t0), channel_id=1, source_target_pairs={{0,5},{1,4},{2,7},{3,6},{4,1},{5,0},{6,3},{7,2},{8,13},{9,12},{10,... | collective-permute-start | bytes 614408 | tf_op jit(solution)/shard_map/ppermute | solution.py:316
  11.8 28.6 %collective-permute-start.3 = (bf16[25,16,256]{2,1,0:T(8,128)(2,1)S(1)}, bf16[25,16,256]{2,1,0:T(8,128)(2,1)S(1)}, u32[]{:S(2)}, u32[]{:S(2)}) collective-permute-start(bf16[25,16,256]{2,1,0:T(8,128)(2,1)S(1)} %tables.1.t0), channel_id=1, source_target_pairs={{0,4},{1,5},{2,6},{3,7},{4,0},{5,1},{6,2},{7,3},{8,12},{9,13},{10,... | collective-permute-start | bytes 614408 | tf_op jit(solution)/shard_map/ppermute | solution.py:316
  13.5 26.9 %collective-permute-start.2 = (bf16[25,16,256]{2,1,0:T(8,128)(2,1)S(1)}, bf16[25,16,256]{2,1,0:T(8,128)(2,1)S(1)}, u32[]{:S(2)}, u32[]{:S(2)}) collective-permute-start(bf16[25,16,256]{2,1,0:T(8,128)(2,1)S(1)} %tables.1.t0), channel_id=1, source_target_pairs={{0,3},{1,2},{2,1},{3,0},{4,7},{5,6},{6,5},{7,4},{8,11},{9,10},{10,... | collective-permute-start | bytes 614408 | tf_op jit(solution)/shard_map/ppermute | solution.py:316
  24.5 15.8 %collective-permute-start.1 = (bf16[25,16,256]{2,1,0:T(8,128)(2,1)S(1)}, bf16[25,16,256]{2,1,0:T(8,128)(2,1)S(1)}, u32[]{:S(2)}, u32[]{:S(2)}) collective-permute-start(bf16[25,16,256]{2,1,0:T(8,128)(2,1)S(1)} %tables.1.t0), channel_id=1, source_target_pairs={{0,2},{1,3},{2,0},{3,1},{4,6},{5,7},{6,4},{7,5},{8,10},{9,11},{10,... | collective-permute-start | bytes 614408 | tf_op jit(solution)/shard_map/ppermute | solution.py:316
  29.0 11.4 %collective-permute-start = (bf16[25,16,256]{2,1,0:T(8,128)(2,1)S(1)}, bf16[25,16,256]{2,1,0:T(8,128)(2,1)S(1)}, u32[]{:S(2)}, u32[]{:S(2)}) collective-permute-start(bf16[25,16,256]{2,1,0:T(8,128)(2,1)S(1)} %tables.1.t0), channel_id=1, source_target_pairs={{0,1},{1,0},{2,3},{3,2},{4,5},{5,4},{6,7},{7,6},{8,9},{9,8},{10,11... | collective-permute-start | bytes 614408 | tf_op jit(solution)/shard_map/ppermute | solution.py:316
  87.3 14.4 %collective-permute-start.14 = (f32[8,384]{1,0:T(8,128)S(1)}, f32[8,384]{1,0:T(8,128)S(1)}, u32[]{:S(2)}, u32[]{:S(2)}) collective-permute-start(f32[8,384]{1,0:T(8,128)S(1)} %get-tuple-element.59), channel_id=1, source_target_pairs={{0,8},{8,16},{16,24},{24,32},{32,40},{40,48},{48,56},{56,64},{64,7... | collective-permute-start | bytes 36872 | tf_op jit(solution)/shard_map/ppermute | solution.py:329
  89.6 15.3 %collective-permute-start.15 = (f32[8,384]{1,0:T(8,128)S(1)}, f32[8,384]{1,0:T(8,128)S(1)}, u32[]{:S(2)}, u32[]{:S(2)}) collective-permute-start(f32[8,384]{1,0:T(8,128)S(1)} %get-tuple-element.60), channel_id=1, source_target_pairs={{0,16},{8,24},{16,32},{24,40},{32,48},{40,56},{48,64},{56,72},{64,... | collective-permute-start | bytes 36872 | tf_op jit(solution)/shard_map/ppermute | solution.py:329
  94.0 13.9 %collective-permute-start.16 = (f32[8,384]{1,0:T(8,128)S(1)}, f32[8,384]{1,0:T(8,128)S(1)}, u32[]{:S(2)}, u32[]{:S(2)}) collective-permute-start(f32[8,384]{1,0:T(8,128)S(1)} %get-tuple-element.61), channel_id=1, source_target_pairs={{0,24},{8,32},{16,40},{24,48},{32,56},{40,64},{48,72},{56,80},{64,... | collective-permute-start | bytes 36872 | tf_op jit(solution)/shard_map/ppermute | solution.py:329
  96.1 11.9 %collective-permute-start.17 = (f32[8,384]{1,0:T(8,128)S(1)}, f32[8,384]{1,0:T(8,128)S(1)}, u32[]{:S(2)}, u32[]{:S(2)}) collective-permute-start(f32[8,384]{1,0:T(8,128)S(1)} %get-tuple-element.62), channel_id=1, source_target_pairs={{0,32},{8,40},{16,48},{24,56},{32,64},{40,72},{48,80},{56,88},{64,... | collective-permute-start | bytes 36872 | tf_op jit(solution)/shard_map/ppermute | solution.py:329
  107.9 11.0 %collective-permute-start.21 = (f32[8,384]{1,0:T(8,128)S(1)}, f32[8,384]{1,0:T(8,128)S(1)}, u32[]{:S(2)}, u32[]{:S(2)}) collective-permute-start(f32[8,384]{1,0:T(8,128)S(1)} %get-tuple-element.66), channel_id=1, source_target_pairs={{0,64},{8,72},{16,80},{24,88},{32,96},{40,104},{48,112},{56,120},{... | collective-permute-start | bytes 36872 | tf_op jit(solution)/shard_map/ppermute | solution.py:329
  108.1 16.4 %collective-permute-start.22 = (f32[8,384]{1,0:T(8,128)S(1)}, f32[8,384]{1,0:T(8,128)S(1)}, u32[]{:S(2)}, u32[]{:S(2)}) collective-permute-start(f32[8,384]{1,0:T(8,128)S(1)} %get-tuple-element.67), channel_id=1, source_target_pairs={{0,72},{8,80},{16,88},{24,96},{32,104},{40,112},{48,120},{56,128},... | collective-permute-start | bytes 36872 | tf_op jit(solution)/shard_map/ppermute | solution.py:329
  108.9 15.7 %collective-permute-start.23 = (f32[8,384]{1,0:T(8,128)S(1)}, f32[8,384]{1,0:T(8,128)S(1)}, u32[]{:S(2)}, u32[]{:S(2)}) collective-permute-start(f32[8,384]{1,0:T(8,128)S(1)} %get-tuple-element.68), channel_id=1, source_target_pairs={{0,80},{8,88},{16,96},{24,104},{32,112},{40,120},{48,128},{56,136}... | collective-permute-start | bytes 36872 | tf_op jit(solution)/shard_map/ppermute | solution.py:329
  111.7 15.4 %collective-permute-start.24 = (f32[8,384]{1,0:T(8,128)S(1)}, f32[8,384]{1,0:T(8,128)S(1)}, u32[]{:S(2)}, u32[]{:S(2)}) collective-permute-start(f32[8,384]{1,0:T(8,128)S(1)} %get-tuple-element.69), channel_id=1, source_target_pairs={{0,88},{8,96},{16,104},{24,112},{32,120},{40,128},{48,136},{56,144... | collective-permute-start | bytes 36872 | tf_op jit(solution)/shard_map/ppermute | solution.py:329
  114.5 14.3 %collective-permute-start.25 = (f32[8,384]{1,0:T(8,128)S(1)}, f32[8,384]{1,0:T(8,128)S(1)}, u32[]{:S(2)}, u32[]{:S(2)}) collective-permute-start(f32[8,384]{1,0:T(8,128)S(1)} %get-tuple-element.70), channel_id=1, source_target_pairs={{0,96},{8,104},{16,112},{24,120},{32,128},{40,136},{48,144},{56,15... | collective-permute-start | bytes 36872 | tf_op jit(solution)/shard_map/ppermute | solution.py:329
  118.9 12.0 %collective-permute-start.26 = (f32[8,384]{1,0:T(8,128)S(1)}, f32[8,384]{1,0:T(8,128)S(1)}, u32[]{:S(2)}, u32[]{:S(2)}) collective-permute-start(f32[8,384]{1,0:T(8,128)S(1)} %get-tuple-element.71), channel_id=1, source_target_pairs={{0,104},{8,112},{16,120},{24,128},{32,136},{40,144},{48,152},{56,1... | collective-permute-start | bytes 36872 | tf_op jit(solution)/shard_map/ppermute | solution.py:329
  124.5 12.9 %collective-permute-start.27 = (f32[8,384]{1,0:T(8,128)S(1)}, f32[8,384]{1,0:T(8,128)S(1)}, u32[]{:S(2)}, u32[]{:S(2)}) collective-permute-start(f32[8,384]{1,0:T(8,128)S(1)} %get-tuple-element.72), channel_id=1, source_target_pairs={{0,112},{8,120},{16,128},{24,136},{32,144},{40,152},{48,160},{56,1... | collective-permute-start | bytes 36872 | tf_op jit(solution)/shard_map/ppermute | solution.py:329
  124.6 13.8 %collective-permute-start.28 = (f32[8,384]{1,0:T(8,128)S(1)}, f32[8,384]{1,0:T(8,128)S(1)}, u32[]{:S(2)}, u32[]{:S(2)}) collective-permute-start(f32[8,384]{1,0:T(8,128)S(1)} %get-tuple-element.73), channel_id=1, source_target_pairs={{0,120},{8,128},{16,136},{24,144},{32,152},{40,160},{48,168},{56,1... | collective-permute-start | bytes 36872 | tf_op jit(solution)/shard_map/ppermute | solution.py:329
  127.0 14.0 %collective-permute-start.29 = (f32[8,384]{1,0:T(8,128)S(1)}, f32[8,384]{1,0:T(8,128)S(1)}, u32[]{:S(2)}, u32[]{:S(2)}) collective-permute-start(f32[8,384]{1,0:T(8,128)S(1)} %get-tuple-element.74), channel_id=1, source_target_pairs={{0,128},{8,136},{16,144},{24,152},{32,160},{40,168},{48,176},{56,1... | collective-permute-start | bytes 36872 | tf_op jit(solution)/shard_map/ppermute | solution.py:329
  128.8 17.1 %collective-permute-start.30 = (f32[8,384]{1,0:T(8,128)S(1)}, f32[8,384]{1,0:T(8,128)S(1)}, u32[]{:S(2)}, u32[]{:S(2)}) collective-permute-start(f32[8,384]{1,0:T(8,128)S(1)} %get-tuple-element.75), channel_id=1, source_target_pairs={{0,136},{8,144},{16,152},{24,160},{32,168},{40,176},{48,184},{56,1... | collective-permute-start | bytes 36872 | tf_op jit(solution)/shard_map/ppermute | solution.py:329
  130.9 17.4 %collective-permute-start.31 = (f32[8,384]{1,0:T(8,128)S(1)}, f32[8,384]{1,0:T(8,128)S(1)}, u32[]{:S(2)}, u32[]{:S(2)}) collective-permute-start(f32[8,384]{1,0:T(8,128)S(1)} %get-tuple-element.76), channel_id=1, source_target_pairs={{0,144},{8,152},{16,160},{24,168},{32,176},{40,184},{48,192},{56,2... | collective-permute-start | bytes 36872 | tf_op jit(solution)/shard_map/ppermute | solution.py:329
  137.4 16.4 %collective-permute-start.32 = (f32[8,384]{1,0:T(8,128)S(1)}, f32[8,384]{1,0:T(8,128)S(1)}, u32[]{:S(2)}, u32[]{:S(2)}) collective-permute-start(f32[8,384]{1,0:T(8,128)S(1)} %get-tuple-element.77), channel_id=1, source_target_pairs={{0,152},{8,160},{16,168},{24,176},{32,184},{40,192},{48,200},{56,2... | collective-permute-start | bytes 36872 | tf_op jit(solution)/shard_map/ppermute | solution.py:329
  138.4 15.5 %collective-permute-start.33 = (f32[8,384]{1,0:T(8,128)S(1)}, f32[8,384]{1,0:T(8,128)S(1)}, u32[]{:S(2)}, u32[]{:S(2)}) collective-permute-start(f32[8,384]{1,0:T(8,128)S(1)} %get-tuple-element.78), channel_id=1, source_target_pairs={{0,160},{8,168},{16,176},{24,184},{32,192},{40,200},{48,208},{56,2... | collective-permute-start | bytes 36872 | tf_op jit(solution)/shard_map/ppermute | solution.py:329
  141.0 12.9 %collective-permute-start.34 = (f32[8,384]{1,0:T(8,128)S(1)}, f32[8,384]{1,0:T(8,128)S(1)}, u32[]{:S(2)}, u32[]{:S(2)}) collective-permute-start(f32[8,384]{1,0:T(8,128)S(1)} %get-tuple-element.79), channel_id=1, source_target_pairs={{0,168},{8,176},{16,184},{24,192},{32,200},{40,208},{48,216},{56,2... | collective-permute-start | bytes 36872 | tf_op jit(solution)/shard_map/ppermute | solution.py:329
  153.9 14.2 %collective-permute-start.38 = (f32[8,384]{1,0:T(8,128)S(1)}, f32[8,384]{1,0:T(8,128)S(1)}, u32[]{:S(2)}, u32[]{:S(2)}) collective-permute-start(f32[8,384]{1,0:T(8,128)S(1)} %get-tuple-element.83), channel_id=1, source_target_pairs={{0,200},{8,208},{16,216},{24,224},{32,232},{40,240},{48,248},{56,0... | collective-permute-start | bytes 36872 | tf_op jit(solution)/shard_map/ppermute | solution.py:329
  153.9 20.1 %collective-permute-start.39 = (f32[8,384]{1,0:T(8,128)S(1)}, f32[8,384]{1,0:T(8,128)S(1)}, u32[]{:S(2)}, u32[]{:S(2)}) collective-permute-start(f32[8,384]{1,0:T(8,128)S(1)} %get-tuple-element.84), channel_id=1, source_target_pairs={{0,208},{8,216},{16,224},{24,232},{32,240},{40,248},{48,0},{56,8},... | collective-permute-start | bytes 36872 | tf_op jit(solution)/shard_map/ppermute | solution.py:329
  156.6 29.9 %collective-permute-start.40 = (f32[8,384]{1,0:T(8,128)S(1)}, f32[8,384]{1,0:T(8,128)S(1)}, u32[]{:S(2)}, u32[]{:S(2)}) collective-permute-start(f32[8,384]{1,0:T(8,128)S(1)} %get-tuple-element.85), channel_id=1, source_target_pairs={{0,216},{8,224},{16,232},{24,240},{32,248},{40,0},{48,8},{56,16},{... | collective-permute-start | bytes 36872 | tf_op jit(solution)/shard_map/ppermute | solution.py:329
  158.1 28.4 %collective-permute-start.41 = (f32[8,384]{1,0:T(8,128)S(1)}, f32[8,384]{1,0:T(8,128)S(1)}, u32[]{:S(2)}, u32[]{:S(2)}) collective-permute-start(f32[8,384]{1,0:T(8,128)S(1)} %get-tuple-element.86), channel_id=1, source_target_pairs={{0,224},{8,232},{16,240},{24,248},{32,0},{40,8},{48,16},{56,24},{6... | collective-permute-start | bytes 36872 | tf_op jit(solution)/shard_map/ppermute | solution.py:329
  161.4 25.1 %collective-permute-start.42 = (f32[8,384]{1,0:T(8,128)S(1)}, f32[8,384]{1,0:T(8,128)S(1)}, u32[]{:S(2)}, u32[]{:S(2)}) collective-permute-start(f32[8,384]{1,0:T(8,128)S(1)} %get-tuple-element.87), channel_id=1, source_target_pairs={{0,232},{8,240},{16,248},{24,0},{32,8},{40,16},{48,24},{56,32},{64... | collective-permute-start | bytes 36872 | tf_op jit(solution)/shard_map/ppermute | solution.py:329
  168.1 18.5 %collective-permute-start.43 = (f32[8,384]{1,0:T(8,128)S(1)}, f32[8,384]{1,0:T(8,128)S(1)}, u32[]{:S(2)}, u32[]{:S(2)}) collective-permute-start(f32[8,384]{1,0:T(8,128)S(1)} %get-tuple-element.88), channel_id=1, source_target_pairs={{0,240},{8,248},{16,0},{24,8},{32,16},{40,24},{48,32},{56,40},{64,... | collective-permute-start | bytes 36872 | tf_op jit(solution)/shard_map/ppermute | solution.py:329
  174.0 15.2 %collective-permute-start.44 = (f32[8,384]{1,0:T(8,128)S(1)}, f32[8,384]{1,0:T(8,128)S(1)}, u32[]{:S(2)}, u32[]{:S(2)}) collective-permute-start(f32[8,384]{1,0:T(8,128)S(1)} %get-tuple-element.89), channel_id=1, source_target_pairs={{0,248},{8,0},{16,8},{24,16},{32,24},{40,32},{48,40},{56,48},{64,5... | collective-permute-start | bytes 36872 | tf_op jit(solution)/shard_map/ppermute | solution.py:329
  (21 other events, 154.7 us)

commit v2 on v1

v2 whole, which is shorter than its diff:
```python
import jax
import jax.numpy as jnp
from jax import lax
from jax.experimental import pallas as pl
from jax.experimental.pallas import tpu as pltpu
from jax.sharding import PartitionSpec as P

NEL = 50
ROWS = 56
V = 128
NBAS = 512
STATES = 4
BLOCK = 128
OWN = 16
GROUP = 128
KD = 8192
NBLK = KD // BLOCK
PAIRS = NBLK // 2
JP = NEL // 2
NDET = 8
NWALK = 32
JPAD = 64
MIB = 1024 * 1024

F32, BF16 = jnp.float32, jnp.bfloat16
NN = (((1,), (0,)), ((), ()))
NT = (((1,), (1,)), ((), ()))


def dot(a, b, dims=NN):
    return lax.dot_general(a, b, dims, preferred_element_type=F32)


def split(x):
    hi = x.astype(BF16)
    return hi, (x - hi.astype(F32)).astype(BF16)


def vmem(n):
    return [pl.BlockSpec(memory_space=pltpu.VMEM)] * n


def table_kernel(pos_hbm, inv_hbm, cen_hbm, exp_hbm, orb_hbm, out_ref, pos_ref, inv_ref, cen_ref, exp_ref, orb_ref,
                 pos_s, basis_s, virt_s, inv_s, tab_s, sems):
    copies = [pltpu.make_async_copy(src, dst, sems.at[n]) for n, (src, dst) in enumerate(
        ((pos_hbm, pos_ref), (cen_hbm, cen_ref), (exp_hbm, exp_ref), (orb_hbm, orb_ref), (inv_hbm, inv_ref)))]
    for copy in copies:
        copy.start()
    pos_s[...] = jnp.zeros_like(pos_s)
    virt_s[...] = jnp.zeros_like(virt_s)
    inv_s[...] = jnp.zeros_like(inv_s)
    for copy in copies[:3]:
        copy.wait()
    for c in range(3):
        pos_s[c * OWN:(c + 1) * OWN, 0:NEL] = pos_ref[c]
    cols = pos_s[...].T
    neg = -exp_ref[...]
    for w in range(OWN):
        dist = jnp.zeros((ROWS, NBAS), F32)
        for c in range(3):
            off = cols[0:ROWS, c * OWN + w:c * OWN + w + 1] - cen_ref[c:c + 1, :]
            dist = dist + off * off
        basis_s[w * ROWS:(w + 1) * ROWS, :] = jnp.exp(neg * dist)
    b_hi, b_lo = split(basis_s[...])
    copies[3].wait()
    o_hi, o_lo = split(orb_ref[...])
    virt = dot(b_hi, o_hi) + (dot(b_hi, o_lo) + dot(b_lo, o_hi))
    for w in range(OWN):
        virt_s[w, 0:ROWS, :] = virt[w * ROWS:(w + 1) * ROWS]
    copies[4].wait()
    for w in range(OWN):
        inv_s[w, 0:NEL, 0:NEL] = inv_ref[:, w, :]
    for w in range(OWN):
        i_hi, i_lo = split(inv_s[w])
        v_hi, v_lo = split(virt_s[w])
        table = dot(i_hi, v_hi) + (dot(i_hi, v_lo) + dot(i_lo, v_hi))
        tab_s[pl.ds(w, ROWS, stride=OWN), :] = table[0:ROWS]
    for i in range(NEL):
        out_ref[i // 2, :, (i % 2) * V:(i % 2 + 1) * V] = tab_s[i * OWN:(i + 1) * OWN, :].astype(BF16)


def picks_kernel(exc_smem, exc_ref, coef_ref, obt_ref, ojt_ref, c16_ref, oa_ref, oa_s):
    lane = lax.broadcasted_iota(jnp.int32, (1, V), 1)

    def one_row(blk, _):
        oa_s[pl.ds(blk, 1), :] = jnp.where(lane == exc_smem[1, blk * BLOCK], 1.0, 0.0).astype(F32)
        return _

    lax.fori_loop(0, NBLK, one_row, 0)
    oa_ref[...] = oa_s[...].astype(BF16)
    lane_b = lax.broadcasted_iota(jnp.int32, (2 * BLOCK, V), 1)

    def pair(p, _):
        where = pl.ds(pl.multiple_of(p * 2 * BLOCK, 2 * BLOCK), 2 * BLOCK)
        c4 = coef_ref[:, where]
        c_hi, c_lo = split(jnp.concatenate([c4, c4], axis=0))
        c16_ref[:, where] = jnp.concatenate([c_hi.astype(F32), c_lo.astype(F32)], axis=0).astype(BF16)
        both = exc_ref[2:4, where]
        idx = jnp.concatenate([both, both, both, both], axis=0).astype(F32).T
        obt_ref[where, :] = jnp.where(idx[:, 1:2].astype(jnp.int32) == lane_b, 1.0, 0.0).astype(BF16)
        ojt_ref[where, :] = jnp.where(idx[:, 0:1].astype(jnp.int32) == lane_b, 1.0, 0.0).astype(BF16)
        return _

    lax.fori_loop(0, PAIRS, pair, 0)


def spread_kernel(exc_ref, coef_ref, chi_ref, clo_ref):
    sub_b = lax.broadcasted_iota(jnp.int32, (V, 2 * BLOCK), 0)
    half = lax.broadcasted_iota(jnp.int32, (8, 2 * BLOCK), 1) // BLOCK
    upper = lax.broadcasted_iota(jnp.int32, (8, 2 * BLOCK), 0) // STATES

    def quad(q, _):
        parts = []
        for h in range(2):
            where = pl.ds(pl.multiple_of((2 * q + h) * 2 * BLOCK, 2 * BLOCK), 2 * BLOCK)
            j_row, b_row = exc_ref[2:3, where], exc_ref[3:4, where]
            c4 = coef_ref[:, where]
            c_hi, c_lo = split(jnp.concatenate([c4, c4], axis=0))
            own = half == upper
            q_hi = jnp.where(own, c_hi.astype(F32), 0.0)
            q_lo = jnp.where(own, c_lo.astype(F32), 0.0)
            pick_b = jnp.where(sub_b == b_row, 1.0, 0.0).astype(BF16)
            w_hi, w_lo = [], []
            for jp in range(JP):
                m0, m1 = j_row == 2 * jp, j_row == 2 * jp + 1
                w_hi.append(jnp.concatenate([jnp.where(m0, q_hi, 0.0), jnp.where(m1, q_hi, 0.0)], axis=0).astype(BF16))
                w_lo.append(jnp.concatenate([jnp.where(m0, q_lo, 0.0), jnp.where(m1, q_lo, 0.0)], axis=0).astype(BF16))
            parts.append(dot(jnp.concatenate(w_hi, axis=0), pick_b, NT) + dot(jnp.concatenate(w_lo, axis=0), pick_b, NT))
        rows = pl.ds(pl.multiple_of(q * 16, 16), 16)
        for j in range(NEL):
            both = jnp.concatenate([parts[0][j * 8:(j + 1) * 8], parts[1][j * 8:(j + 1) * 8]], axis=0)
            hi, lo = split(both)
            lanes = slice((j % 2) * V, (j % 2 + 1) * V)
            chi_ref[j // 2, rows, lanes] = hi
            clo_ref[j // 2, rows, lanes] = lo
        return _

    lax.fori_loop(0, PAIRS // 2, quad, 0)


def value_kernel(exc_smem, me_ref, t0, t1, t2, t3, t4, t5, t6, t7, chi_ref, clo_ref, obt_ref, ojt_ref, c16_ref, oa_ref,
                 part_ref, tab_ref, p_ref, tia_ref, v_s, x_s, acc_s):
    x, c = lax.shift_right_logical(me_ref[1], 1), jnp.bitwise_and(me_ref[1], 1)
    ahead = 1 - 2 * c
    sources = ((x, c), (x - ahead, c), (x + ahead, c), (x + 2, c),
               (x, 1 - c), (x + ahead, 1 - c), (x - ahead, 1 - c), (x + 2, 1 - c))
    for t_ref, (xx, cc) in zip((t0, t1, t2, t3, t4, t5, t6, t7), sources):
        source = 2 * jnp.bitwise_and(xx + 4, 3) + cc
        tab_ref[:, pl.ds(pl.multiple_of(source * OWN, OWN), OWN), :] = t_ref[...]
    for j in range(NEL, JPAD):
        v_s[pl.ds(j, NBLK, stride=JPAD), :] = jnp.zeros((NBLK, GROUP), F32)
    x_s[...] = jnp.zeros_like(x_s)
    pick_a = oa_ref[...]

    def over_rows(jp, _):
        t = tab_ref[jp]
        x_s[...] += dot(chi_ref[jp], t, NT) + dot(clo_ref[jp], t, NT)
        for j2 in range(2):
            v_s[pl.ds(2 * jp + j2, NBLK, stride=JPAD), :] = dot(pick_a, t[:, j2 * V:(j2 + 1) * V], NT)
        return _

    lax.fori_loop(0, JP, over_rows, 0)

    def own_entry(blk, _):
        row = v_s[pl.ds(blk * JPAD + exc_smem[0, blk * BLOCK], 1), :]
        tia_ref[pl.ds(pl.multiple_of(blk * 8, 8), 8), :] = jnp.broadcast_to(row, (8, GROUP))
        return _

    lax.fori_loop(0, NBLK, own_entry, 0)
    acc_s[...] = jnp.zeros_like(acc_s)
    low = lax.broadcasted_iota(jnp.int32, (8, GROUP), 0) < STATES

    def pair(p, first):
        for h in range(2):
            blk = 2 * p + h
            dets = pl.ds(pl.multiple_of(blk * BLOCK, BLOCK), BLOCK)
            i = exc_smem[0, blk * BLOCK]
            t_i = tab_ref[lax.shift_right_logical(i, 1), :, pl.ds(pl.multiple_of(jnp.bitwise_and(i, 1) * V, V), V)]
            along = dot(obt_ref[dets, :], t_i, NT)
            column = v_s[pl.ds(pl.multiple_of(blk * JPAD, JPAD), JPAD), :].astype(BF16)
            down = dot(ojt_ref[dets, 0:JPAD], column)
            hi, lo = split(along * down)
            p_ref[dets, 0:GROUP] = hi
            p_ref[dets, GROUP:2 * GROUP] = lo
        both = pl.ds(pl.multiple_of(p * 2 * BLOCK, 2 * BLOCK), 2 * BLOCK)
        acc_s[...] += dot(c16_ref[:, both], p_ref[both, :])
        tia = jnp.where(low, tia_ref[pl.ds(pl.multiple_of(p * 16, 16), 8), :],
                        tia_ref[pl.ds(pl.multiple_of(p * 16 + 8, 8), 8), :])
        return first + x_s[pl.ds(pl.multiple_of(p * 8, 8), 8), :] * tia

    first = lax.fori_loop(0, PAIRS, pair, jnp.zeros((8, GROUP), F32))
    first = first + jnp.concatenate([first[STATES:], first[:STATES]], axis=0)
    second = acc_s[0:8, :] + acc_s[8:16, :]
    part_ref[...] = first - (second[:, 0:GROUP] + second[:, GROUP:2 * GROUP])


def grad_kernel(me_ref, p0, p1, p2, p3, energy_ref, exc_ref, tab_ref, p_ref, tia_ref, own_ref, out_ref, g_s, order_s):
    me = me_ref[1]
    for d, part in enumerate((p0, p1, p2, p3)):
        order_s[jnp.bitwise_and(lax.shift_right_logical(me, 1) - d + 4, 3)] = part[...]
    val = (order_s[0] + order_s[1]) + (order_s[2] + order_s[3])
    own = val[0:STATES, 0:OWN]
    for d in range(1, NDET):
        own = jnp.where(me == d, val[0:STATES, d * OWN:(d + 1) * OWN], own)
    own_ref[...] = own
    low = lax.broadcasted_iota(jnp.int32, (8, GROUP), 0) < STATES
    lane = lax.broadcasted_iota(jnp.int32, (8, GROUP), 1)
    square = val * val
    guide = 1.0 + jnp.sum(jnp.where(low, square, 0.0), axis=0, keepdims=True)
    energy = jnp.concatenate([energy_ref[...], energy_ref[...]], axis=0)
    middle = jnp.sum(energy, axis=1, keepdims=True) * (1.0 / GROUP)
    scaled = val / guide
    weight = square / guide
    sums = jnp.sum(jnp.where(low, weight, weight * energy), axis=1, keepdims=True)
    meta = jnp.where(lane == 0, sums, jnp.where(lane == 1, middle, 0.0))
    factor = jnp.where(low, scaled * (energy - middle), scaled)
    f_hi, f_lo = split(factor)
    f16 = jnp.concatenate([f_hi.astype(F32), f_lo.astype(F32)], axis=0).astype(BF16)
    f16 = jnp.concatenate([f16, f16], axis=1)
    lhs = tia_ref[...].reshape(NBLK, 8, GROUP) * factor[None]
    l_hi, l_lo = split(lhs.reshape(NBLK * 8, GROUP))
    lhs = jnp.concatenate([l_hi, l_lo], axis=1)

    def over_rows(jp, _):
        t = tab_ref[jp]
        g = dot(lhs, jnp.concatenate([t, t], axis=0)).reshape(NBLK, 8, 2 * V)
        hi, lo = split(jnp.concatenate([g[:, :, 0:V], g[:, :, V:2 * V]], axis=1))
        rows = pl.ds(pl.multiple_of(jp * 16, 16), 16)
        g_s[:, rows, 0:V] = hi
        g_s[:, rows, V:2 * V] = lo
        return _

    lax.fori_loop(0, JP, over_rows, 0)
    sub_b = lax.broadcasted_iota(jnp.int32, (V, BLOCK), 0)

    def slot(p, _):
        both = pl.ds(pl.multiple_of(p * 2 * BLOCK, 2 * BLOCK), 2 * BLOCK)
        second = dot(f16, p_ref[both, :], NT)
        second = second[0:8] + second[8:16]
        for h in range(2):
            dets = pl.ds(pl.multiple_of(p * 2 * BLOCK + h * BLOCK, BLOCK), BLOCK)
            j_row, b_row = exc_ref[2:3, dets], exc_ref[3:4, dets]
            pick_b = jnp.where(sub_b == b_row, 1.0, 0.0).astype(BF16)
            y = dot(g_s[2 * p + h], jnp.concatenate([pick_b, pick_b], axis=0))
            first = jnp.zeros((8, BLOCK), F32)
            for j in range(NEL):
                first = jnp.where(j_row == j, y[j * 8:(j + 1) * 8], first)
            out_ref[p, :, h * BLOCK:(h + 1) * BLOCK] = first - second[:, h * BLOCK:(h + 1) * BLOCK]
        out_ref[p, :, 2 * BLOCK:3 * BLOCK] = meta
        return _

    lax.fori_loop(0, NWALK, slot, 0)


def final_kernel(in_ref, grad_ref, energy_ref):
    meta = in_ref[0, :, 256:384]
    for g in range(1, NWALK):
        meta = meta + in_ref[g, :, 256:384]
    total, weighted = meta[0:STATES, 0:1], meta[STATES:8, 0:1]
    energy = weighted / total
    grad = jnp.zeros((STATES, 256), F32)
    for g in range(NWALK):
        shift = in_ref[g, 0:STATES, 257:258] - energy
        grad = grad + (in_ref[g, 0:STATES, 0:256] + shift * in_ref[g, STATES:8, 0:256])
    grad_ref[:, 0, :] = 2.0 * grad / total
    place = lax.broadcasted_iota(jnp.int32, (STATES, STATES), 0) == lax.broadcasted_iota(jnp.int32, (STATES, STATES), 1)
    energy_ref[...] = jnp.sum(jnp.where(place, energy, 0.0), axis=0, keepdims=True)


def params(mib):
    return pltpu.CompilerParams(vmem_limit_bytes=mib * MIB)


def make_table(positions, inverse, centers, exponent, orbital_weights):
    return pl.pallas_call(
        table_kernel,
        out_shape=jax.ShapeDtypeStruct((JP, OWN, 2 * V), BF16),
        in_specs=[pl.BlockSpec(memory_space=pltpu.HBM)] * 5, out_specs=vmem(1)[0],
        scratch_shapes=[pltpu.VMEM((3, OWN, NEL), F32), pltpu.VMEM((NEL, OWN, NEL), F32), pltpu.VMEM((3, NBAS), F32),
                        pltpu.VMEM((1, NBAS), F32), pltpu.VMEM((NBAS, V), F32), pltpu.VMEM((128, 128), F32), pltpu.VMEM((OWN * ROWS, NBAS), F32),
                        pltpu.VMEM((OWN, 128, V), F32), pltpu.VMEM((OWN, JPAD, 128), F32),
                        pltpu.VMEM((ROWS * OWN, V), F32), pltpu.SemaphoreType.DMA((5,))],
        compiler_params=params(8), name="tables",
    )(positions, inverse.transpose(1, 0, 2), centers, exponent.reshape(1, NBAS), orbital_weights)


def cost(flops):
    return pl.CostEstimate(flops=flops, bytes_accessed=8 * MIB, transcendentals=0)


def picks(excitations, coeffs):
    return pl.pallas_call(
        picks_kernel,
        out_shape=[jax.ShapeDtypeStruct((KD, V), BF16)] * 2
        + [jax.ShapeDtypeStruct((16, KD), BF16), jax.ShapeDtypeStruct((NBLK, V), BF16)],
        in_specs=[pl.BlockSpec(memory_space=pltpu.SMEM)] + vmem(2), out_specs=vmem(4),
        scratch_shapes=[pltpu.VMEM((NBLK, V), F32)],
        compiler_params=params(8), cost_estimate=cost(1_500_000_000), name="picks",
    )(excitations, excitations, coeffs)


def spread(excitations, coeffs):
    return pl.pallas_call(
        spread_kernel,
        out_shape=[jax.ShapeDtypeStruct((JP, NBLK * STATES, 2 * V), BF16)] * 2,
        in_specs=vmem(2), out_specs=vmem(2),
        compiler_params=params(8), cost_estimate=cost(1_500_000_000), name="spread",
    )(excitations, coeffs)


def partial_values(excitations, me, tables, spreads, picked):
    return pl.pallas_call(
        value_kernel,
        out_shape=[jax.ShapeDtypeStruct((8, GROUP), F32), jax.ShapeDtypeStruct((JP, GROUP, 2 * V), BF16),
                   jax.ShapeDtypeStruct((KD, 2 * GROUP), BF16), jax.ShapeDtypeStruct((NBLK * 8, GROUP), F32)],
        in_specs=[pl.BlockSpec(memory_space=pltpu.SMEM)] * 2 + vmem(NDET + 6), out_specs=vmem(4),
        scratch_shapes=[pltpu.VMEM((NBLK * JPAD, GROUP), F32), pltpu.VMEM((NBLK * STATES, GROUP), F32),
                        pltpu.VMEM((16, 2 * GROUP), F32)],
        compiler_params=params(22), name="partial_values",
    )(excitations, me, *tables, *spreads, *picked)


def gradient(me, parts, local_energy, excitations, tab, pair_products, tia):
    return pl.pallas_call(
        grad_kernel,
        out_shape=[jax.ShapeDtypeStruct((STATES, OWN), F32), jax.ShapeDtypeStruct((NWALK, 8, 384), F32)],
        in_specs=[pl.BlockSpec(memory_space=pltpu.SMEM)] + vmem(9), out_specs=vmem(2),
        scratch_shapes=[pltpu.VMEM((NBLK, JP * 16, 2 * V), BF16), pltpu.VMEM((4, 8, GROUP), F32)],
        compiler_params=params(20), name="gradient",
    )(me, *parts, local_energy, excitations, tab, pair_products, tia)


def finish(messages):
    return pl.pallas_call(
        final_kernel,
        out_shape=[jax.ShapeDtypeStruct((STATES, 1, 256), F32), jax.ShapeDtypeStruct((1, STATES), F32)],
        in_specs=vmem(1), out_specs=vmem(2),
        compiler_params=params(8), name="finish",
    )(messages)


def across(x, step):
    return lax.ppermute(x, "det", [(i, (i + 2 * step(i % 2)) % NDET) for i in range(NDET)])


def other_core(x):
    return lax.ppermute(x, "det", [(i, i ^ 1) for i in range(NDET)])


def gather_tables(table):
    ahead = across(table, lambda c: 1 - 2 * c)
    behind = across(table, lambda c: 2 * c - 1)
    beyond = across(ahead, lambda c: 1 - 2 * c)
    mine = [table, ahead, behind, beyond]
    return mine + [other_core(t) for t in mine]


def shards(positions, inverse, centers, exponent, orbital_weights, excitations, state_coeffs, local_energy):
    me = jnp.stack([lax.axis_index("walk"), lax.axis_index("det")])
    tables = gather_tables(make_table(positions, inverse, centers, exponent, orbital_weights))
    spreads = spread(excitations, state_coeffs)
    picked = picks(excitations, state_coeffs)
    part, tab, products, tia = partial_values(excitations, me, tables, spreads, picked)
    chip = part + other_core(part)
    parts = [chip] + [across(chip, lambda c, d=d: d) for d in (1, 2, 3)]
    own, messages = gradient(me, parts, local_energy, excitations, tab, products, tia)
    grad, energy = finish(lax.all_to_all(messages, "walk", 0, 0, tiled=True))
    return grad, own, energy.reshape(STATES)


def solution(mesh):
    in_specs = (
        P(None, ("walk", "det"), None),
        P(("walk", "det"), None, None),
        P(),
        P(),
        P(),
        P(None, "det"),
        P(None, "det"),
        P(None, "walk"),
    )
    out_specs = (P(None, "det", "walk"), P(None, ("walk", "det")), P())
    return jax.shard_map(shards, mesh=mesh, in_specs=in_specs, out_specs=out_specs, check_vma=False)
```

time: 192 us -> 114 us (0.59)
  starting transfers between devices: 113 us -> 9.83 us
  blocking collectives: 0 us -> 24.8 us
  Pallas kernels: 48.1 us -> 63.3 us
  waiting for transfers between devices: 19.9 us -> 9.55 us
  local copies, waits for them, and re-layouts: 8.94 us -> 5.92 us
    ppermute x45 -> x11, starting transfers between devices: 113 us -> 9.83 us  [the longest x6 8.55 us: across(): lax.ppermute(x, 'det', [(i, (i + 2 * step(i % 2)) % NDET) for i in range(...]
    all_to_all x0 -> x1, blocking collectives: none -> 24.8 us  [shards(): grad, energy = finish(lax.all_to_all(messages, 'walk', 0, 0, tiled=True))]
    pallas_call x3 -> x4, Pallas kernels: 25.8 us -> 38 us  [the longest x1 17.3 us: gradient(): pl.pallas_call(grad_kernel, out_shape=[jax.ShapeDtypeStruct((STATES, OWN)...]
    ppermute x45 -> x11, waiting for transfers between devices: 19.9 us -> 9.55 us  [the longest x6 8.48 us: across(): lax.ppermute(x, 'det', [(i, (i + 2 * step(i % 2)) % NDET) for i in range(...]
    pallas_call x1, Pallas kernels: 20 us -> 22.1 us  [partial_values(): pl.pallas_call(value_kernel, out_shape=[jax.ShapeDtypeStruct((8, GROUP),...]
    unnamed x18 -> x20, local copies, waits for them, and re-layouts: 6.62 us -> 5.92 us
  transfers between devices with their start and end apart: 45 -> 11, of which waited for: 6 -> 4; matrix products, arithmetic and copies ran while one was open for 1% -> 0% of each run, Pallas kernels for 4% -> 17%
where the time goes in v2:
time: 114 us
  Pallas kernels  63.3 us (56%)
  blocking collectives  24.8 us (22%)
  starting transfers between devices  9.83 us (9%)
  waiting for transfers between devices  9.55 us (8%)
  local copies, waits for them, and re-layouts  5.92 us (5%)
    all_to_all x1, blocking collectives, shards(): grad, energy = finish(lax.all_to_all(messages, 'walk', 0, 0, tiled=True))  24.8 us
    pallas_call x1, Pallas kernels, partial_values(): pl.pallas_call(value_kernel, out_shape=[jax.ShapeDtypeStruct((8, GROUP),...  22.1 us
    pallas_call x1, Pallas kernels, gradient(): pl.pallas_call(grad_kernel, out_shape=[jax.ShapeDtypeStruct((STATES, OWN)...  17.3 us
    pallas_call x1, Pallas kernels, picks(): pl.pallas_call(picks_kernel, out_shape=[jax.ShapeDtypeStruct((KD, V), BF1...  13.2 us
    ppermute x6, starting transfers between devices, across(): lax.ppermute(x, 'det', [(i, (i + 2 * step(i % 2)) % NDET) for i in range(...  8.55 us
    ppermute x6, waiting for transfers between devices, across(): lax.ppermute(x, 'det', [(i, (i + 2 * step(i % 2)) % NDET) for i in range(...  8.48 us
    pallas_call x1, Pallas kernels, spread(): pl.pallas_call(spread_kernel, out_shape=[jax.ShapeDtypeStruct((JP, NBLK *...  6.73 us
    unnamed x20, local copies, waits for them, and re-layouts  5.92 us
  transfers between devices with their start and end apart: 11, of which 4 were waited for; matrix products, arithmetic and copies ran while one was open for 0% of the time, Pallas kernels for 17%

profile of v2, /device:TPU:32, one launch (start us, length us, event | category | flops | bytes accessed | tf_op | source)
XLA Modules:
  0.0 114.1 jit_solution(10815014927826629605)
XLA Ops:
  0.6 0.0 copy-start.1
  0.7 1.0 copy-done.2
  1.7 0.9 copy-done.3
  2.6 0.7 copy-done.4
  3.4 0.7 copy-done.5
  4.1 0.7 copy-done.6
  4.8 3.2 %tables.1.t0 = bf16[25,16,256]{2,1,0:T(8,128)(2,1)S(1)} custom-call(f32[3,16,50]{2,1,0:T(8,128)S(1)} %copy-done.4, f32[50,16,50]{2,1,0:T(8,128)S(1)} %bitcast.5, f32[3,512]{1,0:T(4,128)S(1)} %copy-done.5, f32[1,512]{1,0:T(1,128)S(1)} %bitcast.6, f32[512,128]{1,0:T(8,128)S(1)} %copy-done.3), custom_call_target="tpu_custom_call" | custom-call | tf_op jit(solution)/shard_map/tables/pallas_call | solution.py:275
  8.0 1.6 %collective-permute-start = (bf16[25,16,256]{2,1,0:T(8,128)(2,1)S(1)}, bf16[25,16,256]{2,1,0:T(8,128)(2,1)S(1)}, u32[]{:S(2)}, u32[]{:S(2)}) collective-permute-start(bf16[25,16,256]{2,1,0:T(8,128)(2,1)S(1)} %tables.1.t0), channel_id=1, source_target_pairs={{0,2},{1,7},{2,4},{3,1},{4,6},{5,3},{6,0},{7,5},{8,10},{9,15},{10,... | collective-permute-start | bytes 614408 | tf_op jit(solution)/shard_map/ppermute | solution.py:343
  9.5 1.7 %collective-permute-start.1 = (bf16[25,16,256]{2,1,0:T(8,128)(2,1)S(1)}, bf16[25,16,256]{2,1,0:T(8,128)(2,1)S(1)}, u32[]{:S(2)}, u32[]{:S(2)}) collective-permute-start(bf16[25,16,256]{2,1,0:T(8,128)(2,1)S(1)} %tables.1.t0), channel_id=1, source_target_pairs={{0,6},{1,3},{2,0},{3,5},{4,2},{5,7},{6,4},{7,1},{8,14},{9,11},{10,... | collective-permute-start | bytes 614408 | tf_op jit(solution)/shard_map/ppermute | solution.py:343
  11.3 4.5 %collective-permute-done.t1 = bf16[25,16,256]{2,1,0:T(8,128)(2,1)S(1)} collective-permute-done((bf16[25,16,256]{2,1,0:T(8,128)(2,1)S(1)}, bf16[25,16,256]{2,1,0:T(8,128)(2,1)S(1)}, u32[]{:S(2)}, u32[]{:S(2)}) %collective-permute-start) | collective-permute-done | bytes 204832 | tf_op jit(solution)/shard_map/ppermute | solution.py:343
  15.8 1.5 %collective-permute-start.2 = (bf16[25,16,256]{2,1,0:T(8,128)(2,1)S(1)}, bf16[25,16,256]{2,1,0:T(8,128)(2,1)S(1)}, u32[]{:S(2)}, u32[]{:S(2)}) collective-permute-start(bf16[25,16,256]{2,1,0:T(8,128)(2,1)S(1)} %collective-permute-done.t1), channel_id=1, source_target_pairs={{0,2},{1,7},{2,4},{3,1},{4,6},{5,3},{6,0},{7,5},{8,10},{9,15},{10,... | collective-permute-start | bytes 614408 | tf_op jit(solution)/shard_map/ppermute | solution.py:343
  17.4 0.9 copy-done
  18.3 0.9 copy-done.8
  19.2 13.2 %picks.1 = (bf16[8192,128]{1,0:T(8,128)(2,1)S(1)}, bf16[8192,128]{1,0:T(8,128)(2,1)S(1)}, bf16[16,8192]{1,0:T(8,128)(2,1)S(1)}, bf16[64,128]{1,0:T(8,128)(2,1)S(1)}) custom-call(s32[4,8192]{1,0:T(4,128)S(1)} %copy-done, s32[4,8192]{1,0:T(4,128)S(1)} %copy-done, f32[4,8192]{1,0:T(4,128)S(1)} %copy-done.8), custom_call_target="tpu_custom_call" | custom-call | flops 1500000000 | bytes 8388608 | tf_op jit(solution)/shard_map/picks/pallas_call | solution.py:292
  32.4 0.6 collective-permute-start.4
  33.0 0.1 collective-permute-start.5
  33.1 0.0 collective-permute-done.2.t3
  33.1 0.4 collective-permute-start.6
  33.5 0.1 pad_add_fusion.me_ref
  33.5 6.7 %spread.1 = (bf16[25,256,256]{2,1,0:T(8,128)(2,1)S(1)}, bf16[25,256,256]{2,1,0:T(8,128)(2,1)S(1)}) custom-call(s32[4,8192]{1,0:T(4,128)S(1)} %copy-done.1, f32[4,8192]{1,0:T(4,128)S(1)} %copy-done.9), custom_call_target="tpu_custom_call" | custom-call | flops 1500000000 | bytes 8388608 | tf_op jit(solution)/shard_map/spread/pallas_call | solution.py:303
  40.3 0.0 copy-start.7
  40.3 22.1 %partial_values.1 = (f32[8,128]{1,0:T(8,128)S(1)}, bf16[25,128,256]{2,1,0:T(8,128)(2,1)S(1)}, bf16[8192,256]{1,0:T(8,128)(2,1)S(1)}, f32[512,128]{1,0:T(8,128)S(1)}) custom-call(s32[4,8192]{1,0:T(4,128)S(1)} %copy-done.1, s32[2]{0:T(128)S(1)} %pad_add_fusion.me_ref, bf16[25,16,256]{2,1,0:T(8,128)(2,1)S(1)} %tables.1.t0, ...), custom_call_target="tpu_custom_call" | custom-call | tf_op jit(solution)/shard_map/partial_values/pallas_call | solution.py:312
  62.4 0.2 collective-permute-start.7
  62.6 1.1 collective-permute-done.7
  63.6 1.7 %collective-permute-start.10 = (f32[8,128]{1,0:T(8,128)S(1)}, f32[8,128]{1,0:T(8,128)S(1)}, u32[]{:S(2)}, u32[]{:S(2)}) collective-permute-start(f32[8,128]{1,0:T(8,128)S(1)} %add.3.p0), channel_id=1, source_target_pairs={{0,6},{1,7},{2,0},{3,1},{4,2},{5,3},{6,4},{7,5},{8,14},{9,15},{10,... | collective-permute-start | bytes 12296 | tf_op jit(solution)/shard_map/ppermute | solution.py:343
  65.3 1.1 collective-permute-start.9
  66.4 0.9 collective-permute-start.8
  67.3 3.1 %collective-permute-done.9.p2 = f32[8,128]{1,0:T(8,128)S(1)} collective-permute-done((f32[8,128]{1,0:T(8,128)S(1)}, f32[8,128]{1,0:T(8,128)S(1)}, u32[]{:S(2)}, u32[]{:S(2)}) %collective-permute-start.9) | collective-permute-done | bytes 4128 | tf_op jit(solution)/shard_map/ppermute | solution.py:343
  70.4 0.8 collective-permute-done.8.p1
  71.3 17.3 %gradient.1 = (f32[4,16]{1,0:T(4,128)}, f32[32,8,384]{2,1,0:T(8,128)S(1)}) custom-call(s32[2]{0:T(128)S(1)} %pad_add_fusion.me_ref, f32[8,128]{1,0:T(8,128)S(1)} %add.3.p0, f32[8,128]{1,0:T(8,128)S(1)} %collective-permute-done.8.p1, f32[8,128]{1,0:T(8,128)S(1)} %collective-permute-done.9.p2, f32[8,128]{1,0:T(8,128)S(1)} %collective-permute-done.10.p3, ...), custom_call_target="tpu_custom_call" | custom-call | tf_op jit(solution)/shard_map/gradient/pallas_call | solution.py:324
  88.5 24.8 %all_to_all.5.in_ref = f32[32,8,384]{2,1,0:T(8,128)S(1)} all-to-all(f32[32,8,384]{2,1,0:T(8,128)S(1)} %get-tuple-element.27), channel_id=1, replica_groups=mesh['walk'=32,'det'=8] {'walk'}, dimensions={0} | all-to-all | bytes 786432 | tf_op jit(solution)/shard_map/all_to_all | solution.py:367
  113.3 0.8 finish.1
  (19 shorter events, 0.0 us)
Async XLA Ops:
  0.6 32.9 %copy-start.1 = (s32[4,8192]{1,0:T(4,128)S(1)}, s32[4,8192]{1,0:T(4,128)}, u32[]{:S(2)}) copy-start(s32[4,8192]{1,0:T(4,128)} %exc_ref.5) | copy-start | bytes 393220
  0.6 1.0 copy-start.2
  1.7 0.9 copy-start.3
  2.6 0.7 copy-start.4
  3.4 0.7 copy-start.5
  4.1 0.7 copy-start.6
  4.7 28.8 %copy-start.9 = (f32[4,8192]{1,0:T(4,128)S(1)}, f32[4,8192]{1,0:T(4,128)}, u32[]{:S(2)}) copy-start(f32[4,8192]{1,0:T(4,128)} %coef_ref.3) | copy-start | bytes 393220
  8.0 7.9 %collective-permute-start = (bf16[25,16,256]{2,1,0:T(8,128)(2,1)S(1)}, bf16[25,16,256]{2,1,0:T(8,128)(2,1)S(1)}, u32[]{:S(2)}, u32[]{:S(2)}) collective-permute-start(bf16[25,16,256]{2,1,0:T(8,128)(2,1)S(1)} %tables.1.t0), channel_id=1, source_target_pairs={{0,2},{1,7},{2,4},{3,1},{4,6},{5,3},{6,0},{7,5},{8,10},{9,15},{10,... | collective-permute-start | bytes 614408 | tf_op jit(solution)/shard_map/ppermute | solution.py:343
  9.5 23.4 %collective-permute-start.1 = (bf16[25,16,256]{2,1,0:T(8,128)(2,1)S(1)}, bf16[25,16,256]{2,1,0:T(8,128)(2,1)S(1)}, u32[]{:S(2)}, u32[]{:S(2)}) collective-permute-start(bf16[25,16,256]{2,1,0:T(8,128)(2,1)S(1)} %tables.1.t0), channel_id=1, source_target_pairs={{0,6},{1,3},{2,0},{3,5},{4,2},{5,7},{6,4},{7,1},{8,14},{9,11},{10,... | collective-permute-start | bytes 614408 | tf_op jit(solution)/shard_map/ppermute | solution.py:343
  15.8 17.2 %collective-permute-start.2 = (bf16[25,16,256]{2,1,0:T(8,128)(2,1)S(1)}, bf16[25,16,256]{2,1,0:T(8,128)(2,1)S(1)}, u32[]{:S(2)}, u32[]{:S(2)}) collective-permute-start(bf16[25,16,256]{2,1,0:T(8,128)(2,1)S(1)} %collective-permute-done.t1), channel_id=1, source_target_pairs={{0,2},{1,7},{2,4},{3,1},{4,6},{5,3},{6,0},{7,5},{8,10},{9,15},{10,... | collective-permute-start | bytes 614408 | tf_op jit(solution)/shard_map/ppermute | solution.py:343
  17.4 22.9 %collective-permute-start.3 = (bf16[25,16,256]{2,1,0:T(8,128)(2,1)S(1)}, bf16[25,16,256]{2,1,0:T(8,128)(2,1)S(1)}, u32[]{:S(2)}, u32[]{:S(2)}) collective-permute-start(bf16[25,16,256]{2,1,0:T(8,128)(2,1)S(1)} %tables.1.t0), channel_id=1, source_target_pairs={{0,1},{1,0},{2,3},{3,2},{4,5},{5,4},{6,7},{7,6},{8,9},{9,8},{10,11... | collective-permute-start | bytes 614408 | tf_op jit(solution)/shard_map/ppermute | solution.py:347
  17.4 0.9 copy-start
  18.3 0.9 copy-start.8
  32.4 8.0 %collective-permute-start.4 = (bf16[25,16,256]{2,1,0:T(8,128)(2,1)S(1)}, bf16[25,16,256]{2,1,0:T(8,128)(2,1)S(1)}, u32[]{:S(2)}, u32[]{:S(2)}) collective-permute-start(bf16[25,16,256]{2,1,0:T(8,128)(2,1)S(1)} %collective-permute-done.t1), channel_id=1, source_target_pairs={{0,1},{1,0},{2,3},{3,2},{4,5},{5,4},{6,7},{7,6},{8,9},{9,8},{10,11... | collective-permute-start | bytes 614408 | tf_op jit(solution)/shard_map/ppermute | solution.py:347
  33.0 7.3 %collective-permute-start.5 = (bf16[25,16,256]{2,1,0:T(8,128)(2,1)S(1)}, bf16[25,16,256]{2,1,0:T(8,128)(2,1)S(1)}, u32[]{:S(2)}, u32[]{:S(2)}) collective-permute-start(bf16[25,16,256]{2,1,0:T(8,128)(2,1)S(1)} %collective-permute-done.1.t2), channel_id=1, source_target_pairs={{0,1},{1,0},{2,3},{3,2},{4,5},{5,4},{6,7},{7,6},{8,9},{9,8},{10,11... | collective-permute-start | bytes 614408 | tf_op jit(solution)/shard_map/ppermute | solution.py:347
  33.1 7.3 %collective-permute-start.6 = (bf16[25,16,256]{2,1,0:T(8,128)(2,1)S(1)}, bf16[25,16,256]{2,1,0:T(8,128)(2,1)S(1)}, u32[]{:S(2)}, u32[]{:S(2)}) collective-permute-start(bf16[25,16,256]{2,1,0:T(8,128)(2,1)S(1)} %collective-permute-done.2.t3), channel_id=1, source_target_pairs={{0,1},{1,0},{2,3},{3,2},{4,5},{5,4},{6,7},{7,6},{8,9},{9,8},{10,11... | collective-permute-start | bytes 614408 | tf_op jit(solution)/shard_map/ppermute | solution.py:347
  40.3 30.9 %copy-start.7 = (f32[4,128]{1,0:T(4,128)S(1)}, f32[4,128]{1,0:T(4,128)}, u32[]{:S(2)}) copy-start(f32[4,128]{1,0:T(4,128)} %energy_ref.1) | copy-start | bytes 6148
  62.4 1.2 %collective-permute-start.7 = (f32[8,128]{1,0:T(8,128)S(1)}, f32[8,128]{1,0:T(8,128)S(1)}, u32[]{:S(2)}, u32[]{:S(2)}) collective-permute-start(f32[8,128]{1,0:T(8,128)S(1)} %get-tuple-element.23), channel_id=1, source_target_pairs={{0,1},{1,0},{2,3},{3,2},{4,5},{5,4},{6,7},{7,6},{8,9},{9,8},{10,11... | collective-permute-start | bytes 12296 | tf_op jit(solution)/shard_map/ppermute | solution.py:347
  63.6 3.7 %collective-permute-start.10 = (f32[8,128]{1,0:T(8,128)S(1)}, f32[8,128]{1,0:T(8,128)S(1)}, u32[]{:S(2)}, u32[]{:S(2)}) collective-permute-start(f32[8,128]{1,0:T(8,128)S(1)} %add.3.p0), channel_id=1, source_target_pairs={{0,6},{1,7},{2,0},{3,1},{4,2},{5,3},{6,4},{7,5},{8,14},{9,15},{10,... | collective-permute-start | bytes 12296 | tf_op jit(solution)/shard_map/ppermute | solution.py:343
  65.3 5.1 %collective-permute-start.9 = (f32[8,128]{1,0:T(8,128)S(1)}, f32[8,128]{1,0:T(8,128)S(1)}, u32[]{:S(2)}, u32[]{:S(2)}) collective-permute-start(f32[8,128]{1,0:T(8,128)S(1)} %add.3.p0), channel_id=1, source_target_pairs={{0,4},{1,5},{2,6},{3,7},{4,0},{5,1},{6,2},{7,3},{8,12},{9,13},{10,... | collective-permute-start | bytes 12296 | tf_op jit(solution)/shard_map/ppermute | solution.py:343
  66.4 4.8 %collective-permute-start.8 = (f32[8,128]{1,0:T(8,128)S(1)}, f32[8,128]{1,0:T(8,128)S(1)}, u32[]{:S(2)}, u32[]{:S(2)}) collective-permute-start(f32[8,128]{1,0:T(8,128)S(1)} %add.3.p0), channel_id=1, source_target_pairs={{0,2},{1,3},{2,4},{3,5},{4,6},{5,7},{6,0},{7,1},{8,10},{9,11},{10,... | collective-permute-start | bytes 12296 | tf_op jit(solution)/shard_map/ppermute | solution.py:343

commit v3 on v2

--- a/solution.py
+++ b/solution.py
@@ -21,10 +21,12 @@
 NWALK = 32
 JPAD = 64
 MIB = 1024 * 1024
+UNROLL = 8
 
 F32, BF16 = jnp.float32, jnp.bfloat16
 NN = (((1,), (0,)), ((), ()))
 NT = (((1,), (1,)), ((), ()))
+TN = (((0,), (0,)), ((), ()))
 
 
 def dot(a, b, dims=NN):
@@ -76,35 +78,10 @@
         table = dot(i_hi, v_hi) + (dot(i_hi, v_lo) + dot(i_lo, v_hi))
         tab_s[pl.ds(w, ROWS, stride=OWN), :] = table[0:ROWS]
     for i in range(NEL):
-        out_ref[i // 2, :, (i % 2) * V:(i % 2 + 1) * V] = tab_s[i * OWN:(i + 1) * OWN, :].astype(BF16)
-
-
-def picks_kernel(exc_smem, exc_ref, coef_ref, obt_ref, ojt_ref, c16_ref, oa_ref, oa_s):
-    lane = lax.broadcasted_iota(jnp.int32, (1, V), 1)
-
-    def one_row(blk, _):
-        oa_s[pl.ds(blk, 1), :] = jnp.where(lane == exc_smem[1, blk * BLOCK], 1.0, 0.0).astype(F32)
-        return _
-
-    lax.fori_loop(0, NBLK, one_row, 0)
-    oa_ref[...] = oa_s[...].astype(BF16)
-    lane_b = lax.broadcasted_iota(jnp.int32, (2 * BLOCK, V), 1)
-
-    def pair(p, _):
-        where = pl.ds(pl.multiple_of(p * 2 * BLOCK, 2 * BLOCK), 2 * BLOCK)
-        c4 = coef_ref[:, where]
-        c_hi, c_lo = split(jnp.concatenate([c4, c4], axis=0))
-        c16_ref[:, where] = jnp.concatenate([c_hi.astype(F32), c_lo.astype(F32)], axis=0).astype(BF16)
-        both = exc_ref[2:4, where]
-        idx = jnp.concatenate([both, both, both, both], axis=0).astype(F32).T
-        obt_ref[where, :] = jnp.where(idx[:, 1:2].astype(jnp.int32) == lane_b, 1.0, 0.0).astype(BF16)
-        ojt_ref[where, :] = jnp.where(idx[:, 0:1].astype(jnp.int32) == lane_b, 1.0, 0.0).astype(BF16)
-        return _
-
-    lax.fori_loop(0, PAIRS, pair, 0)
-
-
-def spread_kernel(exc_ref, coef_ref, chi_ref, clo_ref):
+        out_ref[:, i * V:(i + 1) * V] = tab_s[i * OWN:(i + 1) * OWN, :].astype(BF16)
+
+
+def spread_kernel(exc_ref, coef_ref, spread_ref):
     sub_b = lax.broadcasted_iota(jnp.int32, (V, 2 * BLOCK), 0)
     half = lax.broadcasted_iota(jnp.int32, (8, 2 * BLOCK), 1) // BLOCK
     upper = lax.broadcasted_iota(jnp.int32, (8, 2 * BLOCK), 0) // STATES
@@ -126,72 +103,75 @@
                 w_hi.append(jnp.concatenate([jnp.where(m0, q_hi, 0.0), jnp.where(m1, q_hi, 0.0)], axis=0).astype(BF16))
                 w_lo.append(jnp.concatenate([jnp.where(m0, q_lo, 0.0), jnp.where(m1, q_lo, 0.0)], axis=0).astype(BF16))
             parts.append(dot(jnp.concatenate(w_hi, axis=0), pick_b, NT) + dot(jnp.concatenate(w_lo, axis=0), pick_b, NT))
-        rows = pl.ds(pl.multiple_of(q * 16, 16), 16)
+        high = pl.ds(pl.multiple_of(q * 16, 16), 16)
+        low = pl.ds(pl.multiple_of(NBLK * STATES + q * 16, 16), 16)
         for j in range(NEL):
             both = jnp.concatenate([parts[0][j * 8:(j + 1) * 8], parts[1][j * 8:(j + 1) * 8]], axis=0)
             hi, lo = split(both)
-            lanes = slice((j % 2) * V, (j % 2 + 1) * V)
-            chi_ref[j // 2, rows, lanes] = hi
-            clo_ref[j // 2, rows, lanes] = lo
+            spread_ref[high, j * V:(j + 1) * V] = hi
+            spread_ref[low, j * V:(j + 1) * V] = lo
         return _
 
     lax.fori_loop(0, PAIRS // 2, quad, 0)
 
 
-def value_kernel(exc_smem, me_ref, t0, t1, t2, t3, t4, t5, t6, t7, chi_ref, clo_ref, obt_ref, ojt_ref, c16_ref, oa_ref,
-                 part_ref, tab_ref, p_ref, tia_ref, v_s, x_s, acc_s):
+def value_kernel(par_ref, me_ref, t0, t1, t2, t3, t4, t5, t6, t7, spread_ref, exc_ref, coef_ref,
+                 part_ref, tab_ref, p_ref, tia_ref, v_s, x_s, oa_s, acc_s):
     x, c = lax.shift_right_logical(me_ref[1], 1), jnp.bitwise_and(me_ref[1], 1)
     ahead = 1 - 2 * c
     sources = ((x, c), (x - ahead, c), (x + ahead, c), (x + 2, c),
                (x, 1 - c), (x + ahead, 1 - c), (x - ahead, 1 - c), (x + 2, 1 - c))
     for t_ref, (xx, cc) in zip((t0, t1, t2, t3, t4, t5, t6, t7), sources):
         source = 2 * jnp.bitwise_and(xx + 4, 3) + cc
-        tab_ref[:, pl.ds(pl.multiple_of(source * OWN, OWN), OWN), :] = t_ref[...]
+        tab_ref[pl.ds(pl.multiple_of(source * OWN, OWN), OWN), :] = t_ref[...]
     for j in range(NEL, JPAD):
         v_s[pl.ds(j, NBLK, stride=JPAD), :] = jnp.zeros((NBLK, GROUP), F32)
-    x_s[...] = jnp.zeros_like(x_s)
-    pick_a = oa_ref[...]
-
-    def over_rows(jp, _):
-        t = tab_ref[jp]
-        x_s[...] += dot(chi_ref[jp], t, NT) + dot(clo_ref[jp], t, NT)
-        for j2 in range(2):
-            v_s[pl.ds(2 * jp + j2, NBLK, stride=JPAD), :] = dot(pick_a, t[:, j2 * V:(j2 + 1) * V], NT)
-        return _
-
-    lax.fori_loop(0, JP, over_rows, 0)
+    lane = lax.broadcasted_iota(jnp.int32, (1, V), 1)
+    for blk in range(NBLK):
+        oa_s[blk:blk + 1, :] = jnp.where(lane == par_ref[1, blk], 1.0, 0.0).astype(F32)
+    pick_a = oa_s[...].astype(BF16)
+    x = dot(spread_ref[...], tab_ref[...], NT)
+    x_s[...] = x[0:NBLK * STATES] + x[NBLK * STATES:]
+    for j in range(NEL):
+        v_s[pl.ds(j, NBLK, stride=JPAD), :] = dot(pick_a, tab_ref[:, j * V:(j + 1) * V], NT)
 
     def own_entry(blk, _):
-        row = v_s[pl.ds(blk * JPAD + exc_smem[0, blk * BLOCK], 1), :]
+        row = v_s[pl.ds(blk * JPAD + par_ref[0, blk], 1), :]
         tia_ref[pl.ds(pl.multiple_of(blk * 8, 8), 8), :] = jnp.broadcast_to(row, (8, GROUP))
         return _
 
-    lax.fori_loop(0, NBLK, own_entry, 0)
+    lax.fori_loop(0, NBLK, own_entry, 0, unroll=8)
     acc_s[...] = jnp.zeros_like(acc_s)
     low = lax.broadcasted_iota(jnp.int32, (8, GROUP), 0) < STATES
+    sub_b = lax.broadcasted_iota(jnp.int32, (V, BLOCK), 0)
+    sub_j = lax.broadcasted_iota(jnp.int32, (JPAD, BLOCK), 0)
 
     def pair(p, first):
+        products = []
         for h in range(2):
             blk = 2 * p + h
             dets = pl.ds(pl.multiple_of(blk * BLOCK, BLOCK), BLOCK)
-            i = exc_smem[0, blk * BLOCK]
-            t_i = tab_ref[lax.shift_right_logical(i, 1), :, pl.ds(pl.multiple_of(jnp.bitwise_and(i, 1) * V, V), V)]
-            along = dot(obt_ref[dets, :], t_i, NT)
+            pick_j = jnp.where(sub_j == exc_ref[2:3, dets], 1.0, 0.0).astype(BF16)
+            pick_b = jnp.where(sub_b == exc_ref[3:4, dets], 1.0, 0.0).astype(BF16)
+            t_i = tab_ref[:, pl.ds(pl.multiple_of(par_ref[0, blk] * V, V), V)]
+            along = dot(t_i, pick_b)
             column = v_s[pl.ds(pl.multiple_of(blk * JPAD, JPAD), JPAD), :].astype(BF16)
-            down = dot(ojt_ref[dets, 0:JPAD], column)
-            hi, lo = split(along * down)
-            p_ref[dets, 0:GROUP] = hi
-            p_ref[dets, GROUP:2 * GROUP] = lo
-        both = pl.ds(pl.multiple_of(p * 2 * BLOCK, 2 * BLOCK), 2 * BLOCK)
-        acc_s[...] += dot(c16_ref[:, both], p_ref[both, :])
+            down = dot(column, pick_j, TN)
+            product = along * down
+            hi, lo = split(product)
+            p_ref[0:GROUP, dets] = hi
+            p_ref[GROUP:2 * GROUP, dets] = lo
+            products.append((product, dets))
+        for s in range(STATES):
+            acc_s[s] += products[0][0] * coef_ref[s:s + 1, products[0][1]] + products[1][0] * coef_ref[s:s + 1, products[1][1]]
         tia = jnp.where(low, tia_ref[pl.ds(pl.multiple_of(p * 16, 16), 8), :],
                         tia_ref[pl.ds(pl.multiple_of(p * 16 + 8, 8), 8), :])
         return first + x_s[pl.ds(pl.multiple_of(p * 8, 8), 8), :] * tia
 
-    first = lax.fori_loop(0, PAIRS, pair, jnp.zeros((8, GROUP), F32))
+    first = lax.fori_loop(0, PAIRS, pair, jnp.zeros((8, GROUP), F32), unroll=UNROLL)
     first = first + jnp.concatenate([first[STATES:], first[:STATES]], axis=0)
-    second = acc_s[0:8, :] + acc_s[8:16, :]
-    part_ref[...] = first - (second[:, 0:GROUP] + second[:, GROUP:2 * GROUP])
+    second = jnp.concatenate([jnp.sum(acc_s[s].T, axis=0, keepdims=True) for s in range(STATES)] * 2, axis=0)
+    part_ref[...] = first - second
 
 
 def grad_kernel(me_ref, p0, p1, p2, p3, energy_ref, exc_ref, tab_ref, p_ref, tia_ref, own_ref, out_ref, g_s, order_s):
@@ -221,21 +201,17 @@
     l_hi, l_lo = split(lhs.reshape(NBLK * 8, GROUP))
     lhs = jnp.concatenate([l_hi, l_lo], axis=1)
 
-    def over_rows(jp, _):
-        t = tab_ref[jp]
+    for jp in range(JP):
+        t = tab_ref[:, jp * 2 * V:(jp + 1) * 2 * V]
         g = dot(lhs, jnp.concatenate([t, t], axis=0)).reshape(NBLK, 8, 2 * V)
         hi, lo = split(jnp.concatenate([g[:, :, 0:V], g[:, :, V:2 * V]], axis=1))
-        rows = pl.ds(pl.multiple_of(jp * 16, 16), 16)
-        g_s[:, rows, 0:V] = hi
-        g_s[:, rows, V:2 * V] = lo
-        return _
-
-    lax.fori_loop(0, JP, over_rows, 0)
+        g_s[:, jp * 16:(jp + 1) * 16, 0:V] = hi
+        g_s[:, jp * 16:(jp + 1) * 16, V:2 * V] = lo
     sub_b = lax.broadcasted_iota(jnp.int32, (V, BLOCK), 0)
 
     def slot(p, _):
         both = pl.ds(pl.multiple_of(p * 2 * BLOCK, 2 * BLOCK), 2 * BLOCK)
-        second = dot(f16, p_ref[both, :], NT)
+        second = dot(f16, p_ref[:, both])
         second = second[0:8] + second[8:16]
         for h in range(2):
             dets = pl.ds(pl.multiple_of(p * 2 * BLOCK + h * BLOCK, BLOCK), BLOCK)
@@ -249,7 +225,7 @@
         out_ref[p, :, 2 * BLOCK:3 * BLOCK] = meta
         return _
 
-    lax.fori_loop(0, NWALK, slot, 0)
+    lax.fori_loop(0, NWALK, slot, 0, unroll=UNROLL)
 
 
 def final_kernel(in_ref, grad_ref, energy_ref):
@@ -274,13 +250,13 @@
 def make_table(positions, inverse, centers, exponent, orbital_weights):
     return pl.pallas_call(
         table_kernel,
-        out_shape=jax.ShapeDtypeStruct((JP, OWN, 2 * V), BF16),
+        out_shape=jax.ShapeDtypeStruct((OWN, NEL * V), BF16),
         in_specs=[pl.BlockSpec(memory_space=pltpu.HBM)] * 5, out_specs=vmem(1)[0],
         scratch_shapes=[pltpu.VMEM((3, OWN, NEL), F32), pltpu.VMEM((NEL, OWN, NEL), F32), pltpu.VMEM((3, NBAS), F32),
                         pltpu.VMEM((1, NBAS), F32), pltpu.VMEM((NBAS, V), F32), pltpu.VMEM((128, 128), F32), pltpu.VMEM((OWN * ROWS, NBAS), F32),
                         pltpu.VMEM((OWN, 128, V), F32), pltpu.VMEM((OWN, JPAD, 128), F32),
                         pltpu.VMEM((ROWS * OWN, V), F32), pltpu.SemaphoreType.DMA((5,))],
-        compiler_params=params(8), name="tables",
+        compiler_params=params(60), name="tables",
     )(positions, inverse.transpose(1, 0, 2), centers, exponent.reshape(1, NBAS), orbital_weights)
 
 
@@ -288,36 +264,25 @@
     return pl.CostEstimate(flops=flops, bytes_accessed=8 * MIB, transcendentals=0)
 
 
-def picks(excitations, coeffs):
-    return pl.pallas_call(
-        picks_kernel,
-        out_shape=[jax.ShapeDtypeStruct((KD, V), BF16)] * 2
-        + [jax.ShapeDtypeStruct((16, KD), BF16), jax.ShapeDtypeStruct((NBLK, V), BF16)],
-        in_specs=[pl.BlockSpec(memory_space=pltpu.SMEM)] + vmem(2), out_specs=vmem(4),
-        scratch_shapes=[pltpu.VMEM((NBLK, V), F32)],
-        compiler_params=params(8), cost_estimate=cost(1_500_000_000), name="picks",
-    )(excitations, excitations, coeffs)
-
-
 def spread(excitations, coeffs):
     return pl.pallas_call(
         spread_kernel,
-        out_shape=[jax.ShapeDtypeStruct((JP, NBLK * STATES, 2 * V), BF16)] * 2,
-        in_specs=vmem(2), out_specs=vmem(2),
+        out_shape=jax.ShapeDtypeStruct((2 * NBLK * STATES, NEL * V), BF16),
+        in_specs=vmem(2), out_specs=vmem(1)[0],
         compiler_params=params(8), cost_estimate=cost(1_500_000_000), name="spread",
     )(excitations, coeffs)
 
 
-def partial_values(excitations, me, tables, spreads, picked):
+def partial_values(parents, me, tables, spreads, excitations, coeffs):
     return pl.pallas_call(
         value_kernel,
-        out_shape=[jax.ShapeDtypeStruct((8, GROUP), F32), jax.ShapeDtypeStruct((JP, GROUP, 2 * V), BF16),
-                   jax.ShapeDtypeStruct((KD, 2 * GROUP), BF16), jax.ShapeDtypeStruct((NBLK * 8, GROUP), F32)],
-        in_specs=[pl.BlockSpec(memory_space=pltpu.SMEM)] * 2 + vmem(NDET + 6), out_specs=vmem(4),
+        out_shape=[jax.ShapeDtypeStruct((8, GROUP), F32), jax.ShapeDtypeStruct((GROUP, NEL * V), BF16),
+                   jax.ShapeDtypeStruct((2 * GROUP, KD), BF16), jax.ShapeDtypeStruct((NBLK * 8, GROUP), F32)],
+        in_specs=[pl.BlockSpec(memory_space=pltpu.SMEM)] * 2 + vmem(NDET + 3), out_specs=vmem(4),
         scratch_shapes=[pltpu.VMEM((NBLK * JPAD, GROUP), F32), pltpu.VMEM((NBLK * STATES, GROUP), F32),
-                        pltpu.VMEM((16, 2 * GROUP), F32)],
+                        pltpu.VMEM((NBLK, V), F32), pltpu.VMEM((STATES, GROUP, BLOCK), F32)],
         compiler_params=params(22), name="partial_values",
-    )(excitations, me, *tables, *spreads, *picked)
+    )(parents, me, *tables, spreads, excitations, coeffs)
 
 
 def gradient(me, parts, local_energy, excitations, tab, pair_products, tia):
@@ -357,10 +322,11 @@
 
 def shards(positions, inverse, centers, exponent, orbital_weights, excitations, state_coeffs, local_energy):
     me = jnp.stack([lax.axis_index("walk"), lax.axis_index("det")])
-    tables = gather_tables(make_table(positions, inverse, centers, exponent, orbital_weights))
+    table = make_table(positions, inverse, centers, exponent, orbital_weights)
+    tables = gather_tables(table)
     spreads = spread(excitations, state_coeffs)
-    picked = picks(excitations, state_coeffs)
-    part, tab, products, tia = partial_values(excitations, me, tables, spreads, picked)
+    parents = excitations[0:2, ::BLOCK]
+    part, tab, products, tia = partial_values(parents, me, tables, spreads, excitations, state_coeffs)
     chip = part + other_core(part)
     parts = [chip] + [across(chip, lambda c, d=d: d) for d in (1, 2, 3)]
     own, messages = gradient(me, parts, local_energy, excitations, tab, products, tia)

time: 114 us -> 80.3 us (0.70)
  Pallas kernels: 63.3 us -> 28.6 us
  waiting for transfers between devices: 9.55 us -> 13.9 us
  local copies, waits for them, and re-layouts: 5.92 us -> 2.88 us
  starting transfers between devices: 9.83 us -> 8.64 us
    pallas_call x1, Pallas kernels: 22.1 us -> 8.27 us  [partial_values(): pl.pallas_call(value_kernel, out_shape=[jax.ShapeDtypeStruct((8, GROUP),...]
    pallas_call x3 -> x2, Pallas kernels: 23.1 us -> 11.1 us  [the longest x1 6.75 us: spread(): pl.pallas_call(spread_kernel, out_shape=jax.ShapeDtypeStruct((2 * NBLK *...]
    pallas_call x1, Pallas kernels: 17.3 us -> 8.34 us  [gradient(): pl.pallas_call(grad_kernel, out_shape=[jax.ShapeDtypeStruct((STATES, OWN)...]
    ppermute x6, waiting for transfers between devices: 8.48 us -> 13.1 us  [across(): lax.ppermute(x, 'det', [(i, (i + 2 * step(i % 2)) % NDET) for i in range(...]
    unnamed x20 -> x12, local copies, waits for them, and re-layouts: 5.92 us -> 1.83 us
    ppermute x6, starting transfers between devices: 8.55 us -> 7.34 us  [across(): lax.ppermute(x, 'det', [(i, (i + 2 * step(i % 2)) % NDET) for i in range(...]
  transfers between devices with their start and end apart: 11 -> 11, of which waited for: 4 -> 6; matrix products, arithmetic and copies ran while one was open for 0% -> 1% of each run, Pallas kernels for 17% -> 8%
where the time goes in v3:
time: 80.3 us; the launch traced here: 80.1 us
  Pallas kernels  28.6 us (36%)
  blocking collectives  25.3 us (32%)
  waiting for transfers between devices  13.9 us (17%)
  starting transfers between devices  8.64 us (11%)
  local copies, waits for them, and re-layouts  2.88 us (4%)
    all_to_all x1, blocking collectives, shards(): grad, energy = finish(lax.all_to_all(messages, 'walk', 0, 0, tiled=True))  25.3 us
    ppermute x6, waiting for transfers between devices, across(): lax.ppermute(x, 'det', [(i, (i + 2 * step(i % 2)) % NDET) for i in range(...  13.1 us
    pallas_call x1, Pallas kernels, gradient(): pl.pallas_call(grad_kernel, out_shape=[jax.ShapeDtypeStruct((STATES, OWN)...  8.34 us
    pallas_call x1, Pallas kernels, partial_values(): pl.pallas_call(value_kernel, out_shape=[jax.ShapeDtypeStruct((8, GROUP),...  8.27 us
    ppermute x6, starting transfers between devices, across(): lax.ppermute(x, 'det', [(i, (i + 2 * step(i % 2)) % NDET) for i in range(...  7.34 us
    pallas_call x1, Pallas kernels, spread(): pl.pallas_call(spread_kernel, out_shape=jax.ShapeDtypeStruct((2 * NBLK *...  6.75 us
    pallas_call x1, Pallas kernels, make_table(): pl.pallas_call(table_kernel, out_shape=jax.ShapeDtypeStruct((OWN, NEL * V...  4.38 us
    unnamed x12, local copies, waits for them, and re-layouts  1.83 us
  transfers between devices with their start and end apart: 11, of which 6 were waited for; matrix products, arithmetic and copies ran while one was open for 1% of the time, Pallas kernels for 8%

profile of v3, /device:TPU:32, one launch (start us, length us, event | category | flops | bytes accessed | tf_op | source)
XLA Modules:
  0.0 80.1 jit_solution(11199445458798417946)
XLA Ops:
  0.6 0.0 copy-start.1
  0.6 0.0 copy-start.4
  0.7 4.4 %tables.1.t0 = bf16[16,6400]{1,0:T(8,128)(2,1)} custom-call(f32[3,16,50]{2,1,0:T(8,128)} %pos_hbm.1, f32[50,16,50]{2,1,0:T(8,128)} %bitcast.5, f32[3,512]{1,0:T(4,128)} %cen_hbm.1, f32[1,512]{1,0:T(1,128)} %bitcast.6, f32[512,128]{1,0:T(8,128)} %orb_hbm.1), custom_call_target="tpu_custom_call" | custom-call | tf_op jit(solution)/shard_map/tables/pallas_call | solution.py:251
  5.0 1.6 %collective-permute-start = (bf16[16,6400]{1,0:T(8,128)(2,1)}, bf16[16,6400]{1,0:T(8,128)(2,1)S(1)}, u32[]{:S(2)}, u32[]{:S(2)}) collective-permute-start(bf16[16,6400]{1,0:T(8,128)(2,1)} %tables.1.t0), channel_id=1, source_target_pairs={{0,2},{1,7},{2,4},{3,1},{4,6},{5,3},{6,0},{7,5},{8,10},{9,15},{10,... | collective-permute-start | bytes 614408 | tf_op jit(solution)/shard_map/ppermute | solution.py:308
  6.6 1.7 %collective-permute-start.1 = (bf16[16,6400]{1,0:T(8,128)(2,1)}, bf16[16,6400]{1,0:T(8,128)(2,1)S(1)}, u32[]{:S(2)}, u32[]{:S(2)}) collective-permute-start(bf16[16,6400]{1,0:T(8,128)(2,1)} %tables.1.t0), channel_id=1, source_target_pairs={{0,6},{1,3},{2,0},{3,5},{4,2},{5,7},{6,4},{7,1},{8,14},{9,11},{10,... | collective-permute-start | bytes 614408 | tf_op jit(solution)/shard_map/ppermute | solution.py:308
  8.4 4.7 %collective-permute-done.t1 = bf16[16,6400]{1,0:T(8,128)(2,1)S(1)} collective-permute-done((bf16[16,6400]{1,0:T(8,128)(2,1)}, bf16[16,6400]{1,0:T(8,128)(2,1)S(1)}, u32[]{:S(2)}, u32[]{:S(2)}) %collective-permute-start) | collective-permute-done | bytes 204832 | tf_op jit(solution)/shard_map/ppermute | solution.py:308
  13.1 1.5 %collective-permute-start.2 = (bf16[16,6400]{1,0:T(8,128)(2,1)S(1)}, bf16[16,6400]{1,0:T(8,128)(2,1)S(1)}, u32[]{:S(2)}, u32[]{:S(2)}) collective-permute-start(bf16[16,6400]{1,0:T(8,128)(2,1)S(1)} %collective-permute-done.t1), channel_id=1, source_target_pairs={{0,2},{1,7},{2,4},{3,1},{4,6},{5,3},{6,0},{7,5},{8,10},{9,15},{10,... | collective-permute-start | bytes 614408 | tf_op jit(solution)/shard_map/ppermute | solution.py:308
  14.6 0.0 collective-permute-start.3
  14.6 1.1 %slice.3.par_ref = s32[2,64]{1,0:T(2,128)S(1)} slice(s32[4,8192]{1,0:T(4,128)} %exc_ref.5), slice={[0:2:1], [0:8192:128]} | slice | bytes 1024 | tf_op jit(solution)/shard_map/slice | solution.py:328
  15.7 0.6 collective-permute-start.4
  16.3 0.1 collective-permute-start.5
  16.4 3.7 %collective-permute-done.2.t3 = bf16[16,6400]{1,0:T(8,128)(2,1)S(1)} collective-permute-done((bf16[16,6400]{1,0:T(8,128)(2,1)S(1)}, bf16[16,6400]{1,0:T(8,128)(2,1)S(1)}, u32[]{:S(2)}, u32[]{:S(2)}) %collective-permute-start.2) | collective-permute-done | bytes 204832 | tf_op jit(solution)/shard_map/ppermute | solution.py:308
  20.1 0.0 collective-permute-start.6
  20.1 0.1 pad_add_fusion.me_ref
  20.2 0.9 %copy-done = s32[4,8192]{1,0:T(4,128)S(1)} copy-done((s32[4,8192]{1,0:T(4,128)S(1)}, s32[4,8192]{1,0:T(4,128)}, u32[]{:S(2)}) %copy-start) | copy-done | bytes 131096
  21.1 0.9 %copy-done.3 = f32[4,8192]{1,0:T(4,128)S(1)} copy-done((f32[4,8192]{1,0:T(4,128)S(1)}, f32[4,8192]{1,0:T(4,128)}, u32[]{:S(2)}) %copy-start.3) | copy-done | bytes 131096
  22.0 6.7 %spread.1.spread_ref = bf16[512,6400]{1,0:T(8,128)(2,1)S(1)} custom-call(s32[4,8192]{1,0:T(4,128)S(1)} %copy-done, f32[4,8192]{1,0:T(4,128)S(1)} %copy-done.3), custom_call_target="tpu_custom_call" | custom-call | flops 1500000000 | bytes 8388608 | tf_op jit(solution)/shard_map/spread/pallas_call | solution.py:268
  28.7 0.0 copy-start.5
  28.8 0.0 collective-permute-done.4.t5
  28.8 0.0 collective-permute-done.6.t7
  28.8 8.3 %partial_values.1 = (f32[8,128]{1,0:T(8,128)S(1)}, bf16[128,6400]{1,0:T(8,128)(2,1)S(1)}, bf16[256,8192]{1,0:T(8,128)(2,1)S(1)}, f32[512,128]{1,0:T(8,128)S(1)}) custom-call(s32[2,64]{1,0:T(2,128)S(1)} %slice.3.par_ref, s32[2]{0:T(128)S(1)} %pad_add_fusion.me_ref, bf16[16,6400]{1,0:T(8,128)(2,1)S(1)} %copy-done.2, ...), custom_call_target="tpu_custom_call" | custom-call | tf_op jit(solution)/shard_map/partial_values/pallas_call | solution.py:277
  37.1 0.6 collective-permute-start.7
  37.7 0.8 %collective-permute-done.7 = f32[8,128]{1,0:T(8,128)S(1)} collective-permute-done((f32[8,128]{1,0:T(8,128)S(1)}, f32[8,128]{1,0:T(8,128)S(1)}, u32[]{:S(2)}, u32[]{:S(2)}) %collective-permute-start.7) | collective-permute-done | bytes 4128 | tf_op jit(solution)/shard_map/ppermute | solution.py:312
  38.5 1.1 %collective-permute-start.10 = (f32[8,128]{1,0:T(8,128)S(1)}, f32[8,128]{1,0:T(8,128)S(1)}, u32[]{:S(2)}, u32[]{:S(2)}) collective-permute-start(f32[8,128]{1,0:T(8,128)S(1)} %add.3.p0), channel_id=1, source_target_pairs={{0,6},{1,7},{2,0},{3,1},{4,2},{5,3},{6,4},{7,5},{8,14},{9,15},{10,... | collective-permute-start | bytes 12296 | tf_op jit(solution)/shard_map/ppermute | solution.py:308
  39.6 1.2 %collective-permute-start.9 = (f32[8,128]{1,0:T(8,128)S(1)}, f32[8,128]{1,0:T(8,128)S(1)}, u32[]{:S(2)}, u32[]{:S(2)}) collective-permute-start(f32[8,128]{1,0:T(8,128)S(1)} %add.3.p0), channel_id=1, source_target_pairs={{0,4},{1,5},{2,6},{3,7},{4,0},{5,1},{6,2},{7,3},{8,12},{9,13},{10,... | collective-permute-start | bytes 12296 | tf_op jit(solution)/shard_map/ppermute | solution.py:308
  40.8 0.2 collective-permute-start.8
  41.0 1.1 %collective-permute-done.10.p3 = f32[8,128]{1,0:T(8,128)S(1)} collective-permute-done((f32[8,128]{1,0:T(8,128)S(1)}, f32[8,128]{1,0:T(8,128)S(1)}, u32[]{:S(2)}, u32[]{:S(2)}) %collective-permute-start.10) | collective-permute-done | bytes 4128 | tf_op jit(solution)/shard_map/ppermute | solution.py:308
  42.1 2.6 %collective-permute-done.9.p2 = f32[8,128]{1,0:T(8,128)S(1)} collective-permute-done((f32[8,128]{1,0:T(8,128)S(1)}, f32[8,128]{1,0:T(8,128)S(1)}, u32[]{:S(2)}, u32[]{:S(2)}) %collective-permute-start.9) | collective-permute-done | bytes 4128 | tf_op jit(solution)/shard_map/ppermute | solution.py:308
  44.8 0.9 %collective-permute-done.8.p1 = f32[8,128]{1,0:T(8,128)S(1)} collective-permute-done((f32[8,128]{1,0:T(8,128)S(1)}, f32[8,128]{1,0:T(8,128)S(1)}, u32[]{:S(2)}, u32[]{:S(2)}) %collective-permute-start.8) | collective-permute-done | bytes 4128 | tf_op jit(solution)/shard_map/ppermute | solution.py:308
  45.7 8.3 %gradient.1 = (f32[4,16]{1,0:T(4,128)}, f32[32,8,384]{2,1,0:T(8,128)S(1)}) custom-call(s32[2]{0:T(128)S(1)} %pad_add_fusion.me_ref, f32[8,128]{1,0:T(8,128)S(1)} %add.3.p0, f32[8,128]{1,0:T(8,128)S(1)} %collective-permute-done.8.p1, f32[8,128]{1,0:T(8,128)S(1)} %collective-permute-done.9.p2, f32[8,128]{1,0:T(8,128)S(1)} %collective-permute-done.10.p3, ...), custom_call_target="tpu_custom_call" | custom-call | tf_op jit(solution)/shard_map/gradient/pallas_call | solution.py:289
  54.0 25.3 %all_to_all.5.in_ref = f32[32,8,384]{2,1,0:T(8,128)S(1)} all-to-all(f32[32,8,384]{2,1,0:T(8,128)S(1)} %get-tuple-element.15), channel_id=1, replica_groups=mesh['walk'=32,'det'=8] {'walk'}, dimensions={0} | all-to-all | bytes 786432 | tf_op jit(solution)/shard_map/all_to_all | solution.py:333
  79.3 0.8 %finish.1 = (f32[4,1,256]{2,1,0:T(1,128)}, f32[1,4]{1,0:T(1,128)}) custom-call(f32[32,8,384]{2,1,0:T(8,128)S(1)} %all_to_all.5.in_ref), custom_call_target="tpu_custom_call" | custom-call | tf_op jit(solution)/shard_map/finish/pallas_call | solution.py:299
  (11 shorter events, 0.0 us)
Async XLA Ops:
  0.6 28.1 %copy-start.1 = (s32[4,8192]{1,0:T(4,128)S(1)}, s32[4,8192]{1,0:T(4,128)}, u32[]{:S(2)}) copy-start(s32[4,8192]{1,0:T(4,128)} %exc_ref.5) | copy-start | bytes 393220
  0.6 28.1 %copy-start.4 = (f32[4,8192]{1,0:T(4,128)S(1)}, f32[4,8192]{1,0:T(4,128)}, u32[]{:S(2)}) copy-start(f32[4,8192]{1,0:T(4,128)} %coef_ref.3) | copy-start | bytes 393220
  5.0 8.1 %collective-permute-start = (bf16[16,6400]{1,0:T(8,128)(2,1)}, bf16[16,6400]{1,0:T(8,128)(2,1)S(1)}, u32[]{:S(2)}, u32[]{:S(2)}) collective-permute-start(bf16[16,6400]{1,0:T(8,128)(2,1)} %tables.1.t0), channel_id=1, source_target_pairs={{0,2},{1,7},{2,4},{3,1},{4,6},{5,3},{6,0},{7,5},{8,10},{9,15},{10,... | collective-permute-start | bytes 614408 | tf_op jit(solution)/shard_map/ppermute | solution.py:308
  6.6 9.6 %collective-permute-start.1 = (bf16[16,6400]{1,0:T(8,128)(2,1)}, bf16[16,6400]{1,0:T(8,128)(2,1)S(1)}, u32[]{:S(2)}, u32[]{:S(2)}) collective-permute-start(bf16[16,6400]{1,0:T(8,128)(2,1)} %tables.1.t0), channel_id=1, source_target_pairs={{0,6},{1,3},{2,0},{3,5},{4,2},{5,7},{6,4},{7,1},{8,14},{9,11},{10,... | collective-permute-start | bytes 614408 | tf_op jit(solution)/shard_map/ppermute | solution.py:308
  13.1 7.0 %collective-permute-start.2 = (bf16[16,6400]{1,0:T(8,128)(2,1)S(1)}, bf16[16,6400]{1,0:T(8,128)(2,1)S(1)}, u32[]{:S(2)}, u32[]{:S(2)}) collective-permute-start(bf16[16,6400]{1,0:T(8,128)(2,1)S(1)} %collective-permute-done.t1), channel_id=1, source_target_pairs={{0,2},{1,7},{2,4},{3,1},{4,6},{5,3},{6,0},{7,5},{8,10},{9,15},{10,... | collective-permute-start | bytes 614408 | tf_op jit(solution)/shard_map/ppermute | solution.py:308
  14.6 14.1 %collective-permute-start.3 = (bf16[16,6400]{1,0:T(8,128)(2,1)}, bf16[16,6400]{1,0:T(8,128)(2,1)S(1)}, u32[]{:S(2)}, u32[]{:S(2)}) collective-permute-start(bf16[16,6400]{1,0:T(8,128)(2,1)} %tables.1.t0), channel_id=1, source_target_pairs={{0,1},{1,0},{2,3},{3,2},{4,5},{5,4},{6,7},{7,6},{8,9},{9,8},{10,11... | collective-permute-start | bytes 614408 | tf_op jit(solution)/shard_map/ppermute | solution.py:312
  15.7 13.1 %collective-permute-start.4 = (bf16[16,6400]{1,0:T(8,128)(2,1)S(1)}, bf16[16,6400]{1,0:T(8,128)(2,1)S(1)}, u32[]{:S(2)}, u32[]{:S(2)}) collective-permute-start(bf16[16,6400]{1,0:T(8,128)(2,1)S(1)} %collective-permute-done.t1), channel_id=1, source_target_pairs={{0,1},{1,0},{2,3},{3,2},{4,5},{5,4},{6,7},{7,6},{8,9},{9,8},{10,11... | collective-permute-start | bytes 614408 | tf_op jit(solution)/shard_map/ppermute | solution.py:312
  16.3 12.5 %collective-permute-start.5 = (bf16[16,6400]{1,0:T(8,128)(2,1)S(1)}, bf16[16,6400]{1,0:T(8,128)(2,1)S(1)}, u32[]{:S(2)}, u32[]{:S(2)}) collective-permute-start(bf16[16,6400]{1,0:T(8,128)(2,1)S(1)} %collective-permute-done.1.t2), channel_id=1, source_target_pairs={{0,1},{1,0},{2,3},{3,2},{4,5},{5,4},{6,7},{7,6},{8,9},{9,8},{10,11... | collective-permute-start | bytes 614408 | tf_op jit(solution)/shard_map/ppermute | solution.py:312
  20.1 8.7 %collective-permute-start.6 = (bf16[16,6400]{1,0:T(8,128)(2,1)S(1)}, bf16[16,6400]{1,0:T(8,128)(2,1)S(1)}, u32[]{:S(2)}, u32[]{:S(2)}) collective-permute-start(bf16[16,6400]{1,0:T(8,128)(2,1)S(1)} %collective-permute-done.2.t3), channel_id=1, source_target_pairs={{0,1},{1,0},{2,3},{3,2},{4,5},{5,4},{6,7},{7,6},{8,9},{9,8},{10,11... | collective-permute-start | bytes 614408 | tf_op jit(solution)/shard_map/ppermute | solution.py:312
  20.2 0.9 %copy-start = (s32[4,8192]{1,0:T(4,128)S(1)}, s32[4,8192]{1,0:T(4,128)}, u32[]{:S(2)}) copy-start(s32[4,8192]{1,0:T(4,128)} %exc_ref.5) | copy-start | bytes 393220
  21.1 0.9 %copy-start.3 = (f32[4,8192]{1,0:T(4,128)S(1)}, f32[4,8192]{1,0:T(4,128)}, u32[]{:S(2)}) copy-start(f32[4,8192]{1,0:T(4,128)} %coef_ref.3) | copy-start | bytes 393220
  22.0 6.8 %copy-start.2 = (bf16[16,6400]{1,0:T(8,128)(2,1)S(1)}, bf16[16,6400]{1,0:T(8,128)(2,1)}, u32[]{:S(2)}) copy-start(bf16[16,6400]{1,0:T(8,128)(2,1)} %tables.1.t0) | copy-start | bytes 614404
  28.7 17.0 %copy-start.5 = (f32[4,128]{1,0:T(4,128)S(1)}, f32[4,128]{1,0:T(4,128)}, u32[]{:S(2)}) copy-start(f32[4,128]{1,0:T(4,128)} %energy_ref.1) | copy-start | bytes 6148
  37.1 1.4 %collective-permute-start.7 = (f32[8,128]{1,0:T(8,128)S(1)}, f32[8,128]{1,0:T(8,128)S(1)}, u32[]{:S(2)}, u32[]{:S(2)}) collective-permute-start(f32[8,128]{1,0:T(8,128)S(1)} %get-tuple-element.11), channel_id=1, source_target_pairs={{0,1},{1,0},{2,3},{3,2},{4,5},{5,4},{6,7},{7,6},{8,9},{9,8},{10,11... | collective-permute-start | bytes 12296 | tf_op jit(solution)/shard_map/ppermute | solution.py:312
  38.5 3.6 %collective-permute-start.10 = (f32[8,128]{1,0:T(8,128)S(1)}, f32[8,128]{1,0:T(8,128)S(1)}, u32[]{:S(2)}, u32[]{:S(2)}) collective-permute-start(f32[8,128]{1,0:T(8,128)S(1)} %add.3.p0), channel_id=1, source_target_pairs={{0,6},{1,7},{2,0},{3,1},{4,2},{5,3},{6,4},{7,5},{8,14},{9,15},{10,... | collective-permute-start | bytes 12296 | tf_op jit(solution)/shard_map/ppermute | solution.py:308
  39.6 5.1 %collective-permute-start.9 = (f32[8,128]{1,0:T(8,128)S(1)}, f32[8,128]{1,0:T(8,128)S(1)}, u32[]{:S(2)}, u32[]{:S(2)}) collective-permute-start(f32[8,128]{1,0:T(8,128)S(1)} %add.3.p0), channel_id=1, source_target_pairs={{0,4},{1,5},{2,6},{3,7},{4,0},{5,1},{6,2},{7,3},{8,12},{9,13},{10,... | collective-permute-start | bytes 12296 | tf_op jit(solution)/shard_map/ppermute | solution.py:308
  40.8 4.8 %collective-permute-start.8 = (f32[8,128]{1,0:T(8,128)S(1)}, f32[8,128]{1,0:T(8,128)S(1)}, u32[]{:S(2)}, u32[]{:S(2)}) collective-permute-start(f32[8,128]{1,0:T(8,128)S(1)} %add.3.p0), channel_id=1, source_target_pairs={{0,2},{1,3},{2,4},{3,5},{4,6},{5,7},{6,0},{7,1},{8,10},{9,11},{10,... | collective-permute-start | bytes 12296 | tf_op jit(solution)/shard_map/ppermute | solution.py:308

commit v4 on v3

--- a/solution.py
+++ b/solution.py
@@ -1,3 +1,5 @@
+import functools
+
 import jax
 import jax.numpy as jnp
 from jax import lax
@@ -22,6 +24,7 @@
 JPAD = 64
 MIB = 1024 * 1024
 UNROLL = 8
+QUADS = PAIRS // 4
 
 F32, BF16 = jnp.float32, jnp.bfloat16
 NN = (((1,), (0,)), ((), ()))
@@ -81,7 +84,15 @@
         out_ref[:, i * V:(i + 1) * V] = tab_s[i * OWN:(i + 1) * OWN, :].astype(BF16)
 
 
-def spread_kernel(exc_ref, coef_ref, spread_ref):
+def columns_kernel(par_ref, exc_ref, coef_ref, spread_ref, oa_ref, oa_s):
+    lane = lax.broadcasted_iota(jnp.int32, (1, V), 1)
+    for blk in range(NBLK):
+        oa_s[blk:blk + 1, :] = jnp.where(lane == par_ref[1, blk], 1.0, 0.0).astype(F32)
+    oa_ref[...] = oa_s[...].astype(BF16)
+    spread_kernel(0, exc_ref, coef_ref, spread_ref)
+
+
+def spread_kernel(side, exc_ref, coef_ref, spread_ref):
     sub_b = lax.broadcasted_iota(jnp.int32, (V, 2 * BLOCK), 0)
     half = lax.broadcasted_iota(jnp.int32, (8, 2 * BLOCK), 1) // BLOCK
     upper = lax.broadcasted_iota(jnp.int32, (8, 2 * BLOCK), 0) // STATES
@@ -89,7 +100,7 @@
     def quad(q, _):
         parts = []
         for h in range(2):
-            where = pl.ds(pl.multiple_of((2 * q + h) * 2 * BLOCK, 2 * BLOCK), 2 * BLOCK)
+            where = pl.ds(pl.multiple_of((side * QUADS * 2 + 2 * q + h) * 2 * BLOCK, 2 * BLOCK), 2 * BLOCK)
             j_row, b_row = exc_ref[2:3, where], exc_ref[3:4, where]
             c4 = coef_ref[:, where]
             c_hi, c_lo = split(jnp.concatenate([c4, c4], axis=0))
@@ -104,7 +115,7 @@
                 w_lo.append(jnp.concatenate([jnp.where(m0, q_lo, 0.0), jnp.where(m1, q_lo, 0.0)], axis=0).astype(BF16))
             parts.append(dot(jnp.concatenate(w_hi, axis=0), pick_b, NT) + dot(jnp.concatenate(w_lo, axis=0), pick_b, NT))
         high = pl.ds(pl.multiple_of(q * 16, 16), 16)
-        low = pl.ds(pl.multiple_of(NBLK * STATES + q * 16, 16), 16)
+        low = pl.ds(pl.multiple_of(QUADS * 16 + q * 16, 16), 16)
         for j in range(NEL):
             both = jnp.concatenate([parts[0][j * 8:(j + 1) * 8], parts[1][j * 8:(j + 1) * 8]], axis=0)
             hi, lo = split(both)
@@ -112,11 +123,11 @@
             spread_ref[low, j * V:(j + 1) * V] = lo
         return _
 
-    lax.fori_loop(0, PAIRS // 2, quad, 0)
-
-
-def value_kernel(par_ref, me_ref, t0, t1, t2, t3, t4, t5, t6, t7, spread_ref, exc_ref, coef_ref,
-                 part_ref, tab_ref, p_ref, tia_ref, v_s, x_s, oa_s, acc_s):
+    lax.fori_loop(0, QUADS, quad, 0)
+
+
+def value_kernel(par_ref, me_ref, t0, t1, t2, t3, t4, t5, t6, t7, half0, half1, oa_ref, exc_ref, coef_ref,
+                 part_ref, tab_ref, p_ref, tia_ref, v_s, x_s, acc_s):
     x, c = lax.shift_right_logical(me_ref[1], 1), jnp.bitwise_and(me_ref[1], 1)
     ahead = 1 - 2 * c
     sources = ((x, c), (x - ahead, c), (x + ahead, c), (x + 2, c),
@@ -126,12 +137,11 @@
         tab_ref[pl.ds(pl.multiple_of(source * OWN, OWN), OWN), :] = t_ref[...]
     for j in range(NEL, JPAD):
         v_s[pl.ds(j, NBLK, stride=JPAD), :] = jnp.zeros((NBLK, GROUP), F32)
-    lane = lax.broadcasted_iota(jnp.int32, (1, V), 1)
-    for blk in range(NBLK):
-        oa_s[blk:blk + 1, :] = jnp.where(lane == par_ref[1, blk], 1.0, 0.0).astype(F32)
-    pick_a = oa_s[...].astype(BF16)
-    x = dot(spread_ref[...], tab_ref[...], NT)
-    x_s[...] = x[0:NBLK * STATES] + x[NBLK * STATES:]
+    rows = QUADS * 16
+    for side, half in enumerate((half0, half1)):
+        x = dot(half[...], tab_ref[...], NT)
+        x_s[side * rows:(side + 1) * rows, :] = x[0:rows] + x[rows:]
+    pick_a = oa_ref[...]
     for j in range(NEL):
         v_s[pl.ds(j, NBLK, stride=JPAD), :] = dot(pick_a, tab_ref[:, j * V:(j + 1) * V], NT)
 
@@ -192,7 +202,13 @@
     scaled = val / guide
     weight = square / guide
     sums = jnp.sum(jnp.where(low, weight, weight * energy), axis=1, keepdims=True)
-    meta = jnp.where(lane == 0, sums, jnp.where(lane == 1, middle, 0.0))
+    meta = jnp.zeros((8, GROUP), F32)
+    for at, value in ((0, sums), (3, middle)):
+        for n in range(3):
+            piece = value.astype(BF16).astype(F32)
+            meta = jnp.where(lane == at + n, piece, meta)
+            value = value - piece
+    meta = jnp.concatenate([meta, meta], axis=0).astype(BF16)
     factor = jnp.where(low, scaled * (energy - middle), scaled)
     f_hi, f_lo = split(factor)
     f16 = jnp.concatenate([f_hi.astype(F32), f_lo.astype(F32)], axis=0).astype(BF16)
@@ -213,6 +229,7 @@
         both = pl.ds(pl.multiple_of(p * 2 * BLOCK, 2 * BLOCK), 2 * BLOCK)
         second = dot(f16, p_ref[:, both])
         second = second[0:8] + second[8:16]
+        terms = []
         for h in range(2):
             dets = pl.ds(pl.multiple_of(p * 2 * BLOCK + h * BLOCK, BLOCK), BLOCK)
             j_row, b_row = exc_ref[2:3, dets], exc_ref[3:4, dets]
@@ -221,24 +238,34 @@
             first = jnp.zeros((8, BLOCK), F32)
             for j in range(NEL):
                 first = jnp.where(j_row == j, y[j * 8:(j + 1) * 8], first)
-            out_ref[p, :, h * BLOCK:(h + 1) * BLOCK] = first - second[:, h * BLOCK:(h + 1) * BLOCK]
-        out_ref[p, :, 2 * BLOCK:3 * BLOCK] = meta
+            terms.append(first - second[:, h * BLOCK:(h + 1) * BLOCK])
+        out_ref[p, :, 0:BLOCK] = jnp.concatenate(terms, axis=0).astype(BF16)
+        out_ref[p, :, BLOCK:2 * BLOCK] = meta
         return _
 
     lax.fori_loop(0, NWALK, slot, 0, unroll=UNROLL)
 
 
 def final_kernel(in_ref, grad_ref, energy_ref):
-    meta = in_ref[0, :, 256:384]
+    lane = lax.broadcasted_iota(jnp.int32, (8, BLOCK), 1)
+    metas = [in_ref[g].astype(F32)[0:8, BLOCK:2 * BLOCK] for g in range(NWALK)]
+    meta = metas[0]
     for g in range(1, NWALK):
-        meta = meta + in_ref[g, :, 256:384]
-    total, weighted = meta[0:STATES, 0:1], meta[STATES:8, 0:1]
+        meta = meta + metas[g]
+    sums = jnp.sum(jnp.where(lane < 3, meta, 0.0), axis=1, keepdims=True)
+    total, weighted = sums[0:STATES], sums[STATES:8]
     energy = weighted / total
-    grad = jnp.zeros((STATES, 256), F32)
+    grads = [jnp.zeros((STATES, BLOCK), F32)] * 2
     for g in range(NWALK):
-        shift = in_ref[g, 0:STATES, 257:258] - energy
-        grad = grad + (in_ref[g, 0:STATES, 0:256] + shift * in_ref[g, STATES:8, 0:256])
-    grad_ref[:, 0, :] = 2.0 * grad / total
+        terms = in_ref[g].astype(F32)
+        middle = jnp.sum(jnp.where((lane >= 3) & (lane < 6), metas[g], 0.0), axis=1, keepdims=True)
+        shift = middle[0:STATES] - energy
+        for h in range(2):
+            grads[h] = grads[h] + (terms[h * 8:h * 8 + STATES, 0:BLOCK]
+                                   + shift * terms[h * 8 + STATES:h * 8 + 8, 0:BLOCK])
+    scale = 2.0 / total
+    grad_ref[:, 0, 0:BLOCK] = grads[0] * scale
+    grad_ref[:, 0, BLOCK:2 * BLOCK] = grads[1] * scale
     place = lax.broadcasted_iota(jnp.int32, (STATES, STATES), 0) == lax.broadcasted_iota(jnp.int32, (STATES, STATES), 1)
     energy_ref[...] = jnp.sum(jnp.where(place, energy, 0.0), axis=0, keepdims=True)
 
@@ -264,31 +291,41 @@
     return pl.CostEstimate(flops=flops, bytes_accessed=8 * MIB, transcendentals=0)
 
 
-def spread(excitations, coeffs):
-    return pl.pallas_call(
-        spread_kernel,
-        out_shape=jax.ShapeDtypeStruct((2 * NBLK * STATES, NEL * V), BF16),
+def spread_first(parents, excitations, coeffs):
+    return pl.pallas_call(
+        columns_kernel,
+        out_shape=[jax.ShapeDtypeStruct((QUADS * 32, NEL * V), BF16), jax.ShapeDtypeStruct((NBLK, V), BF16)],
+        in_specs=[pl.BlockSpec(memory_space=pltpu.SMEM)] + vmem(2), out_specs=vmem(2),
+        scratch_shapes=[pltpu.VMEM((NBLK, V), F32)],
+        compiler_params=params(8), cost_estimate=cost(800_000_000), name="spread_first",
+    )(parents, excitations, coeffs)
+
+
+def spread_second(excitations, coeffs):
+    return pl.pallas_call(
+        functools.partial(spread_kernel, 1),
+        out_shape=jax.ShapeDtypeStruct((QUADS * 32, NEL * V), BF16),
         in_specs=vmem(2), out_specs=vmem(1)[0],
-        compiler_params=params(8), cost_estimate=cost(1_500_000_000), name="spread",
+        compiler_params=params(8), cost_estimate=cost(800_000_000), name="spread_second",
     )(excitations, coeffs)
 
 
-def partial_values(parents, me, tables, spreads, excitations, coeffs):
+def partial_values(parents, me, tables, halves, columns, excitations, coeffs):
     return pl.pallas_call(
         value_kernel,
         out_shape=[jax.ShapeDtypeStruct((8, GROUP), F32), jax.ShapeDtypeStruct((GROUP, NEL * V), BF16),
                    jax.ShapeDtypeStruct((2 * GROUP, KD), BF16), jax.ShapeDtypeStruct((NBLK * 8, GROUP), F32)],
-        in_specs=[pl.BlockSpec(memory_space=pltpu.SMEM)] * 2 + vmem(NDET + 3), out_specs=vmem(4),
+        in_specs=[pl.BlockSpec(memory_space=pltpu.SMEM)] * 2 + vmem(NDET + 5), out_specs=vmem(4),
         scratch_shapes=[pltpu.VMEM((NBLK * JPAD, GROUP), F32), pltpu.VMEM((NBLK * STATES, GROUP), F32),
-                        pltpu.VMEM((NBLK, V), F32), pltpu.VMEM((STATES, GROUP, BLOCK), F32)],
+                        pltpu.VMEM((STATES, GROUP, BLOCK), F32)],
         compiler_params=params(22), name="partial_values",
-    )(parents, me, *tables, spreads, excitations, coeffs)
+    )(parents, me, *tables, *halves, columns, excitations, coeffs)
 
 
 def gradient(me, parts, local_energy, excitations, tab, pair_products, tia):
     return pl.pallas_call(
         grad_kernel,
-        out_shape=[jax.ShapeDtypeStruct((STATES, OWN), F32), jax.ShapeDtypeStruct((NWALK, 8, 384), F32)],
+        out_shape=[jax.ShapeDtypeStruct((STATES, OWN), F32), jax.ShapeDtypeStruct((NWALK, 16, 2 * BLOCK), BF16)],
         in_specs=[pl.BlockSpec(memory_space=pltpu.SMEM)] + vmem(9), out_specs=vmem(2),
         scratch_shapes=[pltpu.VMEM((NBLK, JP * 16, 2 * V), BF16), pltpu.VMEM((4, 8, GROUP), F32)],
         compiler_params=params(20), name="gradient",
@@ -312,21 +349,19 @@
     return lax.ppermute(x, "det", [(i, i ^ 1) for i in range(NDET)])
 
 
-def gather_tables(table):
+def shards(positions, inverse, centers, exponent, orbital_weights, excitations, state_coeffs, local_energy):
+    me = jnp.stack([lax.axis_index("walk"), lax.axis_index("det")])
+    parents = excitations[0:2, ::BLOCK]
+    table = make_table(positions, inverse, centers, exponent, orbital_weights)
     ahead = across(table, lambda c: 1 - 2 * c)
     behind = across(table, lambda c: 2 * c - 1)
+    half0, columns = spread_first(parents, excitations, state_coeffs)
+    ahead, columns = lax.optimization_barrier((ahead, columns))
     beyond = across(ahead, lambda c: 1 - 2 * c)
-    mine = [table, ahead, behind, beyond]
-    return mine + [other_core(t) for t in mine]
-
-
-def shards(positions, inverse, centers, exponent, orbital_weights, excitations, state_coeffs, local_energy):
-    me = jnp.stack([lax.axis_index("walk"), lax.axis_index("det")])
-    table = make_table(positions, inverse, centers, exponent, orbital_weights)
-    tables = gather_tables(table)
-    spreads = spread(excitations, state_coeffs)
-    parents = excitations[0:2, ::BLOCK]
-    part, tab, products, tia = partial_values(parents, me, tables, spreads, excitations, state_coeffs)
+    half1 = spread_second(excitations, state_coeffs)
+    tables = [table, ahead, behind, beyond]
+    tables = tables + [other_core(t) for t in tables]
+    part, tab, products, tia = partial_values(parents, me, tables, (half0, half1), columns, excitations, state_coeffs)
     chip = part + other_core(part)
     parts = [chip] + [across(chip, lambda c, d=d: d) for d in (1, 2, 3)]
     own, messages = gradient(me, parts, local_energy, excitations, tab, products, tia)

time: 80.3 us -> 76 us (0.946)
  waiting for transfers between devices: 13.9 us -> 10.1 us
  blocking collectives: 25.3 us -> 22.5 us
  Pallas kernels: 28.6 us -> 30 us
  local copies, waits for them, and re-layouts: 2.88 us -> 4.13 us
    ppermute x6, waiting for transfers between devices: 13.1 us -> 9.27 us  [across(): lax.ppermute(x, 'det', [(i, (i + 2 * step(i % 2)) % NDET) for i in range(...]
    all_to_all x1, blocking collectives: 25.3 us -> 22.5 us  [shards(): grad, energy = finish(lax.all_to_all(messages, 'walk', 0, 0, tiled=True))]
    ppermute x6, starting transfers between devices: 7.34 us -> 5.7 us  [across(): lax.ppermute(x, 'det', [(i, (i + 2 * step(i % 2)) % NDET) for i in range(...]
    ppermute x5, starting transfers between devices: 1.3 us -> 2.55 us  [other_core(): return lax.ppermute(x, 'det', [(i, i ^ 1) for i in range(NDET)])]
    unnamed x12 -> x16, local copies, waits for them, and re-layouts: 1.83 us -> 2.52 us
    pallas_call x1 -> x2, Pallas kernels: 6.75 us -> 7.27 us  [the longest x1 3.96 us: spread_first(): pl.pallas_call(columns_kernel, out_shape=[jax.ShapeDtypeStruct((QUADS * 3...]
  transfers between devices with their start and end apart: 11 -> 11, of which waited for: 6 -> 5; matrix products, arithmetic and copies ran while one was open for 1% -> 2% of each run, Pallas kernels for 8% -> 10%
where the time goes in v4:
time: 76 us; the launch traced here: 75.8 us
  Pallas kernels  30 us (39%)
  blocking collectives  22.5 us (30%)
  waiting for transfers between devices  10.1 us (13%)
  starting transfers between devices  8.24 us (11%)
  local copies, waits for them, and re-layouts  4.13 us (5%)
    all_to_all x1, blocking collectives, shards(): grad, energy = finish(lax.all_to_all(messages, 'walk', 0, 0, tiled=True))  22.5 us
    ppermute x6, waiting for transfers between devices, across(): lax.ppermute(x, 'det', [(i, (i + 2 * step(i % 2)) % NDET) for i in range(...  9.27 us
    pallas_call x1, Pallas kernels, partial_values(): pl.pallas_call(value_kernel, out_shape=[jax.ShapeDtypeStruct((8, GROUP),...  9.02 us
    pallas_call x1, Pallas kernels, gradient(): pl.pallas_call(grad_kernel, out_shape=[jax.ShapeDtypeStruct((STATES, OWN)...  8.32 us
    ppermute x6, starting transfers between devices, across(): lax.ppermute(x, 'det', [(i, (i + 2 * step(i % 2)) % NDET) for i in range(...  5.7 us
    pallas_call x1, Pallas kernels, make_table(): pl.pallas_call(table_kernel, out_shape=jax.ShapeDtypeStruct((OWN, NEL * V...  4.38 us
    pallas_call x1, Pallas kernels, spread_first(): pl.pallas_call(columns_kernel, out_shape=[jax.ShapeDtypeStruct((QUADS * 3...  3.96 us
    pallas_call x1, Pallas kernels, spread_second(): pl.pallas_call(functools.partial(spread_kernel, 1), out_shape=jax.ShapeDt...  3.31 us
  transfers between devices with their start and end apart: 11, of which 5 were waited for; matrix products, arithmetic and copies ran while one was open for 2% of the time, Pallas kernels for 10%

profile of v4, /device:TPU:32, one launch (start us, length us, event | category | flops | bytes accessed | tf_op | source)
XLA Modules:
  0.0 75.8 jit_solution(13341664341866958572)
XLA Ops:
  0.6 0.0 copy-start.1
  0.6 0.0 copy-start.4
  0.7 4.4 %tables.1.t0 = bf16[16,6400]{1,0:T(8,128)(2,1)} custom-call(f32[3,16,50]{2,1,0:T(8,128)} %pos_hbm.1, f32[50,16,50]{2,1,0:T(8,128)} %bitcast.5, f32[3,512]{1,0:T(4,128)} %cen_hbm.1, f32[1,512]{1,0:T(1,128)} %bitcast.6, f32[512,128]{1,0:T(8,128)} %orb_hbm.1), custom_call_target="tpu_custom_call" | custom-call | tf_op jit(solution)/shard_map/tables/pallas_call | solution.py:278
  5.0 1.6 %collective-permute-start = (bf16[16,6400]{1,0:T(8,128)(2,1)}, bf16[16,6400]{1,0:T(8,128)(2,1)}, u32[]{:S(2)}, u32[]{:S(2)}) collective-permute-start(bf16[16,6400]{1,0:T(8,128)(2,1)} %tables.1.t0), channel_id=1, source_target_pairs={{0,2},{1,7},{2,4},{3,1},{4,6},{5,3},{6,0},{7,5},{8,10},{9,15},{10,... | collective-permute-start | bytes 614408 | tf_op jit(solution)/shard_map/ppermute | solution.py:345
  6.6 1.7 %collective-permute-start.1 = (bf16[16,6400]{1,0:T(8,128)(2,1)}, bf16[16,6400]{1,0:T(8,128)(2,1)}, u32[]{:S(2)}, u32[]{:S(2)}) collective-permute-start(bf16[16,6400]{1,0:T(8,128)(2,1)} %tables.1.t0), channel_id=1, source_target_pairs={{0,6},{1,3},{2,0},{3,5},{4,2},{5,7},{6,4},{7,1},{8,14},{9,11},{10,... | collective-permute-start | bytes 614408 | tf_op jit(solution)/shard_map/ppermute | solution.py:345
  8.4 1.6 %slice.3.par_ref = s32[2,64]{1,0:T(2,128)} slice(s32[4,8192]{1,0:T(4,128)} %exc_ref.7), slice={[0:2:1], [0:8192:128]} | slice | bytes 1024 | tf_op jit(solution)/shard_map/slice | solution.py:354
  10.0 0.9 %copy-done = s32[4,8192]{1,0:T(4,128)S(1)} copy-done((s32[4,8192]{1,0:T(4,128)S(1)}, s32[4,8192]{1,0:T(4,128)}, u32[]{:S(2)}) %copy-start) | copy-done | bytes 131096
  10.9 0.9 %copy-done.3 = f32[4,8192]{1,0:T(4,128)S(1)} copy-done((f32[4,8192]{1,0:T(4,128)S(1)}, f32[4,8192]{1,0:T(4,128)}, u32[]{:S(2)}) %copy-start.3) | copy-done | bytes 131096
  11.8 0.7 copy-done.5
  12.5 4.0 %spread_first.1 = (bf16[256,6400]{1,0:T(8,128)(2,1)S(1)}, bf16[64,128]{1,0:T(8,128)(2,1)S(1)}) custom-call(s32[2,64]{1,0:T(2,128)S(1)} %copy-done.5, s32[4,8192]{1,0:T(4,128)S(1)} %copy-done, f32[4,8192]{1,0:T(4,128)S(1)} %copy-done.3), custom_call_target="tpu_custom_call" | custom-call | flops 800000000 | bytes 8388608 | tf_op jit(solution)/shard_map/spread_first/pallas_call | solution.py:295
  16.4 0.4 collective-permute-start.2
  16.8 1.5 %collective-permute-start.3 = (bf16[16,6400]{1,0:T(8,128)(2,1)}, bf16[16,6400]{1,0:T(8,128)(2,1)}, u32[]{:S(2)}, u32[]{:S(2)}) collective-permute-start(bf16[16,6400]{1,0:T(8,128)(2,1)} %tables.1.t0), channel_id=1, source_target_pairs={{0,1},{1,0},{2,3},{3,2},{4,5},{5,4},{6,7},{7,6},{8,9},{9,8},{10,11... | collective-permute-start | bytes 614408 | tf_op jit(solution)/shard_map/ppermute | solution.py:349
  18.3 0.5 collective-permute-start.5
  18.8 5.0 %collective-permute-done.2.t3 = bf16[16,6400]{1,0:T(8,128)(2,1)} collective-permute-done((bf16[16,6400]{1,0:T(8,128)(2,1)}, bf16[16,6400]{1,0:T(8,128)(2,1)}, u32[]{:S(2)}, u32[]{:S(2)}) %collective-permute-start.2) | collective-permute-done | bytes 204832 | tf_op jit(solution)/shard_map/ppermute | solution.py:345
  23.8 0.0 collective-permute-start.6
  23.8 0.0 copy-start.6
  23.8 3.3 %spread_second.1.half1 = bf16[256,6400]{1,0:T(8,128)(2,1)S(1)} custom-call(s32[4,8192]{1,0:T(4,128)S(1)} %copy-done.1, f32[4,8192]{1,0:T(4,128)S(1)} %copy-done.4), custom_call_target="tpu_custom_call" | custom-call | flops 800000000 | bytes 8388608 | tf_op jit(solution)/shard_map/spread_second/pallas_call | solution.py:305
  27.1 0.1 pad_add_fusion.me_ref
  27.2 0.0 collective-permute-done.3.t4
  27.3 0.0 copy-start.7
  27.3 9.0 %partial_values.1 = (f32[8,128]{1,0:T(8,128)S(1)}, bf16[128,6400]{1,0:T(8,128)(2,1)S(1)}, bf16[256,8192]{1,0:T(8,128)(2,1)S(1)}, f32[512,128]{1,0:T(8,128)S(1)}) custom-call(s32[2,64]{1,0:T(2,128)S(1)} %copy-done.6, s32[2]{0:T(128)S(1)} %pad_add_fusion.me_ref, bf16[16,6400]{1,0:T(8,128)(2,1)S(1)} %copy-done.2, bf16[16,6400]{1,0:T(8,128)(2,1)} %collective-permute-done.t1, ...), custom_call_target="tpu_custom_call" | custom-call | tf_op jit(solution)/shard_map/partial_values/pallas_call | solution.py:314
  36.3 0.6 collective-permute-start.7
  36.9 0.8 %collective-permute-done.7 = f32[8,128]{1,0:T(8,128)S(1)} collective-permute-done((f32[8,128]{1,0:T(8,128)S(1)}, f32[8,128]{1,0:T(8,128)S(1)}, u32[]{:S(2)}, u32[]{:S(2)}) %collective-permute-start.7) | collective-permute-done | bytes 4128 | tf_op jit(solution)/shard_map/ppermute | solution.py:349
  37.7 0.7 collective-permute-start.10
  38.4 0.4 collective-permute-start.9
  38.8 0.9 %collective-permute-start.8 = (f32[8,128]{1,0:T(8,128)S(1)}, f32[8,128]{1,0:T(8,128)S(1)}, u32[]{:S(2)}, u32[]{:S(2)}) collective-permute-start(f32[8,128]{1,0:T(8,128)S(1)} %add.3.p0), channel_id=1, source_target_pairs={{0,2},{1,3},{2,4},{3,5},{4,6},{5,7},{6,0},{7,1},{8,10},{9,11},{10,... | collective-permute-start | bytes 12296 | tf_op jit(solution)/shard_map/ppermute | solution.py:345
  39.7 1.6 %collective-permute-done.10.p3 = f32[8,128]{1,0:T(8,128)S(1)} collective-permute-done((f32[8,128]{1,0:T(8,128)S(1)}, f32[8,128]{1,0:T(8,128)S(1)}, u32[]{:S(2)}, u32[]{:S(2)}) %collective-permute-start.10) | collective-permute-done | bytes 4128 | tf_op jit(solution)/shard_map/ppermute | solution.py:345
  41.3 2.2 %collective-permute-done.9.p2 = f32[8,128]{1,0:T(8,128)S(1)} collective-permute-done((f32[8,128]{1,0:T(8,128)S(1)}, f32[8,128]{1,0:T(8,128)S(1)}, u32[]{:S(2)}, u32[]{:S(2)}) %collective-permute-start.9) | collective-permute-done | bytes 4128 | tf_op jit(solution)/shard_map/ppermute | solution.py:345
  43.5 0.5 collective-permute-done.8.p1
  44.0 8.3 %gradient.1 = (f32[4,16]{1,0:T(4,128)}, bf16[32,16,256]{2,1,0:T(8,128)(2,1)S(1)}) custom-call(s32[2]{0:T(128)S(1)} %pad_add_fusion.me_ref, f32[8,128]{1,0:T(8,128)S(1)} %add.3.p0, f32[8,128]{1,0:T(8,128)S(1)} %collective-permute-done.8.p1, f32[8,128]{1,0:T(8,128)S(1)} %collective-permute-done.9.p2, f32[8,128]{1,0:T(8,128)S(1)} %collective-permute-done.10.p3, ...), custom_call_target="tpu_custom_call" | custom-call | tf_op jit(solution)/shard_map/gradient/pallas_call | solution.py:326
  52.3 22.5 %all_to_all.5.in_ref = bf16[32,16,256]{2,1,0:T(8,128)(2,1)S(1)} all-to-all(bf16[32,16,256]{2,1,0:T(8,128)(2,1)S(1)} %get-tuple-element.23), channel_id=1, replica_groups=mesh['walk'=32,'det'=8] {'walk'}, dimensions={0} | all-to-all | bytes 524288 | tf_op jit(solution)/shard_map/all_to_all | solution.py:368
  74.8 1.0 %finish.1 = (f32[4,1,256]{2,1,0:T(1,128)}, f32[1,4]{1,0:T(1,128)}) custom-call(bf16[32,16,256]{2,1,0:T(8,128)(2,1)S(1)} %all_to_all.5.in_ref), custom_call_target="tpu_custom_call" | custom-call | tf_op jit(solution)/shard_map/finish/pallas_call | solution.py:336
  (16 shorter events, 0.0 us)
Async XLA Ops:
  0.6 23.2 %copy-start.1 = (s32[4,8192]{1,0:T(4,128)S(1)}, s32[4,8192]{1,0:T(4,128)}, u32[]{:S(2)}) copy-start(s32[4,8192]{1,0:T(4,128)} %exc_ref.7) | copy-start | bytes 393220
  0.6 23.2 %copy-start.4 = (f32[4,8192]{1,0:T(4,128)S(1)}, f32[4,8192]{1,0:T(4,128)}, u32[]{:S(2)}) copy-start(f32[4,8192]{1,0:T(4,128)} %coef_ref.5) | copy-start | bytes 393220
  5.0 11.4 %collective-permute-start = (bf16[16,6400]{1,0:T(8,128)(2,1)}, bf16[16,6400]{1,0:T(8,128)(2,1)}, u32[]{:S(2)}, u32[]{:S(2)}) collective-permute-start(bf16[16,6400]{1,0:T(8,128)(2,1)} %tables.1.t0), channel_id=1, source_target_pairs={{0,2},{1,7},{2,4},{3,1},{4,6},{5,3},{6,0},{7,5},{8,10},{9,15},{10,... | collective-permute-start | bytes 614408 | tf_op jit(solution)/shard_map/ppermute | solution.py:345
  6.6 11.7 %collective-permute-start.1 = (bf16[16,6400]{1,0:T(8,128)(2,1)}, bf16[16,6400]{1,0:T(8,128)(2,1)}, u32[]{:S(2)}, u32[]{:S(2)}) collective-permute-start(bf16[16,6400]{1,0:T(8,128)(2,1)} %tables.1.t0), channel_id=1, source_target_pairs={{0,6},{1,3},{2,0},{3,5},{4,2},{5,7},{6,4},{7,1},{8,14},{9,11},{10,... | collective-permute-start | bytes 614408 | tf_op jit(solution)/shard_map/ppermute | solution.py:345
  10.0 0.9 %copy-start = (s32[4,8192]{1,0:T(4,128)S(1)}, s32[4,8192]{1,0:T(4,128)}, u32[]{:S(2)}) copy-start(s32[4,8192]{1,0:T(4,128)} %exc_ref.7) | copy-start | bytes 393220
  10.9 0.9 %copy-start.3 = (f32[4,8192]{1,0:T(4,128)S(1)}, f32[4,8192]{1,0:T(4,128)}, u32[]{:S(2)}) copy-start(f32[4,8192]{1,0:T(4,128)} %coef_ref.5) | copy-start | bytes 393220
  11.8 0.7 copy-start.5
  16.4 7.4 %collective-permute-start.2 = (bf16[16,6400]{1,0:T(8,128)(2,1)}, bf16[16,6400]{1,0:T(8,128)(2,1)}, u32[]{:S(2)}, u32[]{:S(2)}) collective-permute-start(bf16[16,6400]{1,0:T(8,128)(2,1)} %collective-permute-done.t1), channel_id=1, source_target_pairs={{0,2},{1,7},{2,4},{3,1},{4,6},{5,3},{6,0},{7,5},{8,10},{9,15},{10,... | collective-permute-start | bytes 614408 | tf_op jit(solution)/shard_map/ppermute | solution.py:345
  16.8 10.4 %collective-permute-start.3 = (bf16[16,6400]{1,0:T(8,128)(2,1)}, bf16[16,6400]{1,0:T(8,128)(2,1)}, u32[]{:S(2)}, u32[]{:S(2)}) collective-permute-start(bf16[16,6400]{1,0:T(8,128)(2,1)} %tables.1.t0), channel_id=1, source_target_pairs={{0,1},{1,0},{2,3},{3,2},{4,5},{5,4},{6,7},{7,6},{8,9},{9,8},{10,11... | collective-permute-start | bytes 614408 | tf_op jit(solution)/shard_map/ppermute | solution.py:349
  18.3 9.0 %collective-permute-start.4 = (bf16[16,6400]{1,0:T(8,128)(2,1)}, bf16[16,6400]{1,0:T(8,128)(2,1)}, u32[]{:S(2)}, u32[]{:S(2)}) collective-permute-start(bf16[16,6400]{1,0:T(8,128)(2,1)} %collective-permute-done.t1), channel_id=1, source_target_pairs={{0,1},{1,0},{2,3},{3,2},{4,5},{5,4},{6,7},{7,6},{8,9},{9,8},{10,11... | collective-permute-start | bytes 614408 | tf_op jit(solution)/shard_map/ppermute | solution.py:349
  18.3 9.0 %collective-permute-start.5 = (bf16[16,6400]{1,0:T(8,128)(2,1)}, bf16[16,6400]{1,0:T(8,128)(2,1)}, u32[]{:S(2)}, u32[]{:S(2)}) collective-permute-start(bf16[16,6400]{1,0:T(8,128)(2,1)} %collective-permute-done.1.t2), channel_id=1, source_target_pairs={{0,1},{1,0},{2,3},{3,2},{4,5},{5,4},{6,7},{7,6},{8,9},{9,8},{10,11... | collective-permute-start | bytes 614408 | tf_op jit(solution)/shard_map/ppermute | solution.py:349
  23.8 3.4 %collective-permute-start.6 = (bf16[16,6400]{1,0:T(8,128)(2,1)}, bf16[16,6400]{1,0:T(8,128)(2,1)}, u32[]{:S(2)}, u32[]{:S(2)}) collective-permute-start(bf16[16,6400]{1,0:T(8,128)(2,1)} %collective-permute-done.2.t3), channel_id=1, source_target_pairs={{0,1},{1,0},{2,3},{3,2},{4,5},{5,4},{6,7},{7,6},{8,9},{9,8},{10,11... | collective-permute-start | bytes 614408 | tf_op jit(solution)/shard_map/ppermute | solution.py:349
  23.8 3.4 %copy-start.2 = (bf16[16,6400]{1,0:T(8,128)(2,1)S(1)}, bf16[16,6400]{1,0:T(8,128)(2,1)}, u32[]{:S(2)}) copy-start(bf16[16,6400]{1,0:T(8,128)(2,1)} %tables.1.t0) | copy-start | bytes 614404
  23.8 3.4 %copy-start.6 = (s32[2,64]{1,0:T(2,128)S(1)}, s32[2,64]{1,0:T(2,128)}, u32[]{:S(2)}) copy-start(s32[2,64]{1,0:T(2,128)} %slice.3.par_ref) | copy-start | bytes 1540
  27.3 16.7 %copy-start.7 = (f32[4,128]{1,0:T(4,128)S(1)}, f32[4,128]{1,0:T(4,128)}, u32[]{:S(2)}) copy-start(f32[4,128]{1,0:T(4,128)} %energy_ref.1) | copy-start | bytes 6148
  36.3 1.4 %collective-permute-start.7 = (f32[8,128]{1,0:T(8,128)S(1)}, f32[8,128]{1,0:T(8,128)S(1)}, u32[]{:S(2)}, u32[]{:S(2)}) collective-permute-start(f32[8,128]{1,0:T(8,128)S(1)} %get-tuple-element.19), channel_id=1, source_target_pairs={{0,1},{1,0},{2,3},{3,2},{4,5},{5,4},{6,7},{7,6},{8,9},{9,8},{10,11... | collective-permute-start | bytes 12296 | tf_op jit(solution)/shard_map/ppermute | solution.py:349
  37.7 3.6 %collective-permute-start.10 = (f32[8,128]{1,0:T(8,128)S(1)}, f32[8,128]{1,0:T(8,128)S(1)}, u32[]{:S(2)}, u32[]{:S(2)}) collective-permute-start(f32[8,128]{1,0:T(8,128)S(1)} %add.3.p0), channel_id=1, source_target_pairs={{0,6},{1,7},{2,0},{3,1},{4,2},{5,3},{6,4},{7,5},{8,14},{9,15},{10,... | collective-permute-start | bytes 12296 | tf_op jit(solution)/shard_map/ppermute | solution.py:345
  38.4 5.1 %collective-permute-start.9 = (f32[8,128]{1,0:T(8,128)S(1)}, f32[8,128]{1,0:T(8,128)S(1)}, u32[]{:S(2)}, u32[]{:S(2)}) collective-permute-start(f32[8,128]{1,0:T(8,128)S(1)} %add.3.p0), channel_id=1, source_target_pairs={{0,4},{1,5},{2,6},{3,7},{4,0},{5,1},{6,2},{7,3},{8,12},{9,13},{10,... | collective-permute-start | bytes 12296 | tf_op jit(solution)/shard_map/ppermute | solution.py:345
  38.8 5.1 %collective-permute-start.8 = (f32[8,128]{1,0:T(8,128)S(1)}, f32[8,128]{1,0:T(8,128)S(1)}, u32[]{:S(2)}, u32[]{:S(2)}) collective-permute-start(f32[8,128]{1,0:T(8,128)S(1)} %add.3.p0), channel_id=1, source_target_pairs={{0,2},{1,3},{2,4},{3,5},{4,6},{5,7},{6,0},{7,1},{8,10},{9,11},{10,... | collective-permute-start | bytes 12296 | tf_op jit(solution)/shard_map/ppermute | solution.py:345

commit v5 on v4

--- a/solution.py
+++ b/solution.py
@@ -84,15 +84,13 @@
         out_ref[:, i * V:(i + 1) * V] = tab_s[i * OWN:(i + 1) * OWN, :].astype(BF16)
 
 
-def columns_kernel(par_ref, exc_ref, coef_ref, spread_ref, oa_ref, oa_s):
+def spread_kernel(side, exc_ref, coef_ref, spread_ref, oa_ref, oa_s):
     lane = lax.broadcasted_iota(jnp.int32, (1, V), 1)
-    for blk in range(NBLK):
-        oa_s[blk:blk + 1, :] = jnp.where(lane == par_ref[1, blk], 1.0, 0.0).astype(F32)
+    for n in range(NBLK // 2):
+        blk = side * (NBLK // 2) + n
+        parent = exc_ref[1:2, blk * BLOCK:(blk + 1) * BLOCK]
+        oa_s[n:n + 1, :] = jnp.where(lane == parent, 1.0, 0.0).astype(F32)
     oa_ref[...] = oa_s[...].astype(BF16)
-    spread_kernel(0, exc_ref, coef_ref, spread_ref)
-
-
-def spread_kernel(side, exc_ref, coef_ref, spread_ref):
     sub_b = lax.broadcasted_iota(jnp.int32, (V, 2 * BLOCK), 0)
     half = lax.broadcasted_iota(jnp.int32, (8, 2 * BLOCK), 1) // BLOCK
     upper = lax.broadcasted_iota(jnp.int32, (8, 2 * BLOCK), 0) // STATES
@@ -126,8 +124,10 @@
     lax.fori_loop(0, QUADS, quad, 0)
 
 
-def value_kernel(par_ref, me_ref, t0, t1, t2, t3, t4, t5, t6, t7, half0, half1, oa_ref, exc_ref, coef_ref,
-                 part_ref, tab_ref, p_ref, tia_ref, v_s, x_s, acc_s):
+def value_kernel(me_ref, t0, t1, t2, t3, t4, t5, t6, t7, half0, half1, oa0, oa1, exc_ref, coef_ref,
+                 part_ref, tab_ref, p_ref, tia_ref, v_s, x_s, acc_s, exc_smem, sem):
+    indices = pltpu.make_async_copy(exc_ref, exc_smem, sem)
+    indices.start()
     x, c = lax.shift_right_logical(me_ref[1], 1), jnp.bitwise_and(me_ref[1], 1)
     ahead = 1 - 2 * c
     sources = ((x, c), (x - ahead, c), (x + ahead, c), (x + 2, c),
@@ -141,12 +141,14 @@
     for side, half in enumerate((half0, half1)):
         x = dot(half[...], tab_ref[...], NT)
         x_s[side * rows:(side + 1) * rows, :] = x[0:rows] + x[rows:]
-    pick_a = oa_ref[...]
+    pick_a = jnp.concatenate([oa0[...], oa1[...]], axis=0)
     for j in range(NEL):
         v_s[pl.ds(j, NBLK, stride=JPAD), :] = dot(pick_a, tab_ref[:, j * V:(j + 1) * V], NT)
 
+    indices.wait()
+
     def own_entry(blk, _):
-        row = v_s[pl.ds(blk * JPAD + par_ref[0, blk], 1), :]
+        row = v_s[pl.ds(blk * JPAD + exc_smem[0, blk * BLOCK], 1), :]
         tia_ref[pl.ds(pl.multiple_of(blk * 8, 8), 8), :] = jnp.broadcast_to(row, (8, GROUP))
         return _
 
@@ -163,7 +165,7 @@
             dets = pl.ds(pl.multiple_of(blk * BLOCK, BLOCK), BLOCK)
             pick_j = jnp.where(sub_j == exc_ref[2:3, dets], 1.0, 0.0).astype(BF16)
             pick_b = jnp.where(sub_b == exc_ref[3:4, dets], 1.0, 0.0).astype(BF16)
-            t_i = tab_ref[:, pl.ds(pl.multiple_of(par_ref[0, blk] * V, V), V)]
+            t_i = tab_ref[:, pl.ds(pl.multiple_of(exc_smem[0, blk * BLOCK] * V, V), V)]
             along = dot(t_i, pick_b)
             column = v_s[pl.ds(pl.multiple_of(blk * JPAD, JPAD), JPAD), :].astype(BF16)
             down = dot(column, pick_j, TN)
@@ -291,35 +293,27 @@
     return pl.CostEstimate(flops=flops, bytes_accessed=8 * MIB, transcendentals=0)
 
 
-def spread_first(parents, excitations, coeffs):
-    return pl.pallas_call(
-        columns_kernel,
-        out_shape=[jax.ShapeDtypeStruct((QUADS * 32, NEL * V), BF16), jax.ShapeDtypeStruct((NBLK, V), BF16)],
-        in_specs=[pl.BlockSpec(memory_space=pltpu.SMEM)] + vmem(2), out_specs=vmem(2),
-        scratch_shapes=[pltpu.VMEM((NBLK, V), F32)],
-        compiler_params=params(8), cost_estimate=cost(800_000_000), name="spread_first",
-    )(parents, excitations, coeffs)
-
-
-def spread_second(excitations, coeffs):
-    return pl.pallas_call(
-        functools.partial(spread_kernel, 1),
-        out_shape=jax.ShapeDtypeStruct((QUADS * 32, NEL * V), BF16),
-        in_specs=vmem(2), out_specs=vmem(1)[0],
-        compiler_params=params(8), cost_estimate=cost(800_000_000), name="spread_second",
+def spread(side, excitations, coeffs):
+    return pl.pallas_call(
+        functools.partial(spread_kernel, side),
+        out_shape=[jax.ShapeDtypeStruct((QUADS * 32, NEL * V), BF16), jax.ShapeDtypeStruct((NBLK // 2, V), BF16)],
+        in_specs=vmem(2), out_specs=vmem(2),
+        scratch_shapes=[pltpu.VMEM((NBLK // 2, V), F32)],
+        compiler_params=params(8), cost_estimate=cost(800_000_000), name="spread",
     )(excitations, coeffs)
 
 
-def partial_values(parents, me, tables, halves, columns, excitations, coeffs):
+def partial_values(me, tables, halves, columns, excitations, coeffs):
     return pl.pallas_call(
         value_kernel,
         out_shape=[jax.ShapeDtypeStruct((8, GROUP), F32), jax.ShapeDtypeStruct((GROUP, NEL * V), BF16),
                    jax.ShapeDtypeStruct((2 * GROUP, KD), BF16), jax.ShapeDtypeStruct((NBLK * 8, GROUP), F32)],
-        in_specs=[pl.BlockSpec(memory_space=pltpu.SMEM)] * 2 + vmem(NDET + 5), out_specs=vmem(4),
+        in_specs=[pl.BlockSpec(memory_space=pltpu.SMEM)] + vmem(NDET + 6), out_specs=vmem(4),
         scratch_shapes=[pltpu.VMEM((NBLK * JPAD, GROUP), F32), pltpu.VMEM((NBLK * STATES, GROUP), F32),
-                        pltpu.VMEM((STATES, GROUP, BLOCK), F32)],
+                        pltpu.VMEM((STATES, GROUP, BLOCK), F32),
+                        pltpu.SMEM((4, KD), jnp.int32), pltpu.SemaphoreType.DMA],
         compiler_params=params(22), name="partial_values",
-    )(parents, me, *tables, *halves, columns, excitations, coeffs)
+    )(me, *tables, *halves, *columns, excitations, coeffs)
 
 
 def gradient(me, parts, local_energy, excitations, tab, pair_products, tia):
@@ -351,17 +345,16 @@
 
 def shards(positions, inverse, centers, exponent, orbital_weights, excitations, state_coeffs, local_energy):
     me = jnp.stack([lax.axis_index("walk"), lax.axis_index("det")])
-    parents = excitations[0:2, ::BLOCK]
     table = make_table(positions, inverse, centers, exponent, orbital_weights)
     ahead = across(table, lambda c: 1 - 2 * c)
     behind = across(table, lambda c: 2 * c - 1)
-    half0, columns = spread_first(parents, excitations, state_coeffs)
-    ahead, columns = lax.optimization_barrier((ahead, columns))
+    half0, columns0 = spread(0, excitations, state_coeffs)
+    ahead, columns0 = lax.optimization_barrier((ahead, columns0))
     beyond = across(ahead, lambda c: 1 - 2 * c)
-    half1 = spread_second(excitations, state_coeffs)
-    tables = [table, ahead, behind, beyond]
-    tables = tables + [other_core(t) for t in tables]
-    part, tab, products, tia = partial_values(parents, me, tables, (half0, half1), columns, excitations, state_coeffs)
+    half1, columns1 = spread(1, excitations, state_coeffs)
+    near = [other_core(t) for t in (table, ahead, behind)]
+    tables = [table, ahead, behind, beyond] + near + [other_core(beyond)]
+    part, tab, products, tia = partial_values(me, tables, (half0, half1), (columns0, columns1), excitations, state_coeffs)
     chip = part + other_core(part)
     parts = [chip] + [across(chip, lambda c, d=d: d) for d in (1, 2, 3)]
     own, messages = gradient(me, parts, local_energy, excitations, tab, products, tia)

time: 76 us -> 78.2 us (1.029)
  local copies, waits for them, and re-layouts: 4.13 us -> 5.43 us
    unnamed x16, local copies, waits for them, and re-layouts: 2.52 us -> 5.43 us
    slice x1 -> x0, local copies, waits for them, and re-layouts: 1.61 us -> none  [shards(): parents = excitations[0:2, ::BLOCK]]
    pallas_call x1, Pallas kernels: 9.02 us -> 9.99 us  [partial_values(): pl.pallas_call(value_kernel, out_shape=[jax.ShapeDtypeStruct((8, GROUP),...]
    ppermute x6, starting transfers between devices: 5.7 us -> 6.53 us  [across(): lax.ppermute(x, 'det', [(i, (i + 2 * step(i % 2)) % NDET) for i in range(...]
  transfers between devices with their start and end apart: 11 -> 11, of which waited for: 5 -> 5; matrix products, arithmetic and copies ran while one was open for 2% -> 0% of each run, Pallas kernels for 10% -> 9%
where the time goes in v5:
time: 78.2 us; the launch traced here: 77.9 us
  Pallas kernels  30.3 us (39%)
  blocking collectives  22.5 us (29%)
  waiting for transfers between devices  10.5 us (13%)
  starting transfers between devices  8.33 us (11%)
  local copies, waits for them, and re-layouts  5.43 us (7%)
    all_to_all x1, blocking collectives, shards(): grad, energy = finish(lax.all_to_all(messages, 'walk', 0, 0, tiled=True))  22.5 us
    pallas_call x1, Pallas kernels, partial_values(): pl.pallas_call(value_kernel, out_shape=[jax.ShapeDtypeStruct((8, GROUP),...  9.99 us
    ppermute x6, waiting for transfers between devices, across(): lax.ppermute(x, 'det', [(i, (i + 2 * step(i % 2)) % NDET) for i in range(...  9.66 us
    pallas_call x1, Pallas kernels, gradient(): pl.pallas_call(grad_kernel, out_shape=[jax.ShapeDtypeStruct((STATES, OWN)...  8.3 us
    pallas_call x2, Pallas kernels, spread(): pl.pallas_call(functools.partial(spread_kernel, side), out_shape=[jax.Sha...  6.72 us
    ppermute x6, starting transfers between devices, across(): lax.ppermute(x, 'det', [(i, (i + 2 * step(i % 2)) % NDET) for i in range(...  6.53 us
    unnamed x16, local copies, waits for them, and re-layouts  5.43 us
    pallas_call x1, Pallas kernels, make_table(): pl.pallas_call(table_kernel, out_shape=jax.ShapeDtypeStruct((OWN, NEL * V...  4.35 us
  transfers between devices with their start and end apart: 11, of which 5 were waited for; matrix products, arithmetic and copies ran while one was open for 0% of the time, Pallas kernels for 9%

profile of v5, /device:TPU:32, one launch (start us, length us, event | category | flops | bytes accessed | tf_op | source)
XLA Modules:
  0.0 77.9 jit_solution(17814984769631714860)
XLA Ops:
  0.6 4.3 %tables.1.t0 = bf16[16,6400]{1,0:T(8,128)(2,1)} custom-call(f32[3,16,50]{2,1,0:T(8,128)} %pos_hbm.1, f32[50,16,50]{2,1,0:T(8,128)} %bitcast.5, f32[3,512]{1,0:T(4,128)} %cen_hbm.1, f32[1,512]{1,0:T(1,128)} %bitcast.6, f32[512,128]{1,0:T(8,128)} %orb_hbm.1), custom_call_target="tpu_custom_call" | custom-call | tf_op jit(solution)/shard_map/tables/pallas_call | solution.py:280
  5.0 1.6 %collective-permute-start = (bf16[16,6400]{1,0:T(8,128)(2,1)}, bf16[16,6400]{1,0:T(8,128)(2,1)}, u32[]{:S(2)}, u32[]{:S(2)}) collective-permute-start(bf16[16,6400]{1,0:T(8,128)(2,1)} %tables.1.t0), channel_id=1, source_target_pairs={{0,2},{1,7},{2,4},{3,1},{4,6},{5,3},{6,0},{7,5},{8,10},{9,15},{10,... | collective-permute-start | bytes 614408 | tf_op jit(solution)/shard_map/ppermute | solution.py:339
  6.6 1.7 %collective-permute-start.1 = (bf16[16,6400]{1,0:T(8,128)(2,1)}, bf16[16,6400]{1,0:T(8,128)(2,1)}, u32[]{:S(2)}, u32[]{:S(2)}) collective-permute-start(bf16[16,6400]{1,0:T(8,128)(2,1)} %tables.1.t0), channel_id=1, source_target_pairs={{0,6},{1,3},{2,0},{3,5},{4,2},{5,7},{6,4},{7,1},{8,14},{9,11},{10,... | collective-permute-start | bytes 614408 | tf_op jit(solution)/shard_map/ppermute | solution.py:339
  8.3 0.9 %copy-done.1 = s32[4,8192]{1,0:T(4,128)S(1)} copy-done((s32[4,8192]{1,0:T(4,128)S(1)}, s32[4,8192]{1,0:T(4,128)}, u32[]{:S(2)}) %copy-start.1) | copy-done | bytes 131096
  9.2 0.9 %copy-done.4 = f32[4,8192]{1,0:T(4,128)S(1)} copy-done((f32[4,8192]{1,0:T(4,128)S(1)}, f32[4,8192]{1,0:T(4,128)}, u32[]{:S(2)}) %copy-start.4) | copy-done | bytes 131096
  10.1 3.4 %spread.2 = (bf16[256,6400]{1,0:T(8,128)(2,1)S(1)}, bf16[32,128]{1,0:T(8,128)(2,1)S(1)}) custom-call(s32[4,8192]{1,0:T(4,128)S(1)} %copy-done.1, f32[4,8192]{1,0:T(4,128)S(1)} %copy-done.4), custom_call_target="tpu_custom_call" | custom-call | flops 800000000 | bytes 8388608 | tf_op jit(solution)/shard_map/spread/pallas_call | solution.py:297
  13.5 0.0 collective-permute-done.t1
  13.5 1.1 %collective-permute-start.2 = (bf16[16,6400]{1,0:T(8,128)(2,1)}, bf16[16,6400]{1,0:T(8,128)(2,1)}, u32[]{:S(2)}, u32[]{:S(2)}) collective-permute-start(bf16[16,6400]{1,0:T(8,128)(2,1)} %collective-permute-done.t1), channel_id=1, source_target_pairs={{0,2},{1,7},{2,4},{3,1},{4,6},{5,3},{6,0},{7,5},{8,10},{9,15},{10,... | collective-permute-start | bytes 614408 | tf_op jit(solution)/shard_map/ppermute | solution.py:339
  14.7 0.7 collective-permute-start.3
  15.4 0.0 collective-permute-start.4
  15.4 0.0 collective-permute-done.1.t2
  15.4 0.5 collective-permute-start.5
  15.9 5.0 %collective-permute-done.2.t3 = bf16[16,6400]{1,0:T(8,128)(2,1)} collective-permute-done((bf16[16,6400]{1,0:T(8,128)(2,1)}, bf16[16,6400]{1,0:T(8,128)(2,1)}, u32[]{:S(2)}, u32[]{:S(2)}) %collective-permute-start.2) | collective-permute-done | bytes 204832 | tf_op jit(solution)/shard_map/ppermute | solution.py:339
  20.9 0.9 %copy-done.2 = s32[4,8192]{1,0:T(4,128)S(1)} copy-done((s32[4,8192]{1,0:T(4,128)S(1)}, s32[4,8192]{1,0:T(4,128)}, u32[]{:S(2)}) %copy-start.2) | copy-done | bytes 131096
  21.8 0.9 %copy-done.5 = f32[4,8192]{1,0:T(4,128)S(1)} copy-done((f32[4,8192]{1,0:T(4,128)S(1)}, f32[4,8192]{1,0:T(4,128)}, u32[]{:S(2)}) %copy-start.5) | copy-done | bytes 131096
  22.7 3.3 %spread.3 = (bf16[256,6400]{1,0:T(8,128)(2,1)S(1)}, bf16[32,128]{1,0:T(8,128)(2,1)S(1)}) custom-call(s32[4,8192]{1,0:T(4,128)S(1)} %copy-done.2, f32[4,8192]{1,0:T(4,128)S(1)} %copy-done.5), custom_call_target="tpu_custom_call" | custom-call | flops 800000000 | bytes 8388608 | tf_op jit(solution)/shard_map/spread/pallas_call | solution.py:297
  26.0 0.1 pad_add_fusion.me_ref
  26.2 0.0 copy-start.3
  26.2 0.9 %copy-done.3 = s32[4,8192]{1,0:T(4,128)S(1)} copy-done((s32[4,8192]{1,0:T(4,128)S(1)}, s32[4,8192]{1,0:T(4,128)}, u32[]{:S(2)}) %copy-start.3) | copy-done | bytes 131096
  27.1 0.9 %copy-done.6 = f32[4,8192]{1,0:T(4,128)S(1)} copy-done((f32[4,8192]{1,0:T(4,128)S(1)}, f32[4,8192]{1,0:T(4,128)}, u32[]{:S(2)}) %copy-start.6) | copy-done | bytes 131096
  28.0 10.0 %partial_values.1 = (f32[8,128]{1,0:T(8,128)S(1)}, bf16[128,6400]{1,0:T(8,128)(2,1)S(1)}, bf16[256,8192]{1,0:T(8,128)(2,1)S(1)}, f32[512,128]{1,0:T(8,128)S(1)}) custom-call(s32[2]{0:T(128)S(1)} %pad_add_fusion.me_ref, bf16[16,6400]{1,0:T(8,128)(2,1)S(1)} %copy-done, bf16[16,6400]{1,0:T(8,128)(2,1)} %collective-permute-done.t1, ...), custom_call_target="tpu_custom_call" | custom-call | tf_op jit(solution)/shard_map/partial_values/pallas_call | solution.py:307
  38.0 0.6 collective-permute-start.7
  38.6 0.8 %collective-permute-done.7 = f32[8,128]{1,0:T(8,128)S(1)} collective-permute-done((f32[8,128]{1,0:T(8,128)S(1)}, f32[8,128]{1,0:T(8,128)S(1)}, u32[]{:S(2)}, u32[]{:S(2)}) %collective-permute-start.7) | collective-permute-done | bytes 4128 | tf_op jit(solution)/shard_map/ppermute | solution.py:343
  39.4 0.7 collective-permute-start.10
  40.1 1.2 %collective-permute-start.9 = (f32[8,128]{1,0:T(8,128)S(1)}, f32[8,128]{1,0:T(8,128)S(1)}, u32[]{:S(2)}, u32[]{:S(2)}) collective-permute-start(f32[8,128]{1,0:T(8,128)S(1)} %add.3.p0), channel_id=1, source_target_pairs={{0,4},{1,5},{2,6},{3,7},{4,0},{5,1},{6,2},{7,3},{8,12},{9,13},{10,... | collective-permute-start | bytes 12296 | tf_op jit(solution)/shard_map/ppermute | solution.py:339
  41.3 0.2 collective-permute-start.8
  41.5 1.5 %collective-permute-done.10.p3 = f32[8,128]{1,0:T(8,128)S(1)} collective-permute-done((f32[8,128]{1,0:T(8,128)S(1)}, f32[8,128]{1,0:T(8,128)S(1)}, u32[]{:S(2)}, u32[]{:S(2)}) %collective-permute-start.10) | collective-permute-done | bytes 4128 | tf_op jit(solution)/shard_map/ppermute | solution.py:339
  43.0 2.2 %collective-permute-done.9.p2 = f32[8,128]{1,0:T(8,128)S(1)} collective-permute-done((f32[8,128]{1,0:T(8,128)S(1)}, f32[8,128]{1,0:T(8,128)S(1)}, u32[]{:S(2)}, u32[]{:S(2)}) %collective-permute-start.9) | collective-permute-done | bytes 4128 | tf_op jit(solution)/shard_map/ppermute | solution.py:339
  45.2 0.9 %collective-permute-done.8.p1 = f32[8,128]{1,0:T(8,128)S(1)} collective-permute-done((f32[8,128]{1,0:T(8,128)S(1)}, f32[8,128]{1,0:T(8,128)S(1)}, u32[]{:S(2)}, u32[]{:S(2)}) %collective-permute-start.8) | collective-permute-done | bytes 4128 | tf_op jit(solution)/shard_map/ppermute | solution.py:339
  46.1 8.3 %gradient.1 = (f32[4,16]{1,0:T(4,128)}, bf16[32,16,256]{2,1,0:T(8,128)(2,1)S(1)}) custom-call(s32[2]{0:T(128)S(1)} %pad_add_fusion.me_ref, f32[8,128]{1,0:T(8,128)S(1)} %add.3.p0, f32[8,128]{1,0:T(8,128)S(1)} %collective-permute-done.8.p1, f32[8,128]{1,0:T(8,128)S(1)} %collective-permute-done.9.p2, f32[8,128]{1,0:T(8,128)S(1)} %collective-permute-done.10.p3, ...), custom_call_target="tpu_custom_call" | custom-call | tf_op jit(solution)/shard_map/gradient/pallas_call | solution.py:320
  54.4 22.5 %all_to_all.5.in_ref = bf16[32,16,256]{2,1,0:T(8,128)(2,1)S(1)} all-to-all(bf16[32,16,256]{2,1,0:T(8,128)(2,1)S(1)} %get-tuple-element.27), channel_id=1, replica_groups=mesh['walk'=32,'det'=8] {'walk'}, dimensions={0} | all-to-all | bytes 524288 | tf_op jit(solution)/shard_map/all_to_all | solution.py:361
  77.0 1.0 %finish.1 = (f32[4,1,256]{2,1,0:T(1,128)}, f32[1,4]{1,0:T(1,128)}) custom-call(bf16[32,16,256]{2,1,0:T(8,128)(2,1)S(1)} %all_to_all.5.in_ref), custom_call_target="tpu_custom_call" | custom-call | tf_op jit(solution)/shard_map/finish/pallas_call | solution.py:330
  (15 shorter events, 0.0 us)
Async XLA Ops:
  5.0 21.2 %copy-start = (bf16[16,6400]{1,0:T(8,128)(2,1)S(1)}, bf16[16,6400]{1,0:T(8,128)(2,1)}, u32[]{:S(2)}) copy-start(bf16[16,6400]{1,0:T(8,128)(2,1)} %tables.1.t0) | copy-start | bytes 614404
  5.0 8.5 %collective-permute-start = (bf16[16,6400]{1,0:T(8,128)(2,1)}, bf16[16,6400]{1,0:T(8,128)(2,1)}, u32[]{:S(2)}, u32[]{:S(2)}) collective-permute-start(bf16[16,6400]{1,0:T(8,128)(2,1)} %tables.1.t0), channel_id=1, source_target_pairs={{0,2},{1,7},{2,4},{3,1},{4,6},{5,3},{6,0},{7,5},{8,10},{9,15},{10,... | collective-permute-start | bytes 614408 | tf_op jit(solution)/shard_map/ppermute | solution.py:339
  6.6 8.8 %collective-permute-start.1 = (bf16[16,6400]{1,0:T(8,128)(2,1)}, bf16[16,6400]{1,0:T(8,128)(2,1)}, u32[]{:S(2)}, u32[]{:S(2)}) collective-permute-start(bf16[16,6400]{1,0:T(8,128)(2,1)} %tables.1.t0), channel_id=1, source_target_pairs={{0,6},{1,3},{2,0},{3,5},{4,2},{5,7},{6,4},{7,1},{8,14},{9,11},{10,... | collective-permute-start | bytes 614408 | tf_op jit(solution)/shard_map/ppermute | solution.py:339
  8.3 0.9 %copy-start.1 = (s32[4,8192]{1,0:T(4,128)S(1)}, s32[4,8192]{1,0:T(4,128)}, u32[]{:S(2)}) copy-start(s32[4,8192]{1,0:T(4,128)} %exc_ref.7) | copy-start | bytes 393220
  9.2 0.9 %copy-start.4 = (f32[4,8192]{1,0:T(4,128)S(1)}, f32[4,8192]{1,0:T(4,128)}, u32[]{:S(2)}) copy-start(f32[4,8192]{1,0:T(4,128)} %coef_ref.5) | copy-start | bytes 393220
  13.5 7.4 %collective-permute-start.2 = (bf16[16,6400]{1,0:T(8,128)(2,1)}, bf16[16,6400]{1,0:T(8,128)(2,1)}, u32[]{:S(2)}, u32[]{:S(2)}) collective-permute-start(bf16[16,6400]{1,0:T(8,128)(2,1)} %collective-permute-done.t1), channel_id=1, source_target_pairs={{0,2},{1,7},{2,4},{3,1},{4,6},{5,3},{6,0},{7,5},{8,10},{9,15},{10,... | collective-permute-start | bytes 614408 | tf_op jit(solution)/shard_map/ppermute | solution.py:339
  14.7 11.5 %collective-permute-start.3 = (bf16[16,6400]{1,0:T(8,128)(2,1)}, bf16[16,6400]{1,0:T(8,128)(2,1)}, u32[]{:S(2)}, u32[]{:S(2)}) collective-permute-start(bf16[16,6400]{1,0:T(8,128)(2,1)} %tables.1.t0), channel_id=1, source_target_pairs={{0,1},{1,0},{2,3},{3,2},{4,5},{5,4},{6,7},{7,6},{8,9},{9,8},{10,11... | collective-permute-start | bytes 614408 | tf_op jit(solution)/shard_map/ppermute | solution.py:343
  15.4 10.8 %collective-permute-start.4 = (bf16[16,6400]{1,0:T(8,128)(2,1)}, bf16[16,6400]{1,0:T(8,128)(2,1)}, u32[]{:S(2)}, u32[]{:S(2)}) collective-permute-start(bf16[16,6400]{1,0:T(8,128)(2,1)} %collective-permute-done.t1), channel_id=1, source_target_pairs={{0,1},{1,0},{2,3},{3,2},{4,5},{5,4},{6,7},{7,6},{8,9},{9,8},{10,11... | collective-permute-start | bytes 614408 | tf_op jit(solution)/shard_map/ppermute | solution.py:343
  15.4 10.8 %collective-permute-start.5 = (bf16[16,6400]{1,0:T(8,128)(2,1)}, bf16[16,6400]{1,0:T(8,128)(2,1)}, u32[]{:S(2)}, u32[]{:S(2)}) collective-permute-start(bf16[16,6400]{1,0:T(8,128)(2,1)} %collective-permute-done.1.t2), channel_id=1, source_target_pairs={{0,1},{1,0},{2,3},{3,2},{4,5},{5,4},{6,7},{7,6},{8,9},{9,8},{10,11... | collective-permute-start | bytes 614408 | tf_op jit(solution)/shard_map/ppermute | solution.py:343
  20.9 5.2 %collective-permute-start.6 = (bf16[16,6400]{1,0:T(8,128)(2,1)}, bf16[16,6400]{1,0:T(8,128)(2,1)}, u32[]{:S(2)}, u32[]{:S(2)}) collective-permute-start(bf16[16,6400]{1,0:T(8,128)(2,1)} %collective-permute-done.2.t3), channel_id=1, source_target_pairs={{0,1},{1,0},{2,3},{3,2},{4,5},{5,4},{6,7},{7,6},{8,9},{9,8},{10,11... | collective-permute-start | bytes 614408 | tf_op jit(solution)/shard_map/ppermute | solution.py:343
  20.9 0.9 %copy-start.2 = (s32[4,8192]{1,0:T(4,128)S(1)}, s32[4,8192]{1,0:T(4,128)}, u32[]{:S(2)}) copy-start(s32[4,8192]{1,0:T(4,128)} %exc_ref.7) | copy-start | bytes 393220
  21.8 0.9 %copy-start.5 = (f32[4,8192]{1,0:T(4,128)S(1)}, f32[4,8192]{1,0:T(4,128)}, u32[]{:S(2)}) copy-start(f32[4,8192]{1,0:T(4,128)} %coef_ref.5) | copy-start | bytes 393220
  26.2 0.9 %copy-start.3 = (s32[4,8192]{1,0:T(4,128)S(1)}, s32[4,8192]{1,0:T(4,128)}, u32[]{:S(2)}) copy-start(s32[4,8192]{1,0:T(4,128)} %exc_ref.7) | copy-start | bytes 393220
  27.1 0.9 %copy-start.6 = (f32[4,8192]{1,0:T(4,128)S(1)}, f32[4,8192]{1,0:T(4,128)}, u32[]{:S(2)}) copy-start(f32[4,8192]{1,0:T(4,128)} %coef_ref.5) | copy-start | bytes 393220
  28.0 18.1 %copy-start.7 = (f32[4,128]{1,0:T(4,128)S(1)}, f32[4,128]{1,0:T(4,128)}, u32[]{:S(2)}) copy-start(f32[4,128]{1,0:T(4,128)} %energy_ref.1) | copy-start | bytes 6148
  38.0 1.4 %collective-permute-start.7 = (f32[8,128]{1,0:T(8,128)S(1)}, f32[8,128]{1,0:T(8,128)S(1)}, u32[]{:S(2)}, u32[]{:S(2)}) collective-permute-start(f32[8,128]{1,0:T(8,128)S(1)} %get-tuple-element.23), channel_id=1, source_target_pairs={{0,1},{1,0},{2,3},{3,2},{4,5},{5,4},{6,7},{7,6},{8,9},{9,8},{10,11... | collective-permute-start | bytes 12296 | tf_op jit(solution)/shard_map/ppermute | solution.py:343
  39.4 3.6 %collective-permute-start.10 = (f32[8,128]{1,0:T(8,128)S(1)}, f32[8,128]{1,0:T(8,128)S(1)}, u32[]{:S(2)}, u32[]{:S(2)}) collective-permute-start(f32[8,128]{1,0:T(8,128)S(1)} %add.3.p0), channel_id=1, source_target_pairs={{0,6},{1,7},{2,0},{3,1},{4,2},{5,3},{6,4},{7,5},{8,14},{9,15},{10,... | collective-permute-start | bytes 12296 | tf_op jit(solution)/shard_map/ppermute | solution.py:339
  40.1 5.1 %collective-permute-start.9 = (f32[8,128]{1,0:T(8,128)S(1)}, f32[8,128]{1,0:T(8,128)S(1)}, u32[]{:S(2)}, u32[]{:S(2)}) collective-permute-start(f32[8,128]{1,0:T(8,128)S(1)} %add.3.p0), channel_id=1, source_target_pairs={{0,4},{1,5},{2,6},{3,7},{4,0},{5,1},{6,2},{7,3},{8,12},{9,13},{10,... | collective-permute-start | bytes 12296 | tf_op jit(solution)/shard_map/ppermute | solution.py:339
  41.3 4.8 %collective-permute-start.8 = (f32[8,128]{1,0:T(8,128)S(1)}, f32[8,128]{1,0:T(8,128)S(1)}, u32[]{:S(2)}, u32[]{:S(2)}) collective-permute-start(f32[8,128]{1,0:T(8,128)S(1)} %add.3.p0), channel_id=1, source_target_pairs={{0,2},{1,3},{2,4},{3,5},{4,6},{5,7},{6,0},{7,1},{8,10},{9,11},{10,... | collective-permute-start | bytes 12296 | tf_op jit(solution)/shard_map/ppermute | solution.py:339

commit v6 on v5

--- a/solution.py
+++ b/solution.py
@@ -84,6 +84,12 @@
         out_ref[:, i * V:(i + 1) * V] = tab_s[i * OWN:(i + 1) * OWN, :].astype(BF16)
 
 
+def first_kernel(exc_ref, coef_ref, spread_ref, oa_ref, exc_out, coef_out, oa_s):
+    exc_out[...] = exc_ref[...]
+    coef_out[...] = coef_ref[...]
+    spread_kernel(0, exc_ref, coef_ref, spread_ref, oa_ref, oa_s)
+
+
 def spread_kernel(side, exc_ref, coef_ref, spread_ref, oa_ref, oa_s):
     lane = lax.broadcasted_iota(jnp.int32, (1, V), 1)
     for n in range(NBLK // 2):
@@ -126,7 +132,7 @@
 
 def value_kernel(me_ref, t0, t1, t2, t3, t4, t5, t6, t7, half0, half1, oa0, oa1, exc_ref, coef_ref,
                  part_ref, tab_ref, p_ref, tia_ref, v_s, x_s, acc_s, exc_smem, sem):
-    indices = pltpu.make_async_copy(exc_ref, exc_smem, sem)
+    indices = pltpu.make_async_copy(exc_ref.at[0:1, :], exc_smem, sem)
     indices.start()
     x, c = lax.shift_right_logical(me_ref[1], 1), jnp.bitwise_and(me_ref[1], 1)
     ahead = 1 - 2 * c
@@ -293,13 +299,24 @@
     return pl.CostEstimate(flops=flops, bytes_accessed=8 * MIB, transcendentals=0)
 
 
+def spread_first(excitations, coeffs):
+    return pl.pallas_call(
+        first_kernel,
+        out_shape=[jax.ShapeDtypeStruct((QUADS * 32, NEL * V), BF16), jax.ShapeDtypeStruct((NBLK // 2, V), BF16),
+                   jax.ShapeDtypeStruct((4, KD), jnp.int32), jax.ShapeDtypeStruct((4, KD), F32)],
+        in_specs=vmem(2), out_specs=vmem(4),
+        scratch_shapes=[pltpu.VMEM((NBLK // 2, V), F32)],
+        compiler_params=params(8), cost_estimate=cost(50_000_000), name="spread_first",
+    )(excitations, coeffs)
+
+
 def spread(side, excitations, coeffs):
     return pl.pallas_call(
         functools.partial(spread_kernel, side),
         out_shape=[jax.ShapeDtypeStruct((QUADS * 32, NEL * V), BF16), jax.ShapeDtypeStruct((NBLK // 2, V), BF16)],
         in_specs=vmem(2), out_specs=vmem(2),
         scratch_shapes=[pltpu.VMEM((NBLK // 2, V), F32)],
-        compiler_params=params(8), cost_estimate=cost(800_000_000), name="spread",
+        compiler_params=params(8), cost_estimate=cost(50_000_000), name="spread",
     )(excitations, coeffs)
 
 
@@ -311,7 +328,7 @@
         in_specs=[pl.BlockSpec(memory_space=pltpu.SMEM)] + vmem(NDET + 6), out_specs=vmem(4),
         scratch_shapes=[pltpu.VMEM((NBLK * JPAD, GROUP), F32), pltpu.VMEM((NBLK * STATES, GROUP), F32),
                         pltpu.VMEM((STATES, GROUP, BLOCK), F32),
-                        pltpu.SMEM((4, KD), jnp.int32), pltpu.SemaphoreType.DMA],
+                        pltpu.SMEM((1, KD), jnp.int32), pltpu.SemaphoreType.DMA],
         compiler_params=params(22), name="partial_values",
     )(me, *tables, *halves, *columns, excitations, coeffs)
 
@@ -348,7 +365,7 @@
     table = make_table(positions, inverse, centers, exponent, orbital_weights)
     ahead = across(table, lambda c: 1 - 2 * c)
     behind = across(table, lambda c: 2 * c - 1)
-    half0, columns0 = spread(0, excitations, state_coeffs)
+    half0, columns0, excitations, state_coeffs = spread_first(excitations, state_coeffs)
     ahead, columns0 = lax.optimization_barrier((ahead, columns0))
     beyond = across(ahead, lambda c: 1 - 2 * c)
     half1, columns1 = spread(1, excitations, state_coeffs)

time: 78.2 us -> 74.5 us (0.953)
  local copies, waits for them, and re-layouts: 5.43 us -> 2.73 us
  Pallas kernels: 30.3 us -> 29.4 us
    pallas_call x0 -> x1, Pallas kernels: none -> 3.41 us  [spread_first(): pl.pallas_call(first_kernel, out_shape=[jax.ShapeDtypeStruct((QUADS * 32,...]
    pallas_call x2 -> x1, Pallas kernels: 6.72 us -> 3.33 us  [spread(): pl.pallas_call(functools.partial(spread_kernel, side), out_shape=[jax.Sha...]
    unnamed x16 -> x8, local copies, waits for them, and re-layouts: 5.43 us -> 2.73 us
    pallas_call x1, Pallas kernels: 9.99 us -> 9.01 us  [partial_values(): pl.pallas_call(value_kernel, out_shape=[jax.ShapeDtypeStruct((8, GROUP),...]
where the time goes in v6:
time: 74.5 us; the launch traced here: 74.2 us
  Pallas kernels  29.4 us (39%)
  blocking collectives  22.5 us (30%)
  waiting for transfers between devices  10.5 us (14%)
  starting transfers between devices  8.32 us (11%)
  local copies, waits for them, and re-layouts  2.73 us (4%)
    all_to_all x1, blocking collectives, shards(): grad, energy = finish(lax.all_to_all(messages, 'walk', 0, 0, tiled=True))  22.5 us
    ppermute x6, waiting for transfers between devices, across(): lax.ppermute(x, 'det', [(i, (i + 2 * step(i % 2)) % NDET) for i in range(...  9.66 us
    pallas_call x1, Pallas kernels, partial_values(): pl.pallas_call(value_kernel, out_shape=[jax.ShapeDtypeStruct((8, GROUP),...  9.01 us
    pallas_call x1, Pallas kernels, gradient(): pl.pallas_call(grad_kernel, out_shape=[jax.ShapeDtypeStruct((STATES, OWN)...  8.32 us
    ppermute x6, starting transfers between devices, across(): lax.ppermute(x, 'det', [(i, (i + 2 * step(i % 2)) % NDET) for i in range(...  6.52 us
    pallas_call x1, Pallas kernels, make_table(): pl.pallas_call(table_kernel, out_shape=jax.ShapeDtypeStruct((OWN, NEL * V...  4.34 us
    pallas_call x1, Pallas kernels, spread_first(): pl.pallas_call(first_kernel, out_shape=[jax.ShapeDtypeStruct((QUADS * 32,...  3.41 us
    pallas_call x1, Pallas kernels, spread(): pl.pallas_call(functools.partial(spread_kernel, side), out_shape=[jax.Sha...  3.33 us
  transfers between devices with their start and end apart: 11, of which 5 were waited for; matrix products, arithmetic and copies ran while one was open for 0% of the time, Pallas kernels for 9%

profile of v6, /device:TPU:32, one launch (start us, length us, event | category | flops | bytes accessed | tf_op | source)
XLA Modules:
  0.0 74.2 jit_solution(9500465617159272929)
XLA Ops:
  0.6 4.3 %tables.1.t0 = bf16[16,6400]{1,0:T(8,128)(2,1)} custom-call(f32[3,16,50]{2,1,0:T(8,128)} %pos_hbm.1, f32[50,16,50]{2,1,0:T(8,128)} %bitcast.5, f32[3,512]{1,0:T(4,128)} %cen_hbm.1, f32[1,512]{1,0:T(1,128)} %bitcast.6, f32[512,128]{1,0:T(8,128)} %orb_hbm.1), custom_call_target="tpu_custom_call" | custom-call | tf_op jit(solution)/shard_map/tables/pallas_call | solution.py:286
  5.0 1.6 %collective-permute-start = (bf16[16,6400]{1,0:T(8,128)(2,1)}, bf16[16,6400]{1,0:T(8,128)(2,1)}, u32[]{:S(2)}, u32[]{:S(2)}) collective-permute-start(bf16[16,6400]{1,0:T(8,128)(2,1)} %tables.1.t0), channel_id=1, source_target_pairs={{0,2},{1,7},{2,4},{3,1},{4,6},{5,3},{6,0},{7,5},{8,10},{9,15},{10,... | collective-permute-start | bytes 614408 | tf_op jit(solution)/shard_map/ppermute | solution.py:356
  6.5 1.7 %collective-permute-start.1 = (bf16[16,6400]{1,0:T(8,128)(2,1)}, bf16[16,6400]{1,0:T(8,128)(2,1)}, u32[]{:S(2)}, u32[]{:S(2)}) collective-permute-start(bf16[16,6400]{1,0:T(8,128)(2,1)} %tables.1.t0), channel_id=1, source_target_pairs={{0,6},{1,3},{2,0},{3,5},{4,2},{5,7},{6,4},{7,1},{8,14},{9,11},{10,... | collective-permute-start | bytes 614408 | tf_op jit(solution)/shard_map/ppermute | solution.py:356
  8.3 0.9 %copy-done.1 = s32[4,8192]{1,0:T(4,128)S(1)} copy-done((s32[4,8192]{1,0:T(4,128)S(1)}, s32[4,8192]{1,0:T(4,128)}, u32[]{:S(2)}) %copy-start.1) | copy-done | bytes 131096
  9.2 0.9 %copy-done.2 = f32[4,8192]{1,0:T(4,128)S(1)} copy-done((f32[4,8192]{1,0:T(4,128)S(1)}, f32[4,8192]{1,0:T(4,128)}, u32[]{:S(2)}) %copy-start.2) | copy-done | bytes 131096
  10.1 3.4 %spread_first.1 = (bf16[256,6400]{1,0:T(8,128)(2,1)S(1)}, bf16[32,128]{1,0:T(8,128)(2,1)S(1)}, s32[4,8192]{1,0:T(4,128)S(1)}, f32[4,8192]{1,0:T(4,128)S(1)}) custom-call(s32[4,8192]{1,0:T(4,128)S(1)} %copy-done.1, f32[4,8192]{1,0:T(4,128)S(1)} %copy-done.2), custom_call_target="tpu_custom_call" | custom-call | flops 50000000 | bytes 8388608 | tf_op jit(solution)/shard_map/spread_first/pallas_call | solution.py:303
  13.5 0.0 collective-permute-done.t1
  13.5 1.1 %collective-permute-start.2 = (bf16[16,6400]{1,0:T(8,128)(2,1)}, bf16[16,6400]{1,0:T(8,128)(2,1)}, u32[]{:S(2)}, u32[]{:S(2)}) collective-permute-start(bf16[16,6400]{1,0:T(8,128)(2,1)} %collective-permute-done.t1), channel_id=1, source_target_pairs={{0,2},{1,7},{2,4},{3,1},{4,6},{5,3},{6,0},{7,5},{8,10},{9,15},{10,... | collective-permute-start | bytes 614408 | tf_op jit(solution)/shard_map/ppermute | solution.py:356
  14.6 0.7 collective-permute-start.3
  15.4 0.0 collective-permute-start.4
  15.4 0.0 collective-permute-done.1.t2
  15.4 0.5 collective-permute-start.5
  15.9 5.0 %collective-permute-done.2.t3 = bf16[16,6400]{1,0:T(8,128)(2,1)} collective-permute-done((bf16[16,6400]{1,0:T(8,128)(2,1)}, bf16[16,6400]{1,0:T(8,128)(2,1)}, u32[]{:S(2)}, u32[]{:S(2)}) %collective-permute-start.2) | collective-permute-done | bytes 204832 | tf_op jit(solution)/shard_map/ppermute | solution.py:356
  20.9 0.0 collective-permute-start.6
  20.9 3.3 %spread.1 = (bf16[256,6400]{1,0:T(8,128)(2,1)S(1)}, bf16[32,128]{1,0:T(8,128)(2,1)S(1)}) custom-call(s32[4,8192]{1,0:T(4,128)S(1)} %get-tuple-element.22.exc_ref, f32[4,8192]{1,0:T(4,128)S(1)} %get-tuple-element.23.coef_ref), custom_call_target="tpu_custom_call" | custom-call | flops 50000000 | bytes 8388608 | tf_op jit(solution)/shard_map/spread/pallas_call | solution.py:314
  24.2 0.1 pad_add_fusion.me_ref
  24.3 0.0 collective-permute-done.3.t4
  24.3 0.0 collective-permute-done.5.t6
  24.3 0.0 collective-permute-done.4.t5
  24.3 0.9 %copy-done = bf16[16,6400]{1,0:T(8,128)(2,1)S(1)} copy-done((bf16[16,6400]{1,0:T(8,128)(2,1)S(1)}, bf16[16,6400]{1,0:T(8,128)(2,1)}, u32[]{:S(2)}) %copy-start) | copy-done | bytes 204824
  25.3 9.0 %partial_values.1 = (f32[8,128]{1,0:T(8,128)S(1)}, bf16[128,6400]{1,0:T(8,128)(2,1)S(1)}, bf16[256,8192]{1,0:T(8,128)(2,1)S(1)}, f32[512,128]{1,0:T(8,128)S(1)}) custom-call(s32[2]{0:T(128)S(1)} %pad_add_fusion.me_ref, bf16[16,6400]{1,0:T(8,128)(2,1)S(1)} %copy-done, bf16[16,6400]{1,0:T(8,128)(2,1)} %collective-permute-done.t1, ...), custom_call_target="tpu_custom_call" | custom-call | tf_op jit(solution)/shard_map/partial_values/pallas_call | solution.py:324
  34.3 0.6 collective-permute-start.7
  34.9 0.8 %collective-permute-done.7 = f32[8,128]{1,0:T(8,128)S(1)} collective-permute-done((f32[8,128]{1,0:T(8,128)S(1)}, f32[8,128]{1,0:T(8,128)S(1)}, u32[]{:S(2)}, u32[]{:S(2)}) %collective-permute-start.7) | collective-permute-done | bytes 4128 | tf_op jit(solution)/shard_map/ppermute | solution.py:360
  35.7 0.7 collective-permute-start.10
  36.4 1.2 %collective-permute-start.9 = (f32[8,128]{1,0:T(8,128)S(1)}, f32[8,128]{1,0:T(8,128)S(1)}, u32[]{:S(2)}, u32[]{:S(2)}) collective-permute-start(f32[8,128]{1,0:T(8,128)S(1)} %add.3.p0), channel_id=1, source_target_pairs={{0,4},{1,5},{2,6},{3,7},{4,0},{5,1},{6,2},{7,3},{8,12},{9,13},{10,... | collective-permute-start | bytes 12296 | tf_op jit(solution)/shard_map/ppermute | solution.py:356
  37.6 0.2 collective-permute-start.8
  37.8 1.5 %collective-permute-done.10.p3 = f32[8,128]{1,0:T(8,128)S(1)} collective-permute-done((f32[8,128]{1,0:T(8,128)S(1)}, f32[8,128]{1,0:T(8,128)S(1)}, u32[]{:S(2)}, u32[]{:S(2)}) %collective-permute-start.10) | collective-permute-done | bytes 4128 | tf_op jit(solution)/shard_map/ppermute | solution.py:356
  39.3 2.2 %collective-permute-done.9.p2 = f32[8,128]{1,0:T(8,128)S(1)} collective-permute-done((f32[8,128]{1,0:T(8,128)S(1)}, f32[8,128]{1,0:T(8,128)S(1)}, u32[]{:S(2)}, u32[]{:S(2)}) %collective-permute-start.9) | collective-permute-done | bytes 4128 | tf_op jit(solution)/shard_map/ppermute | solution.py:356
  41.5 0.9 %collective-permute-done.8.p1 = f32[8,128]{1,0:T(8,128)S(1)} collective-permute-done((f32[8,128]{1,0:T(8,128)S(1)}, f32[8,128]{1,0:T(8,128)S(1)}, u32[]{:S(2)}, u32[]{:S(2)}) %collective-permute-start.8) | collective-permute-done | bytes 4128 | tf_op jit(solution)/shard_map/ppermute | solution.py:356
  42.4 8.3 %gradient.1 = (f32[4,16]{1,0:T(4,128)}, bf16[32,16,256]{2,1,0:T(8,128)(2,1)S(1)}) custom-call(s32[2]{0:T(128)S(1)} %pad_add_fusion.me_ref, f32[8,128]{1,0:T(8,128)S(1)} %add.3.p0, f32[8,128]{1,0:T(8,128)S(1)} %collective-permute-done.8.p1, f32[8,128]{1,0:T(8,128)S(1)} %collective-permute-done.9.p2, f32[8,128]{1,0:T(8,128)S(1)} %collective-permute-done.10.p3, ...), custom_call_target="tpu_custom_call" | custom-call | tf_op jit(solution)/shard_map/gradient/pallas_call | solution.py:337
  50.7 22.5 %all_to_all.5.in_ref = bf16[32,16,256]{2,1,0:T(8,128)(2,1)S(1)} all-to-all(bf16[32,16,256]{2,1,0:T(8,128)(2,1)S(1)} %get-tuple-element.31), channel_id=1, replica_groups=mesh['walk'=32,'det'=8] {'walk'}, dimensions={0} | all-to-all | bytes 524288 | tf_op jit(solution)/shard_map/all_to_all | solution.py:378
  73.3 1.0 %finish.1 = (f32[4,1,256]{2,1,0:T(1,128)}, f32[1,4]{1,0:T(1,128)}) custom-call(bf16[32,16,256]{2,1,0:T(8,128)(2,1)S(1)} %all_to_all.5.in_ref), custom_call_target="tpu_custom_call" | custom-call | tf_op jit(solution)/shard_map/finish/pallas_call | solution.py:347
  (7 shorter events, 0.0 us)
Async XLA Ops:
  5.0 8.5 %collective-permute-start = (bf16[16,6400]{1,0:T(8,128)(2,1)}, bf16[16,6400]{1,0:T(8,128)(2,1)}, u32[]{:S(2)}, u32[]{:S(2)}) collective-permute-start(bf16[16,6400]{1,0:T(8,128)(2,1)} %tables.1.t0), channel_id=1, source_target_pairs={{0,2},{1,7},{2,4},{3,1},{4,6},{5,3},{6,0},{7,5},{8,10},{9,15},{10,... | collective-permute-start | bytes 614408 | tf_op jit(solution)/shard_map/ppermute | solution.py:356
  6.5 8.8 %collective-permute-start.1 = (bf16[16,6400]{1,0:T(8,128)(2,1)}, bf16[16,6400]{1,0:T(8,128)(2,1)}, u32[]{:S(2)}, u32[]{:S(2)}) collective-permute-start(bf16[16,6400]{1,0:T(8,128)(2,1)} %tables.1.t0), channel_id=1, source_target_pairs={{0,6},{1,3},{2,0},{3,5},{4,2},{5,7},{6,4},{7,1},{8,14},{9,11},{10,... | collective-permute-start | bytes 614408 | tf_op jit(solution)/shard_map/ppermute | solution.py:356
  8.3 0.9 %copy-start.1 = (s32[4,8192]{1,0:T(4,128)S(1)}, s32[4,8192]{1,0:T(4,128)}, u32[]{:S(2)}) copy-start(s32[4,8192]{1,0:T(4,128)} %exc_ref.1) | copy-start | bytes 393220
  9.2 0.9 %copy-start.2 = (f32[4,8192]{1,0:T(4,128)S(1)}, f32[4,8192]{1,0:T(4,128)}, u32[]{:S(2)}) copy-start(f32[4,8192]{1,0:T(4,128)} %coef_ref.1) | copy-start | bytes 393220
  13.5 7.4 %collective-permute-start.2 = (bf16[16,6400]{1,0:T(8,128)(2,1)}, bf16[16,6400]{1,0:T(8,128)(2,1)}, u32[]{:S(2)}, u32[]{:S(2)}) collective-permute-start(bf16[16,6400]{1,0:T(8,128)(2,1)} %collective-permute-done.t1), channel_id=1, source_target_pairs={{0,2},{1,7},{2,4},{3,1},{4,6},{5,3},{6,0},{7,5},{8,10},{9,15},{10,... | collective-permute-start | bytes 614408 | tf_op jit(solution)/shard_map/ppermute | solution.py:356
  14.6 9.7 %collective-permute-start.3 = (bf16[16,6400]{1,0:T(8,128)(2,1)}, bf16[16,6400]{1,0:T(8,128)(2,1)}, u32[]{:S(2)}, u32[]{:S(2)}) collective-permute-start(bf16[16,6400]{1,0:T(8,128)(2,1)} %tables.1.t0), channel_id=1, source_target_pairs={{0,1},{1,0},{2,3},{3,2},{4,5},{5,4},{6,7},{7,6},{8,9},{9,8},{10,11... | collective-permute-start | bytes 614408 | tf_op jit(solution)/shard_map/ppermute | solution.py:360
  15.4 9.0 %collective-permute-start.4 = (bf16[16,6400]{1,0:T(8,128)(2,1)}, bf16[16,6400]{1,0:T(8,128)(2,1)}, u32[]{:S(2)}, u32[]{:S(2)}) collective-permute-start(bf16[16,6400]{1,0:T(8,128)(2,1)} %collective-permute-done.t1), channel_id=1, source_target_pairs={{0,1},{1,0},{2,3},{3,2},{4,5},{5,4},{6,7},{7,6},{8,9},{9,8},{10,11... | collective-permute-start | bytes 614408 | tf_op jit(solution)/shard_map/ppermute | solution.py:360
  15.4 9.0 %collective-permute-start.5 = (bf16[16,6400]{1,0:T(8,128)(2,1)}, bf16[16,6400]{1,0:T(8,128)(2,1)}, u32[]{:S(2)}, u32[]{:S(2)}) collective-permute-start(bf16[16,6400]{1,0:T(8,128)(2,1)} %collective-permute-done.1.t2), channel_id=1, source_target_pairs={{0,1},{1,0},{2,3},{3,2},{4,5},{5,4},{6,7},{7,6},{8,9},{9,8},{10,11... | collective-permute-start | bytes 614408 | tf_op jit(solution)/shard_map/ppermute | solution.py:360
  20.9 3.4 %collective-permute-start.6 = (bf16[16,6400]{1,0:T(8,128)(2,1)}, bf16[16,6400]{1,0:T(8,128)(2,1)}, u32[]{:S(2)}, u32[]{:S(2)}) collective-permute-start(bf16[16,6400]{1,0:T(8,128)(2,1)} %collective-permute-done.2.t3), channel_id=1, source_target_pairs={{0,1},{1,0},{2,3},{3,2},{4,5},{5,4},{6,7},{7,6},{8,9},{9,8},{10,11... | collective-permute-start | bytes 614408 | tf_op jit(solution)/shard_map/ppermute | solution.py:360
  24.3 0.9 %copy-start = (bf16[16,6400]{1,0:T(8,128)(2,1)S(1)}, bf16[16,6400]{1,0:T(8,128)(2,1)}, u32[]{:S(2)}) copy-start(bf16[16,6400]{1,0:T(8,128)(2,1)} %tables.1.t0) | copy-start | bytes 614404
  25.3 17.2 %copy-start.3 = (f32[4,128]{1,0:T(4,128)S(1)}, f32[4,128]{1,0:T(4,128)}, u32[]{:S(2)}) copy-start(f32[4,128]{1,0:T(4,128)} %energy_ref.1) | copy-start | bytes 6148
  34.3 1.4 %collective-permute-start.7 = (f32[8,128]{1,0:T(8,128)S(1)}, f32[8,128]{1,0:T(8,128)S(1)}, u32[]{:S(2)}, u32[]{:S(2)}) collective-permute-start(f32[8,128]{1,0:T(8,128)S(1)} %get-tuple-element.27), channel_id=1, source_target_pairs={{0,1},{1,0},{2,3},{3,2},{4,5},{5,4},{6,7},{7,6},{8,9},{9,8},{10,11... | collective-permute-start | bytes 12296 | tf_op jit(solution)/shard_map/ppermute | solution.py:360
  35.7 3.6 %collective-permute-start.10 = (f32[8,128]{1,0:T(8,128)S(1)}, f32[8,128]{1,0:T(8,128)S(1)}, u32[]{:S(2)}, u32[]{:S(2)}) collective-permute-start(f32[8,128]{1,0:T(8,128)S(1)} %add.3.p0), channel_id=1, source_target_pairs={{0,6},{1,7},{2,0},{3,1},{4,2},{5,3},{6,4},{7,5},{8,14},{9,15},{10,... | collective-permute-start | bytes 12296 | tf_op jit(solution)/shard_map/ppermute | solution.py:356
  36.4 5.1 %collective-permute-start.9 = (f32[8,128]{1,0:T(8,128)S(1)}, f32[8,128]{1,0:T(8,128)S(1)}, u32[]{:S(2)}, u32[]{:S(2)}) collective-permute-start(f32[8,128]{1,0:T(8,128)S(1)} %add.3.p0), channel_id=1, source_target_pairs={{0,4},{1,5},{2,6},{3,7},{4,0},{5,1},{6,2},{7,3},{8,12},{9,13},{10,... | collective-permute-start | bytes 12296 | tf_op jit(solution)/shard_map/ppermute | solution.py:356
  37.6 4.8 %collective-permute-start.8 = (f32[8,128]{1,0:T(8,128)S(1)}, f32[8,128]{1,0:T(8,128)S(1)}, u32[]{:S(2)}, u32[]{:S(2)}) collective-permute-start(f32[8,128]{1,0:T(8,128)S(1)} %add.3.p0), channel_id=1, source_target_pairs={{0,2},{1,3},{2,4},{3,5},{4,6},{5,7},{6,0},{7,1},{8,10},{9,11},{10,... | collective-permute-start | bytes 12296 | tf_op jit(solution)/shard_map/ppermute | solution.py:356

commit v7 on v6

--- a/solution.py
+++ b/solution.py
@@ -23,7 +23,7 @@
 NWALK = 32
 JPAD = 64
 MIB = 1024 * 1024
-UNROLL = 8
+UNROLL = 16
 QUADS = PAIRS // 4
 
 F32, BF16 = jnp.float32, jnp.bfloat16
@@ -127,7 +127,7 @@
             spread_ref[low, j * V:(j + 1) * V] = lo
         return _
 
-    lax.fori_loop(0, QUADS, quad, 0)
+    lax.fori_loop(0, QUADS, quad, 0, unroll=2)
 
 
 def value_kernel(me_ref, t0, t1, t2, t3, t4, t5, t6, t7, half0, half1, oa0, oa1, exc_ref, coef_ref,

time: 74.5 us -> 73.6 us (0.988)
  Pallas kernels: 29.4 us -> 28 us
    ppermute x6, starting transfers between devices: 6.52 us -> 7.34 us  [across(): lax.ppermute(x, 'det', [(i, (i + 2 * step(i % 2)) % NDET) for i in range(...]
  transfers between devices with their start and end apart: 11 -> 11, of which waited for: 5 -> 6; matrix products, arithmetic and copies ran while one was open for 0% -> 0% of each run, Pallas kernels for 9% -> 8%
where the time goes in v7:
time: 73.6 us; the launch traced here: 73.4 us
  Pallas kernels  28 us (38%)
  blocking collectives  22.5 us (31%)
  waiting for transfers between devices  10.7 us (15%)
  starting transfers between devices  8.67 us (12%)
  local copies, waits for them, and re-layouts  2.73 us (4%)
    all_to_all x1, blocking collectives, shards(): grad, energy = finish(lax.all_to_all(messages, 'walk', 0, 0, tiled=True))  22.5 us
    ppermute x6, waiting for transfers between devices, across(): lax.ppermute(x, 'det', [(i, (i + 2 * step(i % 2)) % NDET) for i in range(...  9.84 us
    pallas_call x1, Pallas kernels, partial_values(): pl.pallas_call(value_kernel, out_shape=[jax.ShapeDtypeStruct((8, GROUP),...  8.89 us
    pallas_call x1, Pallas kernels, gradient(): pl.pallas_call(grad_kernel, out_shape=[jax.ShapeDtypeStruct((STATES, OWN)...  8 us
    ppermute x6, starting transfers between devices, across(): lax.ppermute(x, 'det', [(i, (i + 2 * step(i % 2)) % NDET) for i in range(...  7.34 us
    pallas_call x1, Pallas kernels, make_table(): pl.pallas_call(table_kernel, out_shape=jax.ShapeDtypeStruct((OWN, NEL * V...  4.34 us
    pallas_call x1, Pallas kernels, spread(): pl.pallas_call(functools.partial(spread_kernel, side), out_shape=[jax.Sha...  2.95 us
    pallas_call x1, Pallas kernels, spread_first(): pl.pallas_call(first_kernel, out_shape=[jax.ShapeDtypeStruct((QUADS * 32,...  2.9 us
  transfers between devices with their start and end apart: 11, of which 6 were waited for; matrix products, arithmetic and copies ran while one was open for 0% of the time, Pallas kernels for 8%

profile of v7, /device:TPU:32, one launch (start us, length us, event | category | flops | bytes accessed | tf_op | source)
XLA Modules:
  0.0 73.4 jit_solution(10834703561971082591)
XLA Ops:
  0.6 4.3 %tables.1.t0 = bf16[16,6400]{1,0:T(8,128)(2,1)} custom-call(f32[3,16,50]{2,1,0:T(8,128)} %pos_hbm.1, f32[50,16,50]{2,1,0:T(8,128)} %bitcast.5, f32[3,512]{1,0:T(4,128)} %cen_hbm.1, f32[1,512]{1,0:T(1,128)} %bitcast.6, f32[512,128]{1,0:T(8,128)} %orb_hbm.1), custom_call_target="tpu_custom_call" | custom-call | tf_op jit(solution)/shard_map/tables/pallas_call | solution.py:286
  5.0 1.6 %collective-permute-start = (bf16[16,6400]{1,0:T(8,128)(2,1)}, bf16[16,6400]{1,0:T(8,128)(2,1)}, u32[]{:S(2)}, u32[]{:S(2)}) collective-permute-start(bf16[16,6400]{1,0:T(8,128)(2,1)} %tables.1.t0), channel_id=1, source_target_pairs={{0,2},{1,7},{2,4},{3,1},{4,6},{5,3},{6,0},{7,5},{8,10},{9,15},{10,... | collective-permute-start | bytes 614408 | tf_op jit(solution)/shard_map/ppermute | solution.py:356
  6.5 1.7 %collective-permute-start.1 = (bf16[16,6400]{1,0:T(8,128)(2,1)}, bf16[16,6400]{1,0:T(8,128)(2,1)}, u32[]{:S(2)}, u32[]{:S(2)}) collective-permute-start(bf16[16,6400]{1,0:T(8,128)(2,1)} %tables.1.t0), channel_id=1, source_target_pairs={{0,6},{1,3},{2,0},{3,5},{4,2},{5,7},{6,4},{7,1},{8,14},{9,11},{10,... | collective-permute-start | bytes 614408 | tf_op jit(solution)/shard_map/ppermute | solution.py:356
  8.3 0.9 %copy-done.1 = s32[4,8192]{1,0:T(4,128)S(1)} copy-done((s32[4,8192]{1,0:T(4,128)S(1)}, s32[4,8192]{1,0:T(4,128)}, u32[]{:S(2)}) %copy-start.1) | copy-done | bytes 131096
  9.2 0.9 %copy-done.2 = f32[4,8192]{1,0:T(4,128)S(1)} copy-done((f32[4,8192]{1,0:T(4,128)S(1)}, f32[4,8192]{1,0:T(4,128)}, u32[]{:S(2)}) %copy-start.2) | copy-done | bytes 131096
  10.1 2.9 %spread_first.1 = (bf16[256,6400]{1,0:T(8,128)(2,1)S(1)}, bf16[32,128]{1,0:T(8,128)(2,1)S(1)}, s32[4,8192]{1,0:T(4,128)S(1)}, f32[4,8192]{1,0:T(4,128)S(1)}) custom-call(s32[4,8192]{1,0:T(4,128)S(1)} %copy-done.1, f32[4,8192]{1,0:T(4,128)S(1)} %copy-done.2), custom_call_target="tpu_custom_call" | custom-call | flops 50000000 | bytes 8388608 | tf_op jit(solution)/shard_map/spread_first/pallas_call | solution.py:303
  13.0 0.1 collective-permute-done.t1
  13.1 1.5 %collective-permute-start.2 = (bf16[16,6400]{1,0:T(8,128)(2,1)}, bf16[16,6400]{1,0:T(8,128)(2,1)}, u32[]{:S(2)}, u32[]{:S(2)}) collective-permute-start(bf16[16,6400]{1,0:T(8,128)(2,1)} %collective-permute-done.t1), channel_id=1, source_target_pairs={{0,2},{1,7},{2,4},{3,1},{4,6},{5,3},{6,0},{7,5},{8,10},{9,15},{10,... | collective-permute-start | bytes 614408 | tf_op jit(solution)/shard_map/ppermute | solution.py:356
  14.6 0.2 collective-permute-start.3
  14.9 0.3 collective-permute-start.4
  15.2 0.0 collective-permute-done.1.t2
  15.2 0.2 collective-permute-start.5
  15.4 5.1 %collective-permute-done.2.t3 = bf16[16,6400]{1,0:T(8,128)(2,1)} collective-permute-done((bf16[16,6400]{1,0:T(8,128)(2,1)}, bf16[16,6400]{1,0:T(8,128)(2,1)}, u32[]{:S(2)}, u32[]{:S(2)}) %collective-permute-start.2) | collective-permute-done | bytes 204832 | tf_op jit(solution)/shard_map/ppermute | solution.py:356
  20.4 0.0 collective-permute-start.6
  20.4 2.9 %spread.1 = (bf16[256,6400]{1,0:T(8,128)(2,1)S(1)}, bf16[32,128]{1,0:T(8,128)(2,1)S(1)}) custom-call(s32[4,8192]{1,0:T(4,128)S(1)} %get-tuple-element.22.exc_ref, f32[4,8192]{1,0:T(4,128)S(1)} %get-tuple-element.23.coef_ref), custom_call_target="tpu_custom_call" | custom-call | flops 50000000 | bytes 8388608 | tf_op jit(solution)/shard_map/spread/pallas_call | solution.py:314
  23.4 0.1 pad_add_fusion.me_ref
  23.5 0.0 collective-permute-done.5.t6
  23.5 0.0 collective-permute-done.4.t5
  23.5 0.0 collective-permute-done.6.t7
  23.5 0.9 %copy-done = bf16[16,6400]{1,0:T(8,128)(2,1)S(1)} copy-done((bf16[16,6400]{1,0:T(8,128)(2,1)S(1)}, bf16[16,6400]{1,0:T(8,128)(2,1)}, u32[]{:S(2)}) %copy-start) | copy-done | bytes 204824
  24.4 8.9 %partial_values.1 = (f32[8,128]{1,0:T(8,128)S(1)}, bf16[128,6400]{1,0:T(8,128)(2,1)S(1)}, bf16[256,8192]{1,0:T(8,128)(2,1)S(1)}, f32[512,128]{1,0:T(8,128)S(1)}) custom-call(s32[2]{0:T(128)S(1)} %pad_add_fusion.me_ref, bf16[16,6400]{1,0:T(8,128)(2,1)S(1)} %copy-done, bf16[16,6400]{1,0:T(8,128)(2,1)} %collective-permute-done.t1, ...), custom_call_target="tpu_custom_call" | custom-call | tf_op jit(solution)/shard_map/partial_values/pallas_call | solution.py:324
  33.3 0.6 collective-permute-start.7
  33.9 0.8 %collective-permute-done.7 = f32[8,128]{1,0:T(8,128)S(1)} collective-permute-done((f32[8,128]{1,0:T(8,128)S(1)}, f32[8,128]{1,0:T(8,128)S(1)}, u32[]{:S(2)}, u32[]{:S(2)}) %collective-permute-start.7) | collective-permute-done | bytes 4128 | tf_op jit(solution)/shard_map/ppermute | solution.py:360
  34.7 1.1 %collective-permute-start.10 = (f32[8,128]{1,0:T(8,128)S(1)}, f32[8,128]{1,0:T(8,128)S(1)}, u32[]{:S(2)}, u32[]{:S(2)}) collective-permute-start(f32[8,128]{1,0:T(8,128)S(1)} %add.3.p0), channel_id=1, source_target_pairs={{0,6},{1,7},{2,0},{3,1},{4,2},{5,3},{6,4},{7,5},{8,14},{9,15},{10,... | collective-permute-start | bytes 12296 | tf_op jit(solution)/shard_map/ppermute | solution.py:356
  35.9 1.2 %collective-permute-start.9 = (f32[8,128]{1,0:T(8,128)S(1)}, f32[8,128]{1,0:T(8,128)S(1)}, u32[]{:S(2)}, u32[]{:S(2)}) collective-permute-start(f32[8,128]{1,0:T(8,128)S(1)} %add.3.p0), channel_id=1, source_target_pairs={{0,4},{1,5},{2,6},{3,7},{4,0},{5,1},{6,2},{7,3},{8,12},{9,13},{10,... | collective-permute-start | bytes 12296 | tf_op jit(solution)/shard_map/ppermute | solution.py:356
  37.1 0.2 collective-permute-start.8
  37.3 1.1 %collective-permute-done.10.p3 = f32[8,128]{1,0:T(8,128)S(1)} collective-permute-done((f32[8,128]{1,0:T(8,128)S(1)}, f32[8,128]{1,0:T(8,128)S(1)}, u32[]{:S(2)}, u32[]{:S(2)}) %collective-permute-start.10) | collective-permute-done | bytes 4128 | tf_op jit(solution)/shard_map/ppermute | solution.py:356
  38.4 2.6 %collective-permute-done.9.p2 = f32[8,128]{1,0:T(8,128)S(1)} collective-permute-done((f32[8,128]{1,0:T(8,128)S(1)}, f32[8,128]{1,0:T(8,128)S(1)}, u32[]{:S(2)}, u32[]{:S(2)}) %collective-permute-start.9) | collective-permute-done | bytes 4128 | tf_op jit(solution)/shard_map/ppermute | solution.py:356
  41.0 0.9 %collective-permute-done.8.p1 = f32[8,128]{1,0:T(8,128)S(1)} collective-permute-done((f32[8,128]{1,0:T(8,128)S(1)}, f32[8,128]{1,0:T(8,128)S(1)}, u32[]{:S(2)}, u32[]{:S(2)}) %collective-permute-start.8) | collective-permute-done | bytes 4128 | tf_op jit(solution)/shard_map/ppermute | solution.py:356
  41.9 8.0 %gradient.1 = (f32[4,16]{1,0:T(4,128)}, bf16[32,16,256]{2,1,0:T(8,128)(2,1)S(1)}) custom-call(s32[2]{0:T(128)S(1)} %pad_add_fusion.me_ref, f32[8,128]{1,0:T(8,128)S(1)} %add.3.p0, f32[8,128]{1,0:T(8,128)S(1)} %collective-permute-done.8.p1, f32[8,128]{1,0:T(8,128)S(1)} %collective-permute-done.9.p2, f32[8,128]{1,0:T(8,128)S(1)} %collective-permute-done.10.p3, ...), custom_call_target="tpu_custom_call" | custom-call | tf_op jit(solution)/shard_map/gradient/pallas_call | solution.py:337
  49.9 22.5 %all_to_all.5.in_ref = bf16[32,16,256]{2,1,0:T(8,128)(2,1)S(1)} all-to-all(bf16[32,16,256]{2,1,0:T(8,128)(2,1)S(1)} %get-tuple-element.31), channel_id=1, replica_groups=mesh['walk'=32,'det'=8] {'walk'}, dimensions={0} | all-to-all | bytes 524288 | tf_op jit(solution)/shard_map/all_to_all | solution.py:378
  72.5 1.0 %finish.1 = (f32[4,1,256]{2,1,0:T(1,128)}, f32[1,4]{1,0:T(1,128)}) custom-call(bf16[32,16,256]{2,1,0:T(8,128)(2,1)S(1)} %all_to_all.5.in_ref), custom_call_target="tpu_custom_call" | custom-call | tf_op jit(solution)/shard_map/finish/pallas_call | solution.py:347
  (7 shorter events, 0.0 us)
Async XLA Ops:
  5.0 8.2 %collective-permute-start = (bf16[16,6400]{1,0:T(8,128)(2,1)}, bf16[16,6400]{1,0:T(8,128)(2,1)}, u32[]{:S(2)}, u32[]{:S(2)}) collective-permute-start(bf16[16,6400]{1,0:T(8,128)(2,1)} %tables.1.t0), channel_id=1, source_target_pairs={{0,2},{1,7},{2,4},{3,1},{4,6},{5,3},{6,0},{7,5},{8,10},{9,15},{10,... | collective-permute-start | bytes 614408 | tf_op jit(solution)/shard_map/ppermute | solution.py:356
  6.5 8.6 %collective-permute-start.1 = (bf16[16,6400]{1,0:T(8,128)(2,1)}, bf16[16,6400]{1,0:T(8,128)(2,1)}, u32[]{:S(2)}, u32[]{:S(2)}) collective-permute-start(bf16[16,6400]{1,0:T(8,128)(2,1)} %tables.1.t0), channel_id=1, source_target_pairs={{0,6},{1,3},{2,0},{3,5},{4,2},{5,7},{6,4},{7,1},{8,14},{9,11},{10,... | collective-permute-start | bytes 614408 | tf_op jit(solution)/shard_map/ppermute | solution.py:356
  8.3 0.9 %copy-start.1 = (s32[4,8192]{1,0:T(4,128)S(1)}, s32[4,8192]{1,0:T(4,128)}, u32[]{:S(2)}) copy-start(s32[4,8192]{1,0:T(4,128)} %exc_ref.1) | copy-start | bytes 393220
  9.2 0.9 %copy-start.2 = (f32[4,8192]{1,0:T(4,128)S(1)}, f32[4,8192]{1,0:T(4,128)}, u32[]{:S(2)}) copy-start(f32[4,8192]{1,0:T(4,128)} %coef_ref.1) | copy-start | bytes 393220
  13.1 7.3 %collective-permute-start.2 = (bf16[16,6400]{1,0:T(8,128)(2,1)}, bf16[16,6400]{1,0:T(8,128)(2,1)}, u32[]{:S(2)}, u32[]{:S(2)}) collective-permute-start(bf16[16,6400]{1,0:T(8,128)(2,1)} %collective-permute-done.t1), channel_id=1, source_target_pairs={{0,2},{1,7},{2,4},{3,1},{4,6},{5,3},{6,0},{7,5},{8,10},{9,15},{10,... | collective-permute-start | bytes 614408 | tf_op jit(solution)/shard_map/ppermute | solution.py:356
  14.6 8.8 %collective-permute-start.3 = (bf16[16,6400]{1,0:T(8,128)(2,1)}, bf16[16,6400]{1,0:T(8,128)(2,1)}, u32[]{:S(2)}, u32[]{:S(2)}) collective-permute-start(bf16[16,6400]{1,0:T(8,128)(2,1)} %tables.1.t0), channel_id=1, source_target_pairs={{0,1},{1,0},{2,3},{3,2},{4,5},{5,4},{6,7},{7,6},{8,9},{9,8},{10,11... | collective-permute-start | bytes 614408 | tf_op jit(solution)/shard_map/ppermute | solution.py:360
  14.9 8.6 %collective-permute-start.4 = (bf16[16,6400]{1,0:T(8,128)(2,1)}, bf16[16,6400]{1,0:T(8,128)(2,1)}, u32[]{:S(2)}, u32[]{:S(2)}) collective-permute-start(bf16[16,6400]{1,0:T(8,128)(2,1)} %collective-permute-done.t1), channel_id=1, source_target_pairs={{0,1},{1,0},{2,3},{3,2},{4,5},{5,4},{6,7},{7,6},{8,9},{9,8},{10,11... | collective-permute-start | bytes 614408 | tf_op jit(solution)/shard_map/ppermute | solution.py:360
  15.2 8.3 %collective-permute-start.5 = (bf16[16,6400]{1,0:T(8,128)(2,1)}, bf16[16,6400]{1,0:T(8,128)(2,1)}, u32[]{:S(2)}, u32[]{:S(2)}) collective-permute-start(bf16[16,6400]{1,0:T(8,128)(2,1)} %collective-permute-done.1.t2), channel_id=1, source_target_pairs={{0,1},{1,0},{2,3},{3,2},{4,5},{5,4},{6,7},{7,6},{8,9},{9,8},{10,11... | collective-permute-start | bytes 614408 | tf_op jit(solution)/shard_map/ppermute | solution.py:360
  20.4 3.1 %collective-permute-start.6 = (bf16[16,6400]{1,0:T(8,128)(2,1)}, bf16[16,6400]{1,0:T(8,128)(2,1)}, u32[]{:S(2)}, u32[]{:S(2)}) collective-permute-start(bf16[16,6400]{1,0:T(8,128)(2,1)} %collective-permute-done.2.t3), channel_id=1, source_target_pairs={{0,1},{1,0},{2,3},{3,2},{4,5},{5,4},{6,7},{7,6},{8,9},{9,8},{10,11... | collective-permute-start | bytes 614408 | tf_op jit(solution)/shard_map/ppermute | solution.py:360
  23.5 0.9 %copy-start = (bf16[16,6400]{1,0:T(8,128)(2,1)S(1)}, bf16[16,6400]{1,0:T(8,128)(2,1)}, u32[]{:S(2)}) copy-start(bf16[16,6400]{1,0:T(8,128)(2,1)} %tables.1.t0) | copy-start | bytes 614404
  24.4 17.5 %copy-start.3 = (f32[4,128]{1,0:T(4,128)S(1)}, f32[4,128]{1,0:T(4,128)}, u32[]{:S(2)}) copy-start(f32[4,128]{1,0:T(4,128)} %energy_ref.1) | copy-start | bytes 6148
  33.3 1.4 %collective-permute-start.7 = (f32[8,128]{1,0:T(8,128)S(1)}, f32[8,128]{1,0:T(8,128)S(1)}, u32[]{:S(2)}, u32[]{:S(2)}) collective-permute-start(f32[8,128]{1,0:T(8,128)S(1)} %get-tuple-element.27), channel_id=1, source_target_pairs={{0,1},{1,0},{2,3},{3,2},{4,5},{5,4},{6,7},{7,6},{8,9},{9,8},{10,11... | collective-permute-start | bytes 12296 | tf_op jit(solution)/shard_map/ppermute | solution.py:360
  34.7 3.6 %collective-permute-start.10 = (f32[8,128]{1,0:T(8,128)S(1)}, f32[8,128]{1,0:T(8,128)S(1)}, u32[]{:S(2)}, u32[]{:S(2)}) collective-permute-start(f32[8,128]{1,0:T(8,128)S(1)} %add.3.p0), channel_id=1, source_target_pairs={{0,6},{1,7},{2,0},{3,1},{4,2},{5,3},{6,4},{7,5},{8,14},{9,15},{10,... | collective-permute-start | bytes 12296 | tf_op jit(solution)/shard_map/ppermute | solution.py:356
  35.9 5.1 %collective-permute-start.9 = (f32[8,128]{1,0:T(8,128)S(1)}, f32[8,128]{1,0:T(8,128)S(1)}, u32[]{:S(2)}, u32[]{:S(2)}) collective-permute-start(f32[8,128]{1,0:T(8,128)S(1)} %add.3.p0), channel_id=1, source_target_pairs={{0,4},{1,5},{2,6},{3,7},{4,0},{5,1},{6,2},{7,3},{8,12},{9,13},{10,... | collective-permute-start | bytes 12296 | tf_op jit(solution)/shard_map/ppermute | solution.py:356
  37.1 4.8 %collective-permute-start.8 = (f32[8,128]{1,0:T(8,128)S(1)}, f32[8,128]{1,0:T(8,128)S(1)}, u32[]{:S(2)}, u32[]{:S(2)}) collective-permute-start(f32[8,128]{1,0:T(8,128)S(1)} %add.3.p0), channel_id=1, source_target_pairs={{0,2},{1,3},{2,4},{3,5},{4,6},{5,7},{6,0},{7,1},{8,10},{9,11},{10,... | collective-permute-start | bytes 12296 | tf_op jit(solution)/shard_map/ppermute | solution.py:356
